TPU v7x, 32 devices: a whole 2x2x4 slice. The times are simulated.
32 devices in a mesh: ab: 4 (over y, core), cd: 8 (over z, x).
Axes of the slice: x: 2, y: 2, z: 4, core: 2. Of those that a mesh axis runs over, the one named last changes fastest.
Arguments:
- pair_values: bfloat16 [8192, 16384], P('ab', 'cd'), may hold values from -0.0625 to 0.0625
- amplitudes: bfloat16 [64, 800, 800], P('ab', 'cd'), may hold values from -6 to 6
- cd_first: int32 [16384], P('cd'), may hold values from 0 to 799, as said below
- cd_second: int32 [16384], P('cd'), may hold values from 0 to 799, as said below
- live_cols: int32 [8], P('cd'), may hold values from 512 to 2048, as said below
Outputs:
- ladder: bfloat16 [64, 8192], P(None, ('ab', 'cd'))
Inputs may be any that keep to these rules, and one draw needn't show every extreme that they name: `cd_first`: slot n lies in slab s = n // 2048 and its c lies in orbitals s * 100 to (s + 1) * 100 - 1. cd_second[n] >= cd_first[n] for every slot. `live_cols`: slots 0 and 1 of every slab are live.
All inputs are finite; a program needn't handle non-finite values.
Results may differ from a plain program's by a relative error of at most 0.0051.
Values may be sent and summed in bfloat16 or wider, within the bound.
No kernel may reach another device: no remote copies, remote signals or barrier semaphores. Data moves between devices by JAX's collectives and lax.ppermute only.
A program may use at most 64 MiB of HBM per device.

v0:
```python
import jax
import jax.numpy as jnp
from jax import lax
from jax.sharding import PartitionSpec as P


def on_device(pair_values, amplitudes, cd_first, cd_second, live_cols):
    slab = lax.axis_index("cd")
    pair_block = amplitudes.shape[0]
    orbit_block = amplitudes.shape[1]
    orbitals = amplitudes.shape[2]
    columns = cd_first.shape[0]
    local_first = cd_first - slab * orbit_block
    own_flat = amplitudes.reshape(pair_block, orbit_block * orbitals)
    direct = jnp.take(own_flat, local_first * orbitals + cd_second, axis=1)
    mirrored = lax.all_to_all(amplitudes, "cd", split_axis=2, concat_axis=1, tiled=True)
    mirror_flat = mirrored.reshape(pair_block, orbitals * orbit_block)
    crossed = jnp.take(mirror_flat, cd_second * orbit_block + local_first, axis=1)
    live_count = live_cols[0]
    slots = jnp.arange(columns, dtype=jnp.int32)
    live = (slots < live_count).astype(jnp.float32)
    half = jnp.where(cd_first == cd_second, jnp.float32(0.5), jnp.float32(1.0))
    weight = half * live
    packed = ((direct.astype(jnp.float32) + crossed.astype(jnp.float32)) * weight[None, :]).astype(
        jnp.bfloat16
    )
    contract = (((1,), (1,)), ((), ()))
    partial_sums = lax.dot_general(
        lax.all_gather(packed, "ab", axis=0, tiled=True),
        pair_values,
        contract,
        preferred_element_type=jnp.float32,
    )
    return lax.psum_scatter(partial_sums, "cd", scatter_dimension=1, tiled=True).astype(
        jnp.bfloat16
    )


def solution(mesh):
    placed = (P("ab", "cd"), P("ab", "cd", None), P("cd"), P("cd"), P("cd"))
    return jax.shard_map(
        on_device, mesh=mesh, in_specs=placed, out_specs=P(None, ("ab", "cd")), check_vma=False
    )
```

profile of v0, /device:TPU:0, one launch (start us, length us, event | category | flops | bytes accessed | tf_op | source)
XLA Modules:
  0.0 219.6 jit_solution(7474212847939082829)
XLA Ops:
  6.5 6.8 %copy.25 = bf16[16,100,800]{1,0,2:T(8,128)(2,1)} copy(bf16[16,100,800]{2,0,1:T(8,128)(2,1)} %param.8) | data formatting | bytes 5120000 | tf_op args[1]
  13.3 7.3 %all-to-all-start = ((bf16[16,100,800]{1,0,2:T(8,128)(2,1)}), bf16[16,100,800]{1,0,2:T(8,128)(2,1)S(1)}, u32[]{:S(2)}, u32[]{:S(2)}) async-start(bf16[16,100,800]{1,0,2:T(8,128)(2,1)} %copy.25), calls=%async_computation | async-start | bytes 6553600 | tf_op jit(solution)/shard_map/all_to_all | solution.py:16
  20.6 0.0 reduce-scatter.2.cloned.1.call-start
  20.6 0.0 copy-start.1
  20.6 0.0 copy-start.2
  20.6 15.6 %copy.23 = bf16[16,100,800]{0,2,1:T(8,128)(2,1)} copy(bf16[16,100,800]{2,0,1:T(8,128)(2,1)} %param.8) | data formatting | bytes 5120000 | tf_op args[1]
  36.3 0.0 copy-done.1
  36.3 0.0 copy-done.2
  36.3 17.1 %gather_fusion = bf16[2048,16]{1,0:T(8,128)(2,1)} fusion(bf16[16,80000]{0,1:T(8,128)(2,1)} %bitcast.11, s32[2048]{0:T(1024)S(1)} %get-tuple-element.8), kind=kCustom, calls=%fused_computation.clone | custom fusion | bytes 139264 | tf_op jit(solution)/shard_map/jit(_take)/gather | solution.py:15
  53.4 1.2 copy.24
  55.3 38.8 %all-to-all-done = bf16[16,100,800]{1,0,2:T(8,128)(2,1)S(1)} async-done(((bf16[16,100,800]{1,0,2:T(8,128)(2,1)}), bf16[16,100,800]{1,0,2:T(8,128)(2,1)S(1)}, u32[]{:S(2)}, u32[]{:S(2)}) %all-to-all-start) | async-done | bytes 2560032 | tf_op jit(solution)/shard_map/all_to_all | solution.py:16
  94.1 0.0 copy-start
  94.1 1.7 copy-done
  95.8 5.6 %copy.26 = bf16[16,100,8,100]{3,1,2,0:T(8,128)(2,1)S(1)} copy(bf16[16,100,8,100]{1,0,3,2:T(8,128)(2,1)} %bitcast.13) | data formatting | bytes 5120000 | tf_op jit(solution)/shard_map/all_to_all | solution.py:16
  101.4 5.8 %reshape.14 = bf16[16,80000]{1,0:T(8,128)(2,1)} reshape(bf16[16,8,100,100]{3,2,1,0:T(8,128)(2,1)S(1)} %bitcast.12) | data formatting | bytes 5120000 | tf_op jit(solution)/shard_map/reshape | solution.py:17
  107.2 14.5 %copy.27 = bf16[16,80000]{0,1:T(8,128)(2,1)} copy(bf16[16,80000]{1,0:T(8,128)(2,1)} %reshape.14) | data formatting | bytes 5120000 | tf_op jit(solution)/shard_map/reshape | solution.py:17
  121.7 15.0 %gather_fusion.1 = bf16[2048,16]{1,0:T(8,128)(2,1)S(1)} fusion(bf16[16,80000]{0,1:T(8,128)(2,1)} %copy.27, s32[2048]{0:T(1024)S(1)} %get-tuple-element.9), kind=kCustom, calls=%fused_computation.1.clone | custom fusion | bytes 139264 | tf_op jit(solution)/shard_map/jit(_take)/gather | solution.py:18
  136.8 0.2 copy.28
  137.0 5.8 %all_gather.3 = bf16[64,2048]{1,0:T(8,128)(2,1)S(1)} all-gather(bf16[16,2048]{1,0:T(8,128)(2,1)S(1)} %multiply_convert_fusion), channel_id=1, replica_groups=mesh['ab'=4,'cd'=8] {'ab'}, dimensions={0}, use_global_device_ids=true | all-gather | bytes 327680 | tf_op jit(solution)/shard_map/all_gather | solution.py:29
  142.8 6.8 %fusion = f32[64,2048]{1,0:T(8,128)} fusion(bf16[64,2048]{1,0:T(8,128)(2,1)S(1)} %all_gather.3, bf16[2048,2048]{1,0:T(8,128)(2,1)} %param.7), kind=kOutput, calls=%fused_computation.11 | convolution fusion | flops 536870912 | bytes 9175040 | tf_op jit(solution)/shard_map/dot_general | solution.py:28
  149.6 0.0 reduce-scatter.2.cloned.1.call-update
  149.7 61.6 %reduce-scatter.2.cloned.1.call-done = f32[64,256]{1,0:T(8,128)} async-done(((f32[64,2048]{1,0:T(8,128)}), f32[64,256]{1,0:T(8,128)}) %reduce-scatter.2.cloned.1.call-update) | async-done | bytes 65552 | tf_op jit(solution)/shard_map/reduce_scatter | solution.py:34
  211.3 1.5 convert_element_type.16
  (4 shorter events, 0.1 us)
Async XLA Ops:
  13.3 80.8 %all-to-all-start = ((bf16[16,100,800]{1,0,2:T(8,128)(2,1)}), bf16[16,100,800]{1,0,2:T(8,128)(2,1)S(1)}, u32[]{:S(2)}, u32[]{:S(2)}) async-start(bf16[16,100,800]{1,0,2:T(8,128)(2,1)} %copy.25), calls=%async_computation | async-start | bytes 6553600 | tf_op jit(solution)/shard_map/all_to_all | solution.py:16
  20.6 190.7 %reduce-scatter.2.cloned.1.call-start = ((), (), s32[]{:S(2)}) async-start(), calls=%async_computation.2 | async-start | bytes 589824 | tf_op jit(solution)/shard_map/reduce_scatter | solution.py:34
  20.6 15.6 %copy-start.1 = (s32[2048]{0:T(1024)S(1)}, s32[2048]{0:T(1024)}, u32[]{:S(2)}) copy-start(s32[2048]{0:T(1024)} %param.10) | copy-start | bytes 24580
  20.6 15.6 %copy-start.2 = (s32[2048]{0:T(1024)S(1)}, s32[2048]{0:T(1024)}, u32[]{:S(2)}) copy-start(s32[2048]{0:T(1024)} %param.9) | copy-start | bytes 24580
  94.1 1.7 copy-start
Sparse Core Ops, SparseCore 0:
  149.8 61.4 reduce-scatter.1
where the time goes:
time: 221 us; the launch traced here: 220 us
  waiting for transfers between devices  100 us (45%)
  local copies, waits for them, and re-layouts  83.6 us (38%)
  between operations  14.1 us (6%)
  starting transfers between devices  7.29 us (3%)
  matrix products  6.83 us (3%)
  blocking collectives  5.79 us (3%)
    reduce_scatter x1, waiting for transfers between devices, on_device(): lax.psum_scatter(partial_sums, 'cd', scatter_dimension=1, tiled=True)  61.6 us
    all_to_all x1, waiting for transfers between devices, on_device(): lax.all_to_all(amplitudes, 'cd', split_axis=2, concat_axis=1, tiled=True)  38.8 us
    unnamed x8, local copies, waits for them, and re-layouts  24.1 us
    reshape x2, local copies, waits for them, and re-layouts, on_device(): mirror_flat = mirrored.reshape(pair_block, orbitals * orbit_block)  20.3 us
    gather x2, local copies, waits for them, and re-layouts, on_device(): direct = jnp.take(own_flat, local_first * orbitals + cd_second, axis=1)  18.3 us
    gather x2, local copies, waits for them, and re-layouts, on_device(): jnp.take(mirror_flat, cd_second * orbit_block + local_first, axis=1)  15.2 us
    all_to_all x1, starting transfers between devices, on_device(): lax.all_to_all(amplitudes, 'cd', split_axis=2, concat_axis=1, tiled=True)  7.25 us
    dot_general x1, matrix products, on_device(): lax.dot_general(lax.all_gather(packed, 'ab', axis=0, tiled=True), pair_va...  6.83 us
  transfers between devices with their start and end apart: 2, of which 2 were waited for; matrix products, arithmetic and copies ran while one was open for 15% of the time, Pallas kernels for 0%

commit v1 on v0

v1 whole, which is shorter than its diff:
```python
import functools

import jax
import jax.numpy as jnp
from jax import lax
from jax.experimental import pallas as pl
from jax.experimental.pallas import tpu as pltpu
from jax.sharding import PartitionSpec as P

LANES = 128
VMEM_LIMIT = 48 * 1024 * 1024


def chunk_of(columns):
    return min(columns, 512)


def one_hot(keys, depth):
    rows = lax.broadcasted_iota(jnp.int32, (depth, keys.shape[1]), 0)
    return jnp.where(rows == keys, 1.0, 0.0).astype(jnp.bfloat16)


def picked(groups, sums, pairs, total):
    for g in range(sums.shape[0] // pairs):
        total = jnp.where(groups == g, sums[g * pairs : (g + 1) * pairs], total)
    return total


def direct_kernel(slabs, orbits, pairs, table_ref, first_ref, second_ref, aligned_ref, direct_ref):
    rows = orbits * pairs
    for s in range(slabs):
        aligned_ref[s, :, :] = jnp.concatenate(
            [
                table_ref[:, s * orbits : (s + 1) * orbits],
                jnp.zeros((rows, LANES - orbits), jnp.bfloat16),
            ],
            axis=1,
        )
    columns = first_ref.shape[1]
    width = chunk_of(columns)

    def step(i, carry):
        at = pl.ds(pl.multiple_of(i * width, width), width)
        second = second_ref[:, at]
        owner = second // orbits
        keys = owner * LANES + (second - owner * orbits)
        hot = one_hot(keys, slabs * LANES)
        sums = jnp.dot(
            jnp.concatenate([aligned_ref[s] for s in range(slabs)], axis=1),
            hot,
            preferred_element_type=jnp.float32,
        )
        zero = jnp.zeros((pairs, width), jnp.float32)
        direct_ref[:, at] = picked(first_ref[:, at], sums, pairs, zero).astype(jnp.bfloat16)
        return carry

    lax.fori_loop(0, columns // width, step, 0)


def crossed_kernel(slabs, orbits, pairs, me_ref, aligned_ref, key_ref, group_ref, crossed_ref):
    columns = key_ref.shape[2]
    width = chunk_of(columns)
    me = me_ref[0]
    halves = orbits // 2

    def slab_step(s, carry):
        def step(i, inner):
            at = pl.ds(pl.multiple_of(i * width, width), width)
            hot = one_hot(key_ref[s, :, at], 2 * LANES)
            even = aligned_ref[s, :, 0].reshape(halves * pairs, LANES)
            odd = aligned_ref[s, :, 1].reshape(halves * pairs, LANES)
            sums = jnp.dot(
                jnp.concatenate([even, odd], axis=1), hot, preferred_element_type=jnp.float32
            )
            zero = jnp.zeros((pairs, width), jnp.float32)
            crossed_ref[s, :, at] = picked(group_ref[s, :, at], sums, pairs, zero).astype(
                jnp.bfloat16
            )
            return inner

        return lax.fori_loop(0, columns // width, step, carry)

    def blank(s, carry):
        crossed_ref[s] = jnp.zeros(crossed_ref.shape[1:], jnp.bfloat16)
        return carry

    lax.fori_loop(0, me + 1, slab_step, 0)
    lax.fori_loop(me + 1, slabs, blank, 0)


def ladder_kernel(slabs, packed_ref, values_ref, out_ref):
    width = out_ref.shape[2]
    out_ref[0] = lax.dot_general(
        packed_ref[...],
        values_ref[...],
        (((1,), (1,)), ((), ())),
        preferred_element_type=jnp.float32,
    ).astype(jnp.bfloat16)


def on_device(pair_values, amplitudes, cd_first, cd_second, live_cols):
    slab = lax.axis_index("cd")
    slabs = lax.axis_size("cd")
    blocks = lax.axis_size("ab")
    pair_block, orbits, orbitals = amplitudes.shape
    columns = cd_first.shape[0]
    rows = pair_values.shape[0]
    pairs = -(-pair_block // 16) * 16
    table = jnp.transpose(amplitudes, (1, 0, 2))
    if pairs != pair_block:
        table = jnp.pad(table, ((0, 0), (0, pairs - pair_block), (0, 0)))
    table = table.reshape(orbits * pairs, orbitals)
    vmem = pl.BlockSpec(memory_space=pltpu.VMEM)
    params = pltpu.CompilerParams(vmem_limit_bytes=VMEM_LIMIT)

    local_first = cd_first - slab * orbits
    coded = (local_first * orbitals + cd_second).reshape(1, columns // LANES, LANES)
    coded = lax.all_to_all(
        jnp.broadcast_to(coded, (slabs,) + coded.shape[1:]), "cd", split_axis=0, concat_axis=0, tiled=True
    )
    aligned, direct = pl.pallas_call(
        functools.partial(direct_kernel, slabs, orbits, pairs),
        out_shape=(
            jax.ShapeDtypeStruct((slabs, orbits * pairs, LANES), jnp.bfloat16),
            jax.ShapeDtypeStruct((pairs, columns), jnp.bfloat16),
        ),
        in_specs=[vmem] * 3,
        out_specs=(vmem, vmem),
        compiler_params=params,
        cost_estimate=pl.CostEstimate(
            flops=2 * orbits * pairs * slabs * LANES * columns, bytes_accessed=6_000_000, transcendentals=0
        ),
        name="direct",
    )(table, local_first.reshape(1, columns), cd_second.reshape(1, columns))

    coded = coded.reshape(slabs, 1, columns)
    first = coded // orbitals
    second = coded - first * orbitals - slab * orbits
    keys = jnp.where(second % 2 == 0, first, first + LANES)
    groups = second >> 1
    crossed = pl.pallas_call(
        functools.partial(crossed_kernel, slabs, orbits, pairs),
        out_shape=jax.ShapeDtypeStruct((slabs, pairs, columns), jnp.bfloat16),
        in_specs=[pl.BlockSpec(memory_space=pltpu.SMEM)] + [vmem] * 3,
        out_specs=vmem,
        compiler_params=params,
        cost_estimate=pl.CostEstimate(
            flops=slabs * orbits * pairs * 2 * LANES * columns, bytes_accessed=6_000_000, transcendentals=0
        ),
        name="crossed",
    )(
        slab.astype(jnp.int32).reshape(1),
        aligned.reshape(slabs, orbits // 2, 2, pairs, LANES),
        keys,
        groups,
    )
    crossed = lax.all_to_all(crossed, "cd", split_axis=0, concat_axis=0, tiled=True)
    crossed = jnp.sum(crossed.astype(jnp.float32), axis=0)

    slots = jnp.arange(columns, dtype=jnp.int32)
    live = (slots < live_cols[0]).astype(jnp.float32)
    half = jnp.where(cd_first == cd_second, jnp.float32(0.5), jnp.float32(1.0))
    packed = ((direct.astype(jnp.float32) + crossed) * (half * live)[None, :]).astype(jnp.bfloat16)
    packed = lax.all_gather(packed[:pair_block], "ab", axis=0, tiled=True)

    width = rows // slabs
    partial_sums = pl.pallas_call(
        functools.partial(ladder_kernel, slabs),
        out_shape=jax.ShapeDtypeStruct((slabs, blocks * pair_block, width), jnp.bfloat16),
        grid=(slabs,),
        in_specs=[
            pl.BlockSpec((blocks * pair_block, columns), lambda i: (0, 0)),
            pl.BlockSpec((width, columns), lambda i: (i, 0)),
        ],
        out_specs=pl.BlockSpec((1, blocks * pair_block, width), lambda i: (i, 0, 0)),
        compiler_params=params,
        cost_estimate=pl.CostEstimate(
            flops=2 * blocks * pair_block * columns * rows, bytes_accessed=rows * columns * 2, transcendentals=0
        ),
        name="ladder",
    )(packed, pair_values)
    partial_sums = lax.all_to_all(partial_sums, "cd", split_axis=0, concat_axis=0, tiled=True)
    return jnp.sum(partial_sums.astype(jnp.float32), axis=0).astype(jnp.bfloat16)


def solution(mesh):
    placed = (P("ab", "cd"), P("ab", "cd", None), P("cd"), P("cd"), P("cd"))
    return jax.shard_map(
        on_device, mesh=mesh, in_specs=placed, out_specs=P(None, ("ab", "cd")), check_vma=False
    )
```

time: 221 us -> 81.2 us (0.37)
  waiting for transfers between devices: 100 us -> 13.3 us
  local copies, waits for them, and re-layouts: 83.6 us -> 3.14 us
  Pallas kernels: 0 us -> 18.8 us
  starting transfers between devices: 7.29 us -> 23.8 us
  between operations: 14.1 us -> 0.75 us
  blocking collectives: 5.79 us -> 18.7 us
  matrix products: 6.83 us -> 0 us
    reduce_scatter x1 -> x0, waiting for transfers between devices: 61.6 us -> none  [on_device(): lax.psum_scatter(partial_sums, 'cd', scatter_dimension=1, tiled=True)]
    gather x4 -> x0, local copies, waits for them, and re-layouts: 33.5 us -> none  [the longest x2 18.3 us: on_device(): direct = jnp.take(own_flat, local_first * orbitals + cd_second, axis=1)]
    all_to_all x1 -> x2, waiting for transfers between devices: 38.8 us -> 13.3 us  [the longest x1 13.3 us: on_device(): lax.all_to_all(crossed, 'cd', split_axis=0, concat_axis=0, tiled=True)]
    unnamed x8, local copies, waits for them, and re-layouts: 24.1 us -> 2.52 us
    reshape x2 -> x0, local copies, waits for them, and re-layouts: 20.3 us -> none  [on_device(): mirror_flat = mirrored.reshape(pair_block, orbitals * orbit_block)]
    pallas_call x0 -> x3, Pallas kernels: none -> 18.8 us  [the longest x1 9.12 us: on_device(): pl.pallas_call(functools.partial(direct_kernel, slabs, orbits, pairs), ou...]
    all_to_all x1 -> x2, starting transfers between devices: 7.25 us -> 23.8 us  [the longest x1 16.6 us: on_device(): lax.all_to_all(crossed, 'cd', split_axis=0, concat_axis=0, tiled=True)]
    all_to_all x0 -> x1, blocking collectives: none -> 12.9 us  [on_device(): lax.all_to_all(partial_sums, 'cd', split_axis=0, concat_axis=0, tiled=True)]
  transfers between devices with their start and end apart: 2 -> 2, of which waited for: 2 -> 1; matrix products, arithmetic and copies ran while one was open for 15% -> 0% of each run, Pallas kernels for 0% -> 11%
where the time goes in v1:
time: 81.2 us; the launch traced here: 80.7 us
  starting transfers between devices  23.8 us (29%)
  Pallas kernels  18.8 us (23%)
  blocking collectives  18.7 us (23%)
  waiting for transfers between devices  13.3 us (16%)
  local copies, waits for them, and re-layouts  3.14 us (4%)
  other arithmetic  2.18 us (3%)
    all_to_all x1, starting transfers between devices, on_device(): lax.all_to_all(crossed, 'cd', split_axis=0, concat_axis=0, tiled=True)  16.6 us
    all_to_all x1, waiting for transfers between devices, on_device(): lax.all_to_all(crossed, 'cd', split_axis=0, concat_axis=0, tiled=True)  13.3 us
    all_to_all x1, blocking collectives, on_device(): lax.all_to_all(partial_sums, 'cd', split_axis=0, concat_axis=0, tiled=True)  12.9 us
    pallas_call x1, Pallas kernels, on_device(): pl.pallas_call(functools.partial(direct_kernel, slabs, orbits, pairs), ou...  9.12 us
    pallas_call x1, Pallas kernels, on_device(): pl.pallas_call(functools.partial(ladder_kernel, slabs), out_shape=jax.Sha...  7.37 us
    all_to_all x1, starting transfers between devices, on_device(): lax.all_to_all(jnp.broadcast_to(coded, (slabs,) + coded.shape[1:]), 'cd',...  7.25 us
    all_gather x1, blocking collectives, on_device(): packed = lax.all_gather(packed[:pair_block], 'ab', axis=0, tiled=True)  5.79 us
    unnamed x8, local copies, waits for them, and re-layouts  2.52 us
  transfers between devices with their start and end apart: 2, of which 1 were waited for; matrix products, arithmetic and copies ran while one was open for 0% of the time, Pallas kernels for 11%

profile of v1, /device:TPU:0, one launch (start us, length us, event | category | flops | bytes accessed | tf_op | source)
XLA Modules:
  0.0 80.7 jit_solution(12532775869496747489)
XLA Ops:
  0.0 0.7 add_bitcast_fusion
  0.7 0.6 broadcast_in_dim.17
  1.3 7.3 %all-to-all-start = ((s32[8,16,128]{2,1,0:T(8,128)}), s32[8,16,128]{2,1,0:T(8,128)S(1)}, u32[]{:S(2)}, u32[]{:S(2)}) async-start(s32[8,16,128]{2,1,0:T(8,128)} %broadcast_in_dim.17), calls=%async_computation | async-start | bytes 131072 | tf_op jit(solution)/shard_map/all_to_all | solution.py:118
  8.6 0.0 copy-start
  8.6 0.7 copy-done
  9.3 0.0 copy-start.2
  9.3 1.8 %copy-done.2 = bf16[16,100,800]{2,0,1:T(8,128)(2,1)S(1)} copy-done((bf16[16,100,800]{2,0,1:T(8,128)(2,1)S(1)}, bf16[16,100,800]{2,0,1:T(8,128)(2,1)}, u32[]{:S(2)}) %copy-start.2) | copy-done | bytes 2560024
  11.1 9.1 %direct.1 = (bf16[8,1600,128]{2,1,0:T(8,128)(2,1)S(1)}, bf16[16,2048]{1,0:T(8,128)(2,1)S(1)}) custom-call(bf16[1600,800]{1,0:T(8,128)(2,1)S(1)} %bitcast.14, s32[1,2048]{1,0:T(1,128)S(1)} %bitcast.13, s32[1,2048]{1,0:T(1,128)S(1)} %bitcast.12), custom_call_target="tpu_custom_call" | custom-call | flops 6710886400 | bytes 6000000 | tf_op jit(solution)/shard_map/direct/pallas_call | solution.py:121
  20.2 0.0 all-to-all-done
  20.2 0.4 broadcast_shift-right-arithmetic_fusion
  20.7 0.3 compare_select_fusion.2.key_ref
  21.0 0.0 copy-start.1
  21.0 0.0 copy-start.3
  21.0 2.4 %crossed.1 = bf16[8,16,2048]{2,1,0:T(8,128)(2,1)} custom-call(s32[1]{0:T(128)} %bitcast.4.me_ref, bf16[8,50,2,16,128]{4,3,2,1,0:T(8,128)(2,1)S(1)} %bitcast.15, s32[8,1,2048]{2,1,0:T(1,128)S(1)} %compare_select_fusion.2.key_ref, s32[8,1,2048]{2,1,0:T(1,128)S(1)} %get-tuple-element.9.group_ref), custom_call_target="tpu_custom_call" | custom-call | flops 6710886400 | bytes 6000000 | tf_op jit(solution)/shard_map/crossed/pallas_call | solution.py:141
  23.3 16.6 %all-to-all-start.1 = ((bf16[8,16,2048]{2,1,0:T(8,128)(2,1)}), bf16[8,16,2048]{2,1,0:T(8,128)(2,1)S(1)}, u32[]{:S(2)}, u32[]{:S(2)}) async-start(bf16[8,16,2048]{2,1,0:T(8,128)(2,1)} %crossed.1), calls=%async_computation.1 | async-start | bytes 1048576 | tf_op jit(solution)/shard_map/all_to_all | solution.py:157
  40.6 0.0 copy-done.1
  40.6 0.0 copy-done.3
  40.6 13.3 %all-to-all-done.1 = bf16[8,16,2048]{2,1,0:T(8,128)(2,1)S(1)} async-done(((bf16[8,16,2048]{2,1,0:T(8,128)(2,1)}), bf16[8,16,2048]{2,1,0:T(8,128)(2,1)S(1)}, u32[]{:S(2)}, u32[]{:S(2)}) %all-to-all-start.1) | async-done | bytes 524320 | tf_op jit(solution)/shard_map/all_to_all | solution.py:157
  53.9 0.1 convert_reduce_fusion
  54.0 5.8 %all_gather.3.packed_ref = bf16[64,2048]{1,0:T(8,128)(2,1)S(1)} all-gather(bf16[16,2048]{1,0:T(8,128)(2,1)S(1)} %multiply_convert_fusion), channel_id=1, replica_groups=mesh['ab'=4,'cd'=8] {'ab'}, dimensions={0}, use_global_device_ids=true | all-gather | bytes 327680 | tf_op jit(solution)/shard_map/all_gather | solution.py:164
  59.8 7.4 %ladder.1 = bf16[8,64,256]{2,1,0:T(8,128)(2,1)S(1)} custom-call(bf16[64,2048]{1,0:T(8,128)(2,1)S(1)} %all_gather.3.packed_ref, bf16[2048,2048]{1,0:T(8,128)(2,1)} %values_ref.1), custom_call_target="tpu_custom_call" | custom-call | flops 536870912 | bytes 8388608 | tf_op jit(solution)/shard_map/ladder/pallas_call | solution.py:167
  67.2 12.9 %all_to_all.15 = bf16[8,64,256]{2,1,0:T(8,128)(2,1)S(1)} all-to-all(bf16[8,64,256]{2,1,0:T(8,128)(2,1)S(1)} %ladder.1), channel_id=1, replica_groups=mesh['ab'=4,'cd'=8] {'cd'}, dimensions={0} | all-to-all | bytes 524288 | tf_op jit(solution)/shard_map/all_to_all | solution.py:182
  80.0 0.7 reduce_sum.22
  (2 shorter events, 0.0 us)
Async XLA Ops:
  1.3 18.9 %all-to-all-start = ((s32[8,16,128]{2,1,0:T(8,128)}), s32[8,16,128]{2,1,0:T(8,128)S(1)}, u32[]{:S(2)}, u32[]{:S(2)}) async-start(s32[8,16,128]{2,1,0:T(8,128)} %broadcast_in_dim.17), calls=%async_computation | async-start | bytes 131072 | tf_op jit(solution)/shard_map/all_to_all | solution.py:118
  8.6 0.7 copy-start
  9.3 1.8 %copy-start.2 = (bf16[16,100,800]{2,0,1:T(8,128)(2,1)S(1)}, bf16[16,100,800]{2,0,1:T(8,128)(2,1)}, u32[]{:S(2)}) copy-start(bf16[16,100,800]{2,0,1:T(8,128)(2,1)} %param.6) | copy-start | bytes 7680004
  21.0 19.6 %copy-start.1 = (s32[2048]{0:T(1024)S(1)}, s32[2048]{0:T(1024)}, u32[]{:S(2)}) copy-start(s32[2048]{0:T(1024)} %param.8) | copy-start | bytes 24580
  21.0 19.6 %copy-start.3 = (s32[2048]{0:T(1024)S(1)}, s32[2048]{0:T(1024)}, u32[]{:S(2)}) copy-start(s32[2048]{0:T(1024)} %param.7) | copy-start | bytes 24580
  23.3 30.6 %all-to-all-start.1 = ((bf16[8,16,2048]{2,1,0:T(8,128)(2,1)}), bf16[8,16,2048]{2,1,0:T(8,128)(2,1)S(1)}, u32[]{:S(2)}, u32[]{:S(2)}) async-start(bf16[8,16,2048]{2,1,0:T(8,128)(2,1)} %crossed.1), calls=%async_computation.1 | async-start | bytes 1048576 | tf_op jit(solution)/shard_map/all_to_all | solution.py:157

commit v2 on v0

v2 whole, which is shorter than its diff:
```python
import functools

import jax
import jax.numpy as jnp
from jax import lax
from jax.experimental import pallas as pl
from jax.experimental.pallas import tpu as pltpu
from jax.sharding import PartitionSpec as P

LANES = 128
DEPTH = 512
MIB = 1024 * 1024
VMEM = pl.BlockSpec(memory_space=pltpu.VMEM)


def group_size(orbits):
    return max(g for g in range(1, orbits + 1) if orbits % g == 0 and g * orbits <= DEPTH)


def params(mib):
    return pltpu.CompilerParams(vmem_limit_bytes=mib * MIB)


def cost(flops, bytes_accessed):
    return pl.CostEstimate(flops=flops, bytes_accessed=bytes_accessed, transcendentals=0)


def code_kernel(slabs, orbits, shift, first_ref, second_ref, coded_ref):
    base = lax.axis_index("cd") * orbits
    coded = ((first_ref[...] - base) << shift) + second_ref[...]
    for s in range(slabs):
        coded_ref[s] = coded


def pack_kernel(slabs, orbits, group, pairs, table_ref, packed_ref):
    for s in range(slabs):
        for g in range(table_ref.shape[0] // (group * pairs)):
            parts = [
                table_ref[(g * group + k) * pairs : (g * group + k + 1) * pairs, s * orbits : (s + 1) * orbits]
                for k in range(group)
            ]
            if group * orbits < DEPTH:
                parts.append(jnp.zeros((pairs, DEPTH - group * orbits), jnp.bfloat16))
            packed_ref[s, g * pairs : (g + 1) * pairs, :] = jnp.concatenate(parts, axis=1)


def lookup(table, pairs, keys, groups, totals):
    per_row = keys.shape[0]
    width = per_row * LANES
    key = jnp.concatenate([keys[j : j + 1] for j in range(per_row)], axis=1)
    chosen = jnp.concatenate([groups[j : j + 1] for j in range(per_row)], axis=1)
    hot = jnp.where(lax.broadcasted_iota(jnp.int32, (DEPTH, width), 0) == key, 1.0, 0.0).astype(jnp.bfloat16)
    sums = jnp.dot(table, hot, preferred_element_type=jnp.float32)
    chosen = jnp.broadcast_to(chosen, (8, width))
    totals = list(totals)
    for g in range(table.shape[0] // pairs):
        mine = chosen == g
        for t in range(pairs // 8):
            at = g * pairs + t * 8
            totals[t] = jnp.where(mine, sums[at : at + 8], totals[t])
    return totals


def crossed_kernel(slabs, orbits, group, pairs, shift, packed_ref, coded_ref, crossed_ref):
    base = lax.axis_index("cd") * orbits
    lines = coded_ref.shape[1]
    for s in range(slabs):
        coded = coded_ref[s]
        first = coded >> shift
        second = (coded & ((1 << shift) - 1)) - base
        here = jnp.logical_and(second >= 0, second < orbits)
        second = jnp.where(here, second, 0)
        groups = lax.div(second, jnp.int32(group))
        keys = (second - groups * group) * orbits + first
        groups = jnp.where(here, groups, -1)
        step = min(lines, 4)
        for i in range(0, lines, step):
            zero = [jnp.zeros((8, step * LANES), jnp.float32)] * (pairs // 8)
            got = lookup(packed_ref[s], pairs, keys[i : i + step], groups[i : i + step], zero)
            crossed_ref[s, :, i * LANES : (i + step) * LANES] = jnp.concatenate(got, axis=0).astype(jnp.bfloat16)


def direct_kernel(slabs, orbits, group, pairs, shift, packed_ref, coded_ref, direct_ref):
    coded = coded_ref[lax.axis_index("cd")]
    first = coded >> shift
    second = coded & ((1 << shift) - 1)
    groups = lax.div(first, jnp.int32(group))
    owner = lax.div(second, jnp.int32(orbits))
    keys = (first - groups * group) * orbits + (second - owner * orbits)
    lines = coded.shape[0]
    step = min(lines, 4)
    for i in range(0, lines, step):
        got = [jnp.zeros((8, step * LANES), jnp.float32)] * (pairs // 8)
        for s in range(slabs):
            chosen = jnp.where(owner[i : i + step] == s, groups[i : i + step], -1)
            got = lookup(packed_ref[s], pairs, keys[i : i + step], chosen, got)
        direct_ref[:, i * LANES : (i + step) * LANES] = jnp.concatenate(got, axis=0).astype(jnp.bfloat16)


def ladder_kernel(packed_ref, values_ref, out_ref):
    slabs, _, width = out_ref.shape
    for s in range(slabs):
        out_ref[s] = lax.dot_general(
            values_ref[s * width : (s + 1) * width, :],
            packed_ref[...],
            (((1,), (1,)), ((), ())),
            preferred_element_type=jnp.float32,
        ).T.astype(jnp.bfloat16)


def on_device(pair_values, amplitudes, cd_first, cd_second, live_cols):
    slabs = lax.axis_size("cd")
    blocks = lax.axis_size("ab")
    pair_block, orbits, orbitals = amplitudes.shape
    columns = cd_first.shape[0]
    rows = pair_values.shape[0]
    lines = columns // LANES
    pairs = -(-pair_block // 16) * 16
    group = group_size(orbits)
    shift = (orbitals - 1).bit_length()

    coded = pl.pallas_call(
        functools.partial(code_kernel, slabs, orbits, shift),
        out_shape=jax.ShapeDtypeStruct((slabs, lines, LANES), jnp.int32),
        in_specs=[VMEM] * 2,
        out_specs=VMEM,
        compiler_params=params(4),
        cost_estimate=cost(slabs * columns, slabs * columns * 4),
        name="code",
    )(cd_first.reshape(lines, LANES), cd_second.reshape(lines, LANES))
    coded = lax.all_to_all(coded, "cd", split_axis=0, concat_axis=0, tiled=True)

    table = jnp.transpose(amplitudes, (1, 0, 2))
    if pairs != pair_block:
        table = jnp.pad(table, ((0, 0), (0, pairs - pair_block), (0, 0)))
    table = table.reshape(orbits * pairs, orbitals)
    packed_rows = orbits // group * pairs
    steps = 4 if orbits // group % 4 == 0 else 1
    table = pl.pallas_call(
        functools.partial(pack_kernel, slabs, orbits, group, pairs),
        out_shape=jax.ShapeDtypeStruct((slabs, packed_rows, DEPTH), jnp.bfloat16),
        grid=(steps,),
        in_specs=[pl.BlockSpec((orbits * pairs // steps, orbitals), lambda i: (i, 0))],
        out_specs=pl.BlockSpec((slabs, packed_rows // steps, DEPTH), lambda i: (0, i, 0)),
        compiler_params=params(16),
        cost_estimate=cost(0, 4 * orbits * pairs * orbitals),
        name="pack",
    )(table)

    lookup_flops = 2 * slabs * packed_rows * DEPTH * columns
    lookup_bytes = slabs * packed_rows * DEPTH * 2 + slabs * columns * pairs * 2
    crossed = pl.pallas_call(
        functools.partial(crossed_kernel, slabs, orbits, group, pairs, shift),
        out_shape=jax.ShapeDtypeStruct((slabs, pairs, columns), jnp.bfloat16),
        in_specs=[VMEM] * 2,
        out_specs=VMEM,
        compiler_params=params(20),
        cost_estimate=cost(lookup_flops, lookup_bytes),
        name="crossed",
    )(table, coded)
    crossed = lax.all_to_all(crossed, "cd", split_axis=0, concat_axis=0, tiled=True)
    direct = pl.pallas_call(
        functools.partial(direct_kernel, slabs, orbits, group, pairs, shift),
        out_shape=jax.ShapeDtypeStruct((pairs, columns), jnp.bfloat16),
        in_specs=[VMEM] * 2,
        out_specs=VMEM,
        compiler_params=params(20),
        cost_estimate=cost(lookup_flops, lookup_bytes),
        name="direct",
    )(table, coded)
    crossed = jnp.sum(crossed.astype(jnp.float32), axis=0)

    slots = jnp.arange(columns, dtype=jnp.int32)
    live = (slots < live_cols[0]).astype(jnp.float32)
    half = jnp.where(cd_first == cd_second, jnp.float32(0.5), jnp.float32(1.0))
    packed = ((direct.astype(jnp.float32) + crossed) * (half * live)[None, :]).astype(jnp.bfloat16)
    packed = lax.all_gather(packed[:pair_block], "ab", axis=0, tiled=True)

    width = rows // slabs
    partial_sums = pl.pallas_call(
        ladder_kernel,
        out_shape=jax.ShapeDtypeStruct((slabs, blocks * pair_block, width), jnp.bfloat16),
        in_specs=[VMEM] * 2,
        out_specs=VMEM,
        compiler_params=params(20),
        cost_estimate=cost(2 * blocks * pair_block * columns * rows, rows * columns * 2),
        name="ladder",
    )(packed, pair_values)
    partial_sums = lax.all_to_all(partial_sums, "cd", split_axis=0, concat_axis=0, tiled=True)
    return jnp.sum(partial_sums.astype(jnp.float32), axis=0).astype(jnp.bfloat16)


def solution(mesh):
    placed = (P("ab", "cd"), P("ab", "cd", None), P("cd"), P("cd"), P("cd"))
    return jax.shard_map(
        on_device, mesh=mesh, in_specs=placed, out_specs=P(None, ("ab", "cd")), check_vma=False
    )
```

time: 221 us -> 66 us (0.30)
  waiting for transfers between devices: 100 us -> 10.1 us
  local copies, waits for them, and re-layouts: 83.6 us -> 6.59 us
  Pallas kernels: 0 us -> 17.9 us
  between operations: 14.1 us -> 0.73 us
  blocking collectives: 5.79 us -> 18.7 us
  matrix products: 6.83 us -> 0 us
  starting transfers between devices: 7.29 us -> 10.7 us
    reduce_scatter x1 -> x0, waiting for transfers between devices: 61.6 us -> none  [on_device(): lax.psum_scatter(partial_sums, 'cd', scatter_dimension=1, tiled=True)]
    gather x4 -> x0, local copies, waits for them, and re-layouts: 33.5 us -> none  [the longest x2 18.3 us: on_device(): direct = jnp.take(own_flat, local_first * orbitals + cd_second, axis=1)]
    all_to_all x1 -> x2, waiting for transfers between devices: 38.8 us -> 10.1 us  [the longest x1 6.8 us: on_device(): lax.all_to_all(crossed, 'cd', split_axis=0, concat_axis=0, tiled=True)]
    reshape x2 -> x0, local copies, waits for them, and re-layouts: 20.3 us -> none  [on_device(): mirror_flat = mirrored.reshape(pair_block, orbitals * orbit_block)]
    pallas_call x0 -> x5, Pallas kernels: none -> 17.9 us  [the longest x1 7.41 us: on_device(): pl.pallas_call(functools.partial(crossed_kernel, slabs, orbits, group, pa...]
    unnamed x8 -> x12, local copies, waits for them, and re-layouts: 24.1 us -> 6.59 us
    all_to_all x0 -> x1, blocking collectives: none -> 12.9 us  [on_device(): lax.all_to_all(partial_sums, 'cd', split_axis=0, concat_axis=0, tiled=True)]
    dot_general x1 -> x0, matrix products: 6.83 us -> none  [on_device(): lax.dot_general(lax.all_gather(packed, 'ab', axis=0, tiled=True), pair_va...]
  transfers between devices with their start and end apart: 2 -> 2, of which waited for: 2 -> 2; matrix products, arithmetic and copies ran while one was open for 15% -> 0% of each run, Pallas kernels for 0% -> 11%
where the time goes in v2:
time: 66 us; the launch traced here: 65.5 us
  blocking collectives  18.7 us (28%)
  Pallas kernels  17.9 us (27%)
  starting transfers between devices  10.7 us (16%)
  waiting for transfers between devices  10.1 us (15%)
  local copies, waits for them, and re-layouts  6.59 us (10%)
  other arithmetic  0.75 us (1%)
  between operations  0.73 us (1%)
    all_to_all x1, blocking collectives, on_device(): lax.all_to_all(partial_sums, 'cd', split_axis=0, concat_axis=0, tiled=True)  12.9 us
    pallas_call x1, Pallas kernels, on_device(): pl.pallas_call(functools.partial(crossed_kernel, slabs, orbits, group, pa...  7.41 us
    all_to_all x1, starting transfers between devices, on_device(): coded = lax.all_to_all(coded, 'cd', split_axis=0, concat_axis=0, tiled=True)  7.25 us
    all_to_all x1, waiting for transfers between devices, on_device(): lax.all_to_all(crossed, 'cd', split_axis=0, concat_axis=0, tiled=True)  6.8 us
    unnamed x12, local copies, waits for them, and re-layouts  6.59 us
    all_gather x1, blocking collectives, on_device(): packed = lax.all_gather(packed[:pair_block], 'ab', axis=0, tiled=True)  5.79 us
    pallas_call x1, Pallas kernels, on_device(): pl.pallas_call(functools.partial(direct_kernel, slabs, orbits, group, pai...  5.77 us
    all_to_all x1, starting transfers between devices, on_device(): lax.all_to_all(crossed, 'cd', split_axis=0, concat_axis=0, tiled=True)  3.49 us
  transfers between devices with their start and end apart: 2, of which 2 were waited for; matrix products, arithmetic and copies ran while one was open for 0% of the time, Pallas kernels for 11%

profile of v2, /device:TPU:0, one launch (start us, length us, event | category | flops | bytes accessed | tf_op | source)
XLA Modules:
  0.0 65.5 jit_solution(9542883601257535375)
XLA Ops:
  0.0 0.0 copy-start.2
  0.0 0.7 %copy-done.2 = s32[2048]{0:T(1024)S(1)} copy-done((s32[2048]{0:T(1024)S(1)}, s32[2048]{0:T(1024)}, u32[]{:S(2)}) %copy-start.2) | copy-done | bytes 8216
  0.7 0.0 copy-start.4
  0.7 0.7 %copy-done.4 = s32[2048]{0:T(1024)S(1)} copy-done((s32[2048]{0:T(1024)S(1)}, s32[2048]{0:T(1024)}, u32[]{:S(2)}) %copy-start.4) | copy-done | bytes 8216
  1.4 0.6 code.1
  2.0 7.3 %all-to-all-start = ((s32[8,16,128]{2,1,0:T(8,128)}), s32[8,16,128]{2,1,0:T(8,128)S(1)}, u32[]{:S(2)}, u32[]{:S(2)}) async-start(s32[8,16,128]{2,1,0:T(8,128)} %code.1), calls=%async_computation | async-start | bytes 131072 | tf_op jit(solution)/shard_map/all_to_all | solution.py:131
  9.3 0.0 copy-start.1
  9.3 1.8 %copy-done.1 = bf16[16,100,800]{2,0,1:T(8,128)(2,1)S(1)} copy-done((bf16[16,100,800]{2,0,1:T(8,128)(2,1)S(1)}, bf16[16,100,800]{2,0,1:T(8,128)(2,1)}, u32[]{:S(2)}) %copy-start.1) | copy-done | bytes 2560024
  11.1 1.7 %pack.1.packed_ref = bf16[8,320,512]{2,1,0:T(8,128)(2,1)S(1)} custom-call(bf16[1600,800]{1,0:T(8,128)(2,1)S(1)} %bitcast.7), custom_call_target="tpu_custom_call" | custom-call | bytes 5120000 | tf_op jit(solution)/shard_map/pack/pallas_call | solution.py:139
  12.8 0.0 copy-start.3
  12.8 0.0 copy-start.5
  12.8 3.3 %all-to-all-done.coded_ref = s32[8,16,128]{2,1,0:T(8,128)S(1)} async-done(((s32[8,16,128]{2,1,0:T(8,128)}), s32[8,16,128]{2,1,0:T(8,128)S(1)}, u32[]{:S(2)}, u32[]{:S(2)}) %all-to-all-start) | async-done | bytes 65568 | tf_op jit(solution)/shard_map/all_to_all | solution.py:131
  16.2 7.4 %crossed.1 = bf16[8,16,2048]{2,1,0:T(8,128)(2,1)} custom-call(bf16[8,320,512]{2,1,0:T(8,128)(2,1)S(1)} %pack.1.packed_ref, s32[8,16,128]{2,1,0:T(8,128)S(1)} %all-to-all-done.coded_ref), custom_call_target="tpu_custom_call" | custom-call | flops 5368709120 | bytes 3145728 | tf_op jit(solution)/shard_map/crossed/pallas_call | solution.py:152
  23.6 3.5 %all-to-all-start.1 = ((bf16[8,16,2048]{2,1,0:T(8,128)(2,1)}), bf16[8,16,2048]{2,1,0:T(8,128)(2,1)S(1)}, u32[]{:S(2)}, u32[]{:S(2)}) async-start(bf16[8,16,2048]{2,1,0:T(8,128)(2,1)} %crossed.1), calls=%async_computation.1 | async-start | bytes 1048576 | tf_op jit(solution)/shard_map/all_to_all | solution.py:161
  27.7 0.0 copy-done.3
  27.7 0.0 copy-done.5
  27.8 5.8 %direct.1 = bf16[16,2048]{1,0:T(8,128)(2,1)S(1)} custom-call(bf16[8,320,512]{2,1,0:T(8,128)(2,1)S(1)} %pack.1.packed_ref, s32[8,16,128]{2,1,0:T(8,128)S(1)} %all-to-all-done.coded_ref), custom_call_target="tpu_custom_call" | custom-call | flops 5368709120 | bytes 3145728 | tf_op jit(solution)/shard_map/direct/pallas_call | solution.py:162
  33.5 6.8 %all-to-all-done.1 = bf16[8,16,2048]{2,1,0:T(8,128)(2,1)S(1)} async-done(((bf16[8,16,2048]{2,1,0:T(8,128)(2,1)}), bf16[8,16,2048]{2,1,0:T(8,128)(2,1)S(1)}, u32[]{:S(2)}, u32[]{:S(2)}) %all-to-all-start.1) | async-done | bytes 524320 | tf_op jit(solution)/shard_map/all_to_all | solution.py:161
  40.3 0.1 convert_reduce_fusion
  40.4 5.8 %all_gather.3.packed_ref = bf16[64,2048]{1,0:T(8,128)(2,1)S(1)} all-gather(bf16[16,2048]{1,0:T(8,128)(2,1)S(1)} %multiply_convert_fusion), channel_id=1, replica_groups=mesh['ab'=4,'cd'=8] {'ab'}, dimensions={0}, use_global_device_ids=true | all-gather | bytes 327680 | tf_op jit(solution)/shard_map/all_gather | solution.py:177
  46.2 0.0 copy-start
  46.2 3.4 %copy-done = bf16[2048,2048]{1,0:T(8,128)(2,1)S(1)} copy-done((bf16[2048,2048]{1,0:T(8,128)(2,1)S(1)}, bf16[2048,2048]{1,0:T(8,128)(2,1)}, u32[]{:S(2)}) %copy-start) | copy-done | bytes 8388632
  49.6 2.4 %ladder.1 = bf16[8,64,256]{2,1,0:T(8,128)(2,1)S(1)} custom-call(bf16[64,2048]{1,0:T(8,128)(2,1)S(1)} %all_gather.3.packed_ref, bf16[2048,2048]{1,0:T(8,128)(2,1)S(1)} %copy-done), custom_call_target="tpu_custom_call" | custom-call | flops 536870912 | bytes 8388608 | tf_op jit(solution)/shard_map/ladder/pallas_call | solution.py:180
  52.0 12.9 %all_to_all.15 = bf16[8,64,256]{2,1,0:T(8,128)(2,1)S(1)} all-to-all(bf16[8,64,256]{2,1,0:T(8,128)(2,1)S(1)} %ladder.1), channel_id=1, replica_groups=mesh['ab'=4,'cd'=8] {'cd'}, dimensions={0} | all-to-all | bytes 524288 | tf_op jit(solution)/shard_map/all_to_all | solution.py:189
  64.9 0.7 reduce_sum.22
  (2 shorter events, 0.0 us)
Async XLA Ops:
  0.0 0.7 %copy-start.2 = (s32[2048]{0:T(1024)S(1)}, s32[2048]{0:T(1024)}, u32[]{:S(2)}) copy-start(s32[2048]{0:T(1024)} %param.7) | copy-start | bytes 24580
  0.7 0.7 %copy-start.4 = (s32[2048]{0:T(1024)S(1)}, s32[2048]{0:T(1024)}, u32[]{:S(2)}) copy-start(s32[2048]{0:T(1024)} %param.8) | copy-start | bytes 24580
  2.0 14.2 %all-to-all-start = ((s32[8,16,128]{2,1,0:T(8,128)}), s32[8,16,128]{2,1,0:T(8,128)S(1)}, u32[]{:S(2)}, u32[]{:S(2)}) async-start(s32[8,16,128]{2,1,0:T(8,128)} %code.1), calls=%async_computation | async-start | bytes 131072 | tf_op jit(solution)/shard_map/all_to_all | solution.py:131
  9.3 1.8 %copy-start.1 = (bf16[16,100,800]{2,0,1:T(8,128)(2,1)S(1)}, bf16[16,100,800]{2,0,1:T(8,128)(2,1)}, u32[]{:S(2)}) copy-start(bf16[16,100,800]{2,0,1:T(8,128)(2,1)} %param.6) | copy-start | bytes 7680004
  12.8 14.9 %copy-start.3 = (s32[2048]{0:T(1024)S(1)}, s32[2048]{0:T(1024)}, u32[]{:S(2)}) copy-start(s32[2048]{0:T(1024)} %param.7) | copy-start | bytes 24580
  12.8 14.9 %copy-start.5 = (s32[2048]{0:T(1024)S(1)}, s32[2048]{0:T(1024)}, u32[]{:S(2)}) copy-start(s32[2048]{0:T(1024)} %param.8) | copy-start | bytes 24580
  23.6 16.8 %all-to-all-start.1 = ((bf16[8,16,2048]{2,1,0:T(8,128)(2,1)}), bf16[8,16,2048]{2,1,0:T(8,128)(2,1)S(1)}, u32[]{:S(2)}, u32[]{:S(2)}) async-start(bf16[8,16,2048]{2,1,0:T(8,128)(2,1)} %crossed.1), calls=%async_computation.1 | async-start | bytes 1048576 | tf_op jit(solution)/shard_map/all_to_all | solution.py:161
  46.2 3.4 %copy-start = (bf16[2048,2048]{1,0:T(8,128)(2,1)S(1)}, bf16[2048,2048]{1,0:T(8,128)(2,1)}, u32[]{:S(2)}) copy-start(bf16[2048,2048]{1,0:T(8,128)(2,1)} %values_ref.1) | copy-start | bytes 25165828

commit v3 on v2

v3 whole, which is shorter than its diff:
```python
import functools

import jax
import jax.numpy as jnp
from jax import lax
from jax.experimental import pallas as pl
from jax.experimental.pallas import tpu as pltpu
from jax.sharding import PartitionSpec as P

LANES = 128
DEPTH = 512
MIB = 1024 * 1024
VMEM = pl.BlockSpec(memory_space=pltpu.VMEM)
ANY = pl.BlockSpec(memory_space=pl.ANY)


def group_size(orbits):
    return max(g for g in range(1, orbits + 1) if orbits % g == 0 and g * orbits <= DEPTH)


def params(mib):
    return pltpu.CompilerParams(vmem_limit_bytes=mib * MIB)


def cost(flops, bytes_accessed):
    return pl.CostEstimate(flops=flops, bytes_accessed=bytes_accessed, transcendentals=0)


SMALL = cost(1, 1)


def swap(x, axis, size, mask):
    return lax.ppermute(x, axis, [(i, i ^ mask) for i in range(size)])


def code_kernel(slabs, orbits, shift, first_ref, second_ref, coded_ref, first_here, second_here, sems):
    copies = [
        pltpu.make_async_copy(first_ref, first_here, sems.at[0]),
        pltpu.make_async_copy(second_ref, second_here, sems.at[1]),
    ]
    for copy in copies:
        copy.start()
    for copy in copies:
        copy.wait()
    base = lax.axis_index("cd") * orbits
    coded = ((first_here[...] - base) << shift) + second_here[...]
    for s in range(slabs):
        coded_ref[s] = coded


def pack_kernel(slabs, orbits, group, pairs, table_ref, packed_ref):
    for s in range(slabs):
        for g in range(table_ref.shape[0] // (group * pairs)):
            parts = [
                table_ref[(g * group + k) * pairs : (g * group + k + 1) * pairs, s * orbits : (s + 1) * orbits]
                for k in range(group)
            ]
            if group * orbits < DEPTH:
                parts.append(jnp.zeros((pairs, DEPTH - group * orbits), jnp.bfloat16))
            packed_ref[s, g * pairs : (g + 1) * pairs, :] = jnp.concatenate(parts, axis=1)


def lookup(table, pairs, keys, groups, totals):
    per_row = keys.shape[0]
    width = per_row * LANES
    key = jnp.concatenate([keys[j : j + 1] for j in range(per_row)], axis=1)
    chosen = jnp.concatenate([groups[j : j + 1] for j in range(per_row)], axis=1)
    hot = jnp.where(lax.broadcasted_iota(jnp.int32, (DEPTH, width), 0) == key, 1.0, 0.0).astype(jnp.bfloat16)
    sums = jnp.dot(table, hot, preferred_element_type=jnp.float32)
    chosen = jnp.broadcast_to(chosen, (8, width))
    totals = list(totals)
    for g in range(table.shape[0] // pairs):
        mine = chosen == g
        for t in range(pairs // 8):
            at = g * pairs + t * 8
            totals[t] = jnp.where(mine, sums[at : at + 8], totals[t])
    return totals


def crossed_blocks(group, pairs, shift, orbits, masks, packed_ref, coded_ref, crossed_ref):
    me = lax.axis_index("cd")
    base = me * orbits
    lines = coded_ref.shape[1]
    step = min(lines, 4)

    def block(out, mask):
        slab = me ^ mask
        coded = coded_ref[slab]
        first = coded >> shift
        second = (coded & ((1 << shift) - 1)) - base
        here = jnp.logical_and(second >= 0, second < orbits)
        second = jnp.where(here, second, 0)
        groups = lax.div(second, jnp.int32(group))
        keys = (second - groups * group) * orbits + first
        groups = jnp.where(here, groups, -1)
        for i in range(0, lines, step):
            zero = [jnp.zeros((8, step * LANES), jnp.float32)] * (pairs // 8)
            got = lookup(packed_ref[slab], pairs, keys[i : i + step], groups[i : i + step], zero)
            crossed_ref[out, :, i * LANES : (i + step) * LANES] = jnp.concatenate(got, axis=0).astype(jnp.bfloat16)

    for at in range(0, len(masks), 2):
        some = list(range(at, min(at + 2, len(masks))))
        needed = functools.reduce(jnp.logical_or, [(me ^ masks[out]) <= me for out in some])

        @pl.when(needed)
        def _(some=some):
            for out in some:
                block(out, masks[out])

        @pl.when(jnp.logical_not(needed))
        def _(some=some):
            for out in some:
                crossed_ref[out] = jnp.zeros(crossed_ref.shape[1:], jnp.bfloat16)


def direct_kernel(group, pairs, shift, orbits, slabs, low, high, packed_ref, coded_ref, *refs):
    old_ref, direct_ref = refs[0], refs[-1]
    me = lax.axis_index("cd")
    coded = coded_ref[0]
    first = coded >> shift
    second = coded & ((1 << shift) - 1)
    groups = lax.div(first, jnp.int32(group))
    owner = lax.div(second, jnp.int32(orbits))
    keys = (first - groups * group) * orbits + (second - owner * orbits)
    lines = coded.shape[0]
    step = min(lines, 4)
    direct_ref[...] = jnp.zeros(direct_ref.shape, jnp.bfloat16) if old_ref is None else old_ref[...]

    for ahead in range(low, high):

        @pl.when(me + ahead < slabs)
        def _(ahead=ahead):
            slab = me + ahead
            for i in range(0, lines, step):
                here = slice(i * LANES, (i + step) * LANES)
                old = direct_ref[:, here].astype(jnp.float32)
                got = [old[t * 8 : (t + 1) * 8] for t in range(pairs // 8)]
                chosen = jnp.where(owner[i : i + step] == slab, groups[i : i + step], -1)
                got = lookup(packed_ref[slab], pairs, keys[i : i + step], chosen, got)
                direct_ref[:, here] = jnp.concatenate(got, axis=0).astype(jnp.bfloat16)


def direct_first(*args):
    *head, direct_ref = args
    direct_kernel(*head, None, direct_ref)


def crossed_kernel(group, pairs, shift, orbits, masks, packed_ref, coded_ref, *refs):
    crossed_ref = refs[-1]
    crossed_blocks(group, pairs, shift, orbits, masks, packed_ref, coded_ref, crossed_ref)


def ladder_kernel(masks, parts, *refs):
    packed_refs, values_ref, out_ref = refs[:parts], refs[parts], refs[-1]
    width = out_ref.shape[2]
    me = lax.axis_index("cd")
    packed = jnp.concatenate([ref[...] for ref in packed_refs], axis=0)
    for out, mask in enumerate(masks):
        at = pl.ds(pl.multiple_of((me ^ mask) * width, width), width)
        out_ref[out] = lax.dot_general(
            values_ref[at, :],
            packed,
            (((1,), (1,)), ((), ())),
            preferred_element_type=jnp.float32,
        ).T.astype(out_ref.dtype)


def on_device(pair_values, amplitudes, cd_first, cd_second, live_cols):
    slabs = lax.axis_size("cd")
    blocks = lax.axis_size("ab")
    pair_block, orbits, orbitals = amplitudes.shape
    columns = cd_first.shape[0]
    rows = pair_values.shape[0]
    lines = columns // LANES
    pairs = -(-pair_block // 16) * 16
    group = group_size(orbits)
    shift = (orbitals - 1).bit_length()
    near = list(range(0, slabs, 2))
    far = list(range(1, slabs, 2))

    coded = pl.pallas_call(
        functools.partial(code_kernel, slabs, orbits, shift),
        out_shape=jax.ShapeDtypeStruct((slabs, lines, LANES), jnp.int32),
        in_specs=[ANY] * 2,
        out_specs=VMEM,
        scratch_shapes=[pltpu.VMEM((lines, LANES), jnp.int32)] * 2 + [pltpu.SemaphoreType.DMA((2,))],
        compiler_params=params(58),
        cost_estimate=cost(slabs * columns, slabs * columns * 4),
        name="code",
    )(cd_first.reshape(lines, LANES), cd_second.reshape(lines, LANES))
    own_coded = coded
    coded = lax.all_to_all(coded, "cd", split_axis=0, concat_axis=0, tiled=True)

    table = jnp.transpose(amplitudes, (1, 0, 2))
    if pairs != pair_block:
        table = jnp.pad(table, ((0, 0), (0, pairs - pair_block), (0, 0)))
    table = table.reshape(orbits * pairs, orbitals)
    packed_rows = orbits // group * pairs
    steps = 4 if orbits // group % 4 == 0 else 1
    table = pl.pallas_call(
        functools.partial(pack_kernel, slabs, orbits, group, pairs),
        out_shape=jax.ShapeDtypeStruct((slabs, packed_rows, DEPTH), jnp.bfloat16),
        grid=(steps,),
        in_specs=[pl.BlockSpec((orbits * pairs // steps, orbitals), lambda i: (i, 0))],
        out_specs=pl.BlockSpec((slabs, packed_rows // steps, DEPTH), lambda i: (0, i, 0)),
        compiler_params=params(16),
        cost_estimate=cost(0, 4 * orbits * pairs * orbitals),
        name="pack",
    )(table)

    lookup_flops = 2 * packed_rows * DEPTH * columns
    lookup_bytes = packed_rows * DEPTH * 2 + columns * pairs * 2

    def direct_for(low, high, *old):
        return pl.pallas_call(
            functools.partial(direct_kernel if old else direct_first, group, pairs, shift, orbits, slabs, low, high),
            out_shape=jax.ShapeDtypeStruct((pairs, columns), jnp.bfloat16),
            in_specs=[VMEM] * 2 + [VMEM, ANY][: len(old)],
            out_specs=VMEM,
            compiler_params=params(20),
            cost_estimate=cost((high - low) * lookup_flops, (high - low) * lookup_bytes),
            name="direct",
        )(table, own_coded, *old)

    direct = direct_for(0, slabs // 2)
    coded, direct = lax.optimization_barrier((coded, direct))

    def crossed_for(masks, name, *after):
        return pl.pallas_call(
            functools.partial(crossed_kernel, group, pairs, shift, orbits, masks),
            out_shape=jax.ShapeDtypeStruct((len(masks), pairs, columns), jnp.bfloat16),
            in_specs=[VMEM] * 2 + [ANY] * len(after),
            out_specs=VMEM,
            compiler_params=params(20),
            cost_estimate=cost(len(masks) * lookup_flops, len(masks) * lookup_bytes),
            name=name,
        )(table, coded, *after)

    arrived, last = [], ()
    for at in reversed(range(0, len(far), 2)):
        last = (crossed_for(far[at : at + 2], "crossed_far", *last),)
        arrived.insert(0, swap(last[0], "cd", slabs, 1))
    crossed = crossed_for(near, "crossed_near", *last)
    direct = direct_for(slabs // 2, slabs, direct, crossed)
    merged = [crossed[k] + arrived[k // 2][k % 2] for k in range(len(near))]
    got = [swap(merged[k], "cd", slabs, near[k]) for k in reversed(range(1, len(near)))]
    crossed = merged[0].astype(jnp.float32)
    for block in got:
        crossed = crossed + block.astype(jnp.float32)

    slots = jnp.arange(columns, dtype=jnp.int32)
    live = (slots < live_cols[0]).astype(jnp.float32)
    half = jnp.where(cd_first == cd_second, jnp.float32(0.5), jnp.float32(1.0))
    packed = ((direct.astype(jnp.float32) + crossed) * (half * live)[None, :]).astype(jnp.bfloat16)

    gathered = [lax.all_gather(packed[:pair_block], "ab", axis=0, tiled=True)]
    all_pairs = blocks * pair_block

    width = rows // slabs

    def ladder_for(masks, dtype, name, *after):
        return pl.pallas_call(
            functools.partial(ladder_kernel, masks, len(gathered)),
            out_shape=jax.ShapeDtypeStruct((len(masks), all_pairs, width), dtype),
            in_specs=[VMEM] * (len(gathered) + 1) + [ANY] * len(after),
            out_specs=VMEM,
            compiler_params=params(16),
            cost_estimate=SMALL,
            name=name,
        )(*gathered, pair_values, *after)

    got, last = [], ()
    for mask in reversed(near[1:]):
        last = (ladder_for([mask, mask + 1], jnp.bfloat16, "ladder", *last),)
        got.append(swap(last[0], "cd", slabs, mask))
    total = ladder_for([0, 1], jnp.float32, "ladder_own", *last)
    for part in got:
        total = total + part.astype(jnp.float32)
    total = total[0] + swap(total[1].astype(jnp.bfloat16), "cd", slabs, 1).astype(jnp.float32)
    return total.astype(jnp.bfloat16)


def solution(mesh):
    placed = (P("ab", "cd"), P("ab", "cd", None), P("cd"), P("cd"), P("cd"))
    return jax.shard_map(
        on_device, mesh=mesh, in_specs=placed, out_specs=P(None, ("ab", "cd")), check_vma=False
    )
```

time: 66 us -> 57.3 us (0.87)
  blocking collectives: 18.7 us -> 5.79 us
  starting transfers between devices: 10.7 us -> 22 us
  local copies, waits for them, and re-layouts: 6.59 us -> 1.84 us
  Pallas kernels: 17.9 us -> 15.2 us
    ppermute x0 -> x9, starting transfers between devices: none -> 14.6 us  [swap(): return lax.ppermute(x, axis, [(i, i ^ mask) for i in range(size)])]
    all_to_all x1 -> x0, blocking collectives: 12.9 us -> none  [on_device(): lax.all_to_all(partial_sums, 'cd', split_axis=0, concat_axis=0, tiled=True)]
    ppermute x0 -> x9, waiting for transfers between devices: none -> 10.5 us  [swap(): return lax.ppermute(x, axis, [(i, i ^ mask) for i in range(size)])]
    all_to_all x1 -> x0, waiting for transfers between devices: 6.8 us -> none  [on_device(): lax.all_to_all(crossed, 'cd', split_axis=0, concat_axis=0, tiled=True)]
    unnamed x12, local copies, waits for them, and re-layouts: 6.59 us -> 1.83 us
    all_to_all x1 -> x0, starting transfers between devices: 3.49 us -> none  [on_device(): lax.all_to_all(crossed, 'cd', split_axis=0, concat_axis=0, tiled=True)]
    pallas_call x3 -> x9, Pallas kernels: 15.5 us -> 12.1 us  [the longest x2 7.3 us: direct_for(): pl.pallas_call(functools.partial(direct_kernel if old else direct_first,...]
    all_to_all x1, waiting for transfers between devices: 3.34 us -> 0.01 us  [on_device(): coded = lax.all_to_all(coded, 'cd', split_axis=0, concat_axis=0, tiled=True)]
  transfers between devices with their start and end apart: 2 -> 10, of which waited for: 2 -> 6; matrix products, arithmetic and copies ran while one was open for 0% -> 0% of each run, Pallas kernels for 11% -> 20%
where the time goes in v3:
time: 57.3 us; the launch traced here: 56.9 us
  starting transfers between devices  22 us (38%)
  Pallas kernels  15.2 us (27%)
  waiting for transfers between devices  10.5 us (18%)
  blocking collectives  5.79 us (10%)
  local copies, waits for them, and re-layouts  1.84 us (3%)
  between operations  0.84 us (1%)
  other arithmetic  0.74 us (1%)
    ppermute x9, starting transfers between devices, swap(): return lax.ppermute(x, axis, [(i, i ^ mask) for i in range(size)])  14.6 us
    ppermute x9, waiting for transfers between devices, swap(): return lax.ppermute(x, axis, [(i, i ^ mask) for i in range(size)])  10.5 us
    all_to_all x1, starting transfers between devices, on_device(): coded = lax.all_to_all(coded, 'cd', split_axis=0, concat_axis=0, tiled=True)  7.4 us
    pallas_call x2, Pallas kernels, direct_for(): pl.pallas_call(functools.partial(direct_kernel if old else direct_first,...  7.3 us
    all_gather x1, blocking collectives, on_device(): gathered = [lax.all_gather(packed[:pair_block], 'ab', axis=0, tiled=True)]  5.79 us
    pallas_call x4, Pallas kernels, ladder_for(): pl.pallas_call(functools.partial(ladder_kernel, masks, len(gathered)), ou...  2.97 us
    unnamed x12, local copies, waits for them, and re-layouts  1.83 us
    pallas_call x3, Pallas kernels, crossed_for(): pl.pallas_call(functools.partial(crossed_kernel, group, pairs, shift, orb...  1.8 us
  transfers between devices with their start and end apart: 10, of which 6 were waited for; matrix products, arithmetic and copies ran while one was open for 0% of the time, Pallas kernels for 20%

profile of v3, /device:TPU:0, one launch (start us, length us, event | category | flops | bytes accessed | tf_op | source)
XLA Modules:
  0.0 56.9 jit_solution(9695694259655295026)
XLA Ops:
  0.0 1.4 %code.1.args_1_.coded_ref = s32[8,16,128]{2,1,0:T(8,128)} custom-call(s32[16,128]{1,0:T(8,128)} %bitcast.29, s32[16,128]{1,0:T(8,128)} %bitcast.30), custom_call_target="tpu_custom_call" | custom-call | flops 16384 | bytes 65536 | tf_op jit(solution)/shard_map/code/pallas_call | solution.py:181
  1.4 0.0 copy-start.1
  1.4 7.4 %all-to-all-start = ((s32[8,16,128]{2,1,0:T(8,128)}), s32[8,16,128]{2,1,0:T(8,128)S(1)}, u32[]{:S(2)}, u32[]{:S(2)}) async-start(s32[8,16,128]{2,1,0:T(8,128)} %code.1.args_1_.coded_ref), calls=%async_computation | async-start | bytes 131072 | tf_op jit(solution)/shard_map/all_to_all | solution.py:192
  8.8 0.0 copy-start
  8.8 1.8 %copy-done = bf16[16,100,800]{2,0,1:T(8,128)(2,1)S(1)} copy-done((bf16[16,100,800]{2,0,1:T(8,128)(2,1)S(1)}, bf16[16,100,800]{2,0,1:T(8,128)(2,1)}, u32[]{:S(2)}) %copy-start) | copy-done | bytes 2560024
  10.6 1.7 %pack.1.args_0_.packed_ref = bf16[8,320,512]{2,1,0:T(8,128)(2,1)S(1)} custom-call(bf16[1600,800]{1,0:T(8,128)(2,1)S(1)} %bitcast.28), custom_call_target="tpu_custom_call" | custom-call | bytes 5120000 | tf_op jit(solution)/shard_map/pack/pallas_call | solution.py:200
  12.3 0.0 copy-done.1
  12.3 0.0 copy-start.2
  12.3 0.0 copy-start.3
  12.4 3.5 %direct.2.refs_0_ = bf16[16,2048]{1,0:T(8,128)(2,1)S(1)} custom-call(bf16[8,320,512]{2,1,0:T(8,128)(2,1)S(1)} %pack.1.args_0_.packed_ref, s32[8,16,128]{2,1,0:T(8,128)S(1)} %copy-done.1), custom_call_target="tpu_custom_call" | custom-call | flops 2684354560 | bytes 1572864 | tf_op jit(solution)/shard_map/direct/pallas_call | solution.py:215
  16.5 0.0 copy-done.2
  16.5 0.0 copy-done.3
  16.5 0.0 all-to-all-done.coded_ref
  16.6 3.8 %collective-permute-start.1 = (bf16[2,16,2048]{2,1,0:T(8,128)(2,1)S(1)}, bf16[2,16,2048]{2,1,0:T(8,128)(2,1)S(1)}, u32[]{:S(2)}, u32[]{:S(2)}) collective-permute-start(bf16[2,16,2048]{2,1,0:T(8,128)(2,1)S(1)} %crossed_far.2.refs_0_), channel_id=1, source_target_pairs={{0,1},{1,0},{2,3},{3,2},{4,5},{5,4},{6,7},{7,6},{8,9},{9,8},{10,11... | collective-permute-start | bytes 393224 | tf_op jit(solution)/shard_map/ppermute | solution.py:33
  20.4 0.1 collective-permute-start
  20.5 0.0 slice-start
  20.5 1.8 %crossed_near.1.refs_1_ = bf16[4,16,2048]{2,1,0:T(8,128)(2,1)S(1)} custom-call(bf16[8,320,512]{2,1,0:T(8,128)(2,1)S(1)} %pack.1.args_0_.packed_ref, s32[8,16,128]{2,1,0:T(8,128)S(1)} %all-to-all-done.coded_ref, bf16[2,16,2048]{2,1,0:T(8,128)(2,1)S(1)} %crossed_far.3.refs_0_), custom_call_target="tpu_custom_call" | custom-call | flops 2684354560 | bytes 1572864 | tf_op jit(solution)/shard_map/crossed_near/pallas_call | solution.py:229
  22.3 3.9 %collective-permute-done = bf16[2,16,2048]{2,1,0:T(8,128)(2,1)S(1)} collective-permute-done((bf16[2,16,2048]{2,1,0:T(8,128)(2,1)S(1)}, bf16[2,16,2048]{2,1,0:T(8,128)(2,1)S(1)}, u32[]{:S(2)}, u32[]{:S(2)}) %collective-permute-start) | collective-permute-done | bytes 131104 | tf_op jit(solution)/shard_map/ppermute | solution.py:33
  26.2 0.0 collective-permute-done.1
  26.2 3.6 %collective-permute-start.2 = (bf16[16,2048]{1,0:T(8,128)(2,1)S(1)}, bf16[16,2048]{1,0:T(8,128)(2,1)S(1)}, u32[]{:S(2)}, u32[]{:S(2)}) collective-permute-start(bf16[16,2048]{1,0:T(8,128)(2,1)S(1)} %get-tuple-element.9), channel_id=1, source_target_pairs={{0,6},{1,7},{2,4},{3,5},{4,2},{5,3},{6,0},{7,1},{8,14},{9,15},{10,... | collective-permute-start | bytes 196616 | tf_op jit(solution)/shard_map/ppermute | solution.py:33
  29.9 0.0 collective-permute-start.3
  29.9 0.0 slice-start.1
  29.9 0.8 %collective-permute-start.4 = (bf16[16,2048]{1,0:T(8,128)(2,1)S(1)}, bf16[16,2048]{1,0:T(8,128)(2,1)S(1)}, u32[]{:S(2)}, u32[]{:S(2)}) collective-permute-start(bf16[16,2048]{1,0:T(8,128)(2,1)S(1)} %get-tuple-element.11), channel_id=1, source_target_pairs={{0,2},{1,3},{2,0},{3,1},{4,6},{5,7},{6,4},{7,5},{8,10},{9,11},{10,... | collective-permute-start | bytes 196616 | tf_op jit(solution)/shard_map/ppermute | solution.py:33
  30.7 3.8 %direct.3 = bf16[16,2048]{1,0:T(8,128)(2,1)S(1)} custom-call(bf16[8,320,512]{2,1,0:T(8,128)(2,1)S(1)} %pack.1.args_0_.packed_ref, s32[8,16,128]{2,1,0:T(8,128)S(1)} %copy-done.1, bf16[16,2048]{1,0:T(8,128)(2,1)S(1)} %direct.2.refs_0_, bf16[4,16,2048]{2,1,0:T(8,128)(2,1)S(1)} %crossed_near.1.refs_1_), custom_call_target="tpu_custom_call" | custom-call | flops 2684354560 | bytes 1572864 | tf_op jit(solution)/shard_map/direct/pallas_call | solution.py:215
  34.5 0.0 collective-permute-done.2
  34.5 0.9 %collective-permute-done.3 = bf16[16,2048]{1,0:T(8,128)(2,1)S(1)} collective-permute-done((bf16[16,2048]{1,0:T(8,128)(2,1)S(1)}, bf16[16,2048]{1,0:T(8,128)(2,1)S(1)}, u32[]{:S(2)}, u32[]{:S(2)}) %collective-permute-start.3) | collective-permute-done | bytes 65568 | tf_op jit(solution)/shard_map/ppermute | solution.py:33
  35.4 0.0 collective-permute-done.4
  35.4 0.1 fusion.4
  35.5 5.8 %all_gather.3.refs_0_ = bf16[64,2048]{1,0:T(8,128)(2,1)S(1)} all-gather(bf16[16,2048]{1,0:T(8,128)(2,1)S(1)} %fusion.4), channel_id=1, replica_groups=mesh['ab'=4,'cd'=8] {'ab'}, dimensions={0}, use_global_device_ids=true | all-gather | bytes 327680 | tf_op jit(solution)/shard_map/all_gather | solution.py:256
  41.2 0.0 slice-done
  41.3 0.0 slice-done.1
  41.3 0.7 %ladder.3.refs_2_ = bf16[2,64,256]{2,1,0:T(8,128)(2,1)S(1)} custom-call(bf16[64,2048]{1,0:T(8,128)(2,1)S(1)} %all_gather.3.refs_0_, bf16[2048,2048]{1,0:T(8,128)(2,1)S(1)} %bitcast.27), custom_call_target="tpu_custom_call" | custom-call | flops 1 | bytes 1 | tf_op jit(solution)/shard_map/ladder/pallas_call | solution.py:262
  42.0 0.7 %ladder.4.refs_2_ = bf16[2,64,256]{2,1,0:T(8,128)(2,1)S(1)} custom-call(bf16[64,2048]{1,0:T(8,128)(2,1)S(1)} %all_gather.3.refs_0_, bf16[2048,2048]{1,0:T(8,128)(2,1)S(1)} %bitcast.27, bf16[2,64,256]{2,1,0:T(8,128)(2,1)S(1)} %ladder.3.refs_2_), custom_call_target="tpu_custom_call" | custom-call | flops 1 | bytes 1 | tf_op jit(solution)/shard_map/ladder/pallas_call | solution.py:262
  42.8 0.7 %ladder.5.refs_2_ = bf16[2,64,256]{2,1,0:T(8,128)(2,1)S(1)} custom-call(bf16[64,2048]{1,0:T(8,128)(2,1)S(1)} %all_gather.3.refs_0_, bf16[2048,2048]{1,0:T(8,128)(2,1)S(1)} %bitcast.27, bf16[2,64,256]{2,1,0:T(8,128)(2,1)S(1)} %ladder.4.refs_2_), custom_call_target="tpu_custom_call" | custom-call | flops 1 | bytes 1 | tf_op jit(solution)/shard_map/ladder/pallas_call | solution.py:262
  43.5 0.2 collective-permute-start.7
  43.7 2.4 %collective-permute-start.6 = (bf16[2,64,256]{2,1,0:T(8,128)(2,1)S(1)}, bf16[2,64,256]{2,1,0:T(8,128)(2,1)S(1)}, u32[]{:S(2)}, u32[]{:S(2)}) collective-permute-start(bf16[2,64,256]{2,1,0:T(8,128)(2,1)S(1)} %ladder.4.refs_2_), channel_id=1, source_target_pairs={{0,4},{1,5},{2,6},{3,7},{4,0},{5,1},{6,2},{7,3},{8,12},{9,13},{10,... | collective-permute-start | bytes 196616 | tf_op jit(solution)/shard_map/ppermute | solution.py:33
  46.1 1.8 %collective-permute-start.5 = (bf16[2,64,256]{2,1,0:T(8,128)(2,1)S(1)}, bf16[2,64,256]{2,1,0:T(8,128)(2,1)S(1)}, u32[]{:S(2)}, u32[]{:S(2)}) collective-permute-start(bf16[2,64,256]{2,1,0:T(8,128)(2,1)S(1)} %ladder.3.refs_2_), channel_id=1, source_target_pairs={{0,6},{1,7},{2,4},{3,5},{4,2},{5,3},{6,0},{7,1},{8,14},{9,15},{10,... | collective-permute-start | bytes 196616 | tf_op jit(solution)/shard_map/ppermute | solution.py:33
  47.9 0.8 %ladder_own.1 = f32[2,64,256]{2,1,0:T(8,128)S(1)} custom-call(bf16[64,2048]{1,0:T(8,128)(2,1)S(1)} %all_gather.3.refs_0_, bf16[2048,2048]{1,0:T(8,128)(2,1)S(1)} %bitcast.27, bf16[2,64,256]{2,1,0:T(8,128)(2,1)S(1)} %ladder.5.refs_2_), custom_call_target="tpu_custom_call" | custom-call | flops 1 | bytes 1 | tf_op jit(solution)/shard_map/ladder_own/pallas_call | solution.py:262
  48.7 0.5 collective-permute-done.7
  49.2 0.3 collective-permute-done.6
  49.5 2.8 %collective-permute-done.5 = bf16[2,64,256]{2,1,0:T(8,128)(2,1)S(1)} collective-permute-done((bf16[2,64,256]{2,1,0:T(8,128)(2,1)S(1)}, bf16[2,64,256]{2,1,0:T(8,128)(2,1)S(1)}, u32[]{:S(2)}, u32[]{:S(2)}) %collective-permute-start.5) | collective-permute-done | bytes 65568 | tf_op jit(solution)/shard_map/ppermute | solution.py:33
  52.3 1.8 %collective-permute-start.8 = (bf16[64,256]{1,0:T(8,128)(2,1)S(1)}, bf16[64,256]{1,0:T(8,128)(2,1)S(1)}, u32[]{:S(2)}, u32[]{:S(2)}) collective-permute-start(bf16[64,256]{1,0:T(8,128)(2,1)S(1)} %fusion.11), channel_id=1, source_target_pairs={{0,1},{1,0},{2,3},{3,2},{4,5},{5,4},{6,7},{7,6},{8,9},{9,8},{10,11... | collective-permute-start | bytes 98312 | tf_op jit(solution)/shard_map/ppermute | solution.py:33
  54.1 2.2 %collective-permute-done.8 = bf16[64,256]{1,0:T(8,128)(2,1)S(1)} collective-permute-done((bf16[64,256]{1,0:T(8,128)(2,1)S(1)}, bf16[64,256]{1,0:T(8,128)(2,1)S(1)}, u32[]{:S(2)}, u32[]{:S(2)}) %collective-permute-start.8) | collective-permute-done | bytes 32800 | tf_op jit(solution)/shard_map/ppermute | solution.py:33
  56.3 0.6 %fusion.6 = bf16[64,256]{1,0:T(8,128)(2,1)} fusion(f32[2,64,256]{2,1,0:T(8,128)S(1)} %convert_add_fusion.1, bf16[64,256]{1,0:T(8,128)(2,1)S(1)} %collective-permute-done.8), kind=kLoop, calls=%fused_computation.10 | loop fusion | flops 49152 | bytes 131072 | tf_op jit(solution)/shard_map/convert_element_type | solution.py:280
  (7 shorter events, 0.1 us)
Async XLA Ops:
  1.4 10.9 %copy-start.1 = (s32[8,16,128]{2,1,0:T(8,128)S(1)}, s32[8,16,128]{2,1,0:T(8,128)}, u32[]{:S(2)}) copy-start(s32[8,16,128]{2,1,0:T(8,128)} %code.1.args_1_.coded_ref) | copy-start | bytes 196612
  1.4 15.2 %all-to-all-start = ((s32[8,16,128]{2,1,0:T(8,128)}), s32[8,16,128]{2,1,0:T(8,128)S(1)}, u32[]{:S(2)}, u32[]{:S(2)}) async-start(s32[8,16,128]{2,1,0:T(8,128)} %code.1.args_1_.coded_ref), calls=%async_computation | async-start | bytes 131072 | tf_op jit(solution)/shard_map/all_to_all | solution.py:192
  8.8 1.8 %copy-start = (bf16[16,100,800]{2,0,1:T(8,128)(2,1)S(1)}, bf16[16,100,800]{2,0,1:T(8,128)(2,1)}, u32[]{:S(2)}) copy-start(bf16[16,100,800]{2,0,1:T(8,128)(2,1)} %param.6) | copy-start | bytes 7680004
  12.3 4.2 %copy-start.2 = (s32[2048]{0:T(1024)S(1)}, s32[2048]{0:T(1024)}, u32[]{:S(2)}) copy-start(s32[2048]{0:T(1024)} %param.7) | copy-start | bytes 24580
  12.3 4.2 %copy-start.3 = (s32[2048]{0:T(1024)S(1)}, s32[2048]{0:T(1024)}, u32[]{:S(2)}) copy-start(s32[2048]{0:T(1024)} %param.8) | copy-start | bytes 24580
  16.6 9.6 %collective-permute-start.1 = (bf16[2,16,2048]{2,1,0:T(8,128)(2,1)S(1)}, bf16[2,16,2048]{2,1,0:T(8,128)(2,1)S(1)}, u32[]{:S(2)}, u32[]{:S(2)}) collective-permute-start(bf16[2,16,2048]{2,1,0:T(8,128)(2,1)S(1)} %crossed_far.2.refs_0_), channel_id=1, source_target_pairs={{0,1},{1,0},{2,3},{3,2},{4,5},{5,4},{6,7},{7,6},{8,9},{9,8},{10,11... | collective-permute-start | bytes 393224 | tf_op jit(solution)/shard_map/ppermute | solution.py:33
  20.4 5.8 %collective-permute-start = (bf16[2,16,2048]{2,1,0:T(8,128)(2,1)S(1)}, bf16[2,16,2048]{2,1,0:T(8,128)(2,1)S(1)}, u32[]{:S(2)}, u32[]{:S(2)}) collective-permute-start(bf16[2,16,2048]{2,1,0:T(8,128)(2,1)S(1)} %crossed_far.3.refs_0_), channel_id=1, source_target_pairs={{0,1},{1,0},{2,3},{3,2},{4,5},{5,4},{6,7},{7,6},{8,9},{9,8},{10,11... | collective-permute-start | bytes 393224 | tf_op jit(solution)/shard_map/ppermute | solution.py:33
  20.5 20.7 %slice-start = ((s8[8388608]{0:T(1024)(128)(4,1)}), s8[4194304]{0:T(1024)(128)(4,1)S(1)}, s32[]{:S(2)}) async-start(s8[8388608]{0:T(1024)(128)(4,1)} %bitcast.26), calls=%async_computation.1 | async-start | bytes 8388608
  26.2 8.3 %collective-permute-start.2 = (bf16[16,2048]{1,0:T(8,128)(2,1)S(1)}, bf16[16,2048]{1,0:T(8,128)(2,1)S(1)}, u32[]{:S(2)}, u32[]{:S(2)}) collective-permute-start(bf16[16,2048]{1,0:T(8,128)(2,1)S(1)} %get-tuple-element.9), channel_id=1, source_target_pairs={{0,6},{1,7},{2,4},{3,5},{4,2},{5,3},{6,0},{7,1},{8,14},{9,15},{10,... | collective-permute-start | bytes 196616 | tf_op jit(solution)/shard_map/ppermute | solution.py:33
  29.9 5.5 %collective-permute-start.3 = (bf16[16,2048]{1,0:T(8,128)(2,1)S(1)}, bf16[16,2048]{1,0:T(8,128)(2,1)S(1)}, u32[]{:S(2)}, u32[]{:S(2)}) collective-permute-start(bf16[16,2048]{1,0:T(8,128)(2,1)S(1)} %get-tuple-element.10), channel_id=1, source_target_pairs={{0,4},{1,5},{2,6},{3,7},{4,0},{5,1},{6,2},{7,3},{8,12},{9,13},{10,... | collective-permute-start | bytes 196616 | tf_op jit(solution)/shard_map/ppermute | solution.py:33
  29.9 11.4 %slice-start.1 = ((s8[8388608]{0:T(1024)(128)(4,1)}), s8[4194304]{0:T(1024)(128)(4,1)S(1)}, s32[]{:S(2)}) async-start(s8[8388608]{0:T(1024)(128)(4,1)} %bitcast.26), calls=%async_computation.2 | async-start | bytes 8388608
  29.9 5.5 %collective-permute-start.4 = (bf16[16,2048]{1,0:T(8,128)(2,1)S(1)}, bf16[16,2048]{1,0:T(8,128)(2,1)S(1)}, u32[]{:S(2)}, u32[]{:S(2)}) collective-permute-start(bf16[16,2048]{1,0:T(8,128)(2,1)S(1)} %get-tuple-element.11), channel_id=1, source_target_pairs={{0,2},{1,3},{2,0},{3,1},{4,6},{5,7},{6,4},{7,5},{8,10},{9,11},{10,... | collective-permute-start | bytes 196616 | tf_op jit(solution)/shard_map/ppermute | solution.py:33
  43.5 5.7 %collective-permute-start.7 = (bf16[2,64,256]{2,1,0:T(8,128)(2,1)S(1)}, bf16[2,64,256]{2,1,0:T(8,128)(2,1)S(1)}, u32[]{:S(2)}, u32[]{:S(2)}) collective-permute-start(bf16[2,64,256]{2,1,0:T(8,128)(2,1)S(1)} %ladder.5.refs_2_), channel_id=1, source_target_pairs={{0,2},{1,3},{2,0},{3,1},{4,6},{5,7},{6,4},{7,5},{8,10},{9,11},{10,... | collective-permute-start | bytes 196616 | tf_op jit(solution)/shard_map/ppermute | solution.py:33
  43.7 5.8 %collective-permute-start.6 = (bf16[2,64,256]{2,1,0:T(8,128)(2,1)S(1)}, bf16[2,64,256]{2,1,0:T(8,128)(2,1)S(1)}, u32[]{:S(2)}, u32[]{:S(2)}) collective-permute-start(bf16[2,64,256]{2,1,0:T(8,128)(2,1)S(1)} %ladder.4.refs_2_), channel_id=1, source_target_pairs={{0,4},{1,5},{2,6},{3,7},{4,0},{5,1},{6,2},{7,3},{8,12},{9,13},{10,... | collective-permute-start | bytes 196616 | tf_op jit(solution)/shard_map/ppermute | solution.py:33
  46.1 6.1 %collective-permute-start.5 = (bf16[2,64,256]{2,1,0:T(8,128)(2,1)S(1)}, bf16[2,64,256]{2,1,0:T(8,128)(2,1)S(1)}, u32[]{:S(2)}, u32[]{:S(2)}) collective-permute-start(bf16[2,64,256]{2,1,0:T(8,128)(2,1)S(1)} %ladder.3.refs_2_), channel_id=1, source_target_pairs={{0,6},{1,7},{2,4},{3,5},{4,2},{5,3},{6,0},{7,1},{8,14},{9,15},{10,... | collective-permute-start | bytes 196616 | tf_op jit(solution)/shard_map/ppermute | solution.py:33
  52.3 4.0 %collective-permute-start.8 = (bf16[64,256]{1,0:T(8,128)(2,1)S(1)}, bf16[64,256]{1,0:T(8,128)(2,1)S(1)}, u32[]{:S(2)}, u32[]{:S(2)}) collective-permute-start(bf16[64,256]{1,0:T(8,128)(2,1)S(1)} %fusion.11), channel_id=1, source_target_pairs={{0,1},{1,0},{2,3},{3,2},{4,5},{5,4},{6,7},{7,6},{8,9},{9,8},{10,11... | collective-permute-start | bytes 98312 | tf_op jit(solution)/shard_map/ppermute | solution.py:33

commit v4 on v3

--- a/solution.py
+++ b/solution.py
@@ -26,17 +26,22 @@
     return pl.CostEstimate(flops=flops, bytes_accessed=bytes_accessed, transcendentals=0)
 
 
-SMALL = cost(1, 1)
+def spent(microseconds):
+    return cost(int(microseconds * 1.1e9), 1)
+
+
+SMALL = spent(0.01)
 
 
 def swap(x, axis, size, mask):
     return lax.ppermute(x, axis, [(i, i ^ mask) for i in range(size)])
 
 
-def code_kernel(slabs, orbits, shift, first_ref, second_ref, coded_ref, first_here, second_here, sems):
+def code_kernel(slabs, orbits, shift, first_ref, second_ref, live_ref, coded_ref, first_here, second_here, live_here, sems):
     copies = [
         pltpu.make_async_copy(first_ref, first_here, sems.at[0]),
         pltpu.make_async_copy(second_ref, second_here, sems.at[1]),
+        pltpu.make_async_copy(live_ref, live_here, sems.at[2]),
     ]
     for copy in copies:
         copy.start()
@@ -44,6 +49,9 @@
         copy.wait()
     base = lax.axis_index("cd") * orbits
     coded = ((first_here[...] - base) << shift) + second_here[...]
+    shape = coded.shape
+    slots = lax.broadcasted_iota(jnp.int32, shape, 0) * shape[1] + lax.broadcasted_iota(jnp.int32, shape, 1)
+    coded = jnp.where(slots < live_here[0], coded, -1)
     for s in range(slabs):
         coded_ref[s] = coded
 
@@ -88,7 +96,7 @@
         coded = coded_ref[slab]
         first = coded >> shift
         second = (coded & ((1 << shift) - 1)) - base
-        here = jnp.logical_and(second >= 0, second < orbits)
+        here = jnp.logical_and(coded >= 0, jnp.logical_and(second >= 0, second < orbits))
         second = jnp.where(here, second, 0)
         groups = lax.div(second, jnp.int32(group))
         keys = (second - groups * group) * orbits + first
@@ -119,9 +127,9 @@
     coded = coded_ref[0]
     first = coded >> shift
     second = coded & ((1 << shift) - 1)
-    groups = lax.div(first, jnp.int32(group))
+    groups = jnp.where(coded >= 0, lax.div(first, jnp.int32(group)), -1)
     owner = lax.div(second, jnp.int32(orbits))
-    keys = (first - groups * group) * orbits + (second - owner * orbits)
+    keys = lax.rem(first, jnp.int32(group)) * orbits + (second - owner * orbits)
     lines = coded.shape[0]
     step = min(lines, 4)
     direct_ref[...] = jnp.zeros(direct_ref.shape, jnp.bfloat16) if old_ref is None else old_ref[...]
@@ -165,6 +173,27 @@
         ).T.astype(out_ref.dtype)
 
 
+def add_kernel(*refs):
+    total = refs[0][...]
+    for ref in refs[1:-1]:
+        total = total + ref[...].astype(jnp.float32)
+    refs[-1][...] = total
+
+
+def add_up(total, parts):
+    for part in parts[:-1]:
+        total = pl.pallas_call(
+            add_kernel,
+            out_shape=jax.ShapeDtypeStruct(total.shape, total.dtype),
+            in_specs=[VMEM] * 2,
+            out_specs=VMEM,
+            compiler_params=params(8),
+            cost_estimate=spent(0.5),
+            name="add",
+        )(total, part)
+    return total + parts[-1].astype(jnp.float32)
+
+
 def on_device(pair_values, amplitudes, cd_first, cd_second, live_cols):
     slabs = lax.axis_size("cd")
     blocks = lax.axis_size("ab")
@@ -181,13 +210,14 @@
     coded = pl.pallas_call(
         functools.partial(code_kernel, slabs, orbits, shift),
         out_shape=jax.ShapeDtypeStruct((slabs, lines, LANES), jnp.int32),
-        in_specs=[ANY] * 2,
+        in_specs=[ANY] * 3,
         out_specs=VMEM,
-        scratch_shapes=[pltpu.VMEM((lines, LANES), jnp.int32)] * 2 + [pltpu.SemaphoreType.DMA((2,))],
+        scratch_shapes=[pltpu.VMEM((lines, LANES), jnp.int32)] * 2
+        + [pltpu.SMEM((1,), jnp.int32), pltpu.SemaphoreType.DMA((3,))],
         compiler_params=params(58),
-        cost_estimate=cost(slabs * columns, slabs * columns * 4),
+        cost_estimate=spent(20),
         name="code",
-    )(cd_first.reshape(lines, LANES), cd_second.reshape(lines, LANES))
+    )(cd_first.reshape(lines, LANES), cd_second.reshape(lines, LANES), live_cols)
     own_coded = coded
     coded = lax.all_to_all(coded, "cd", split_axis=0, concat_axis=0, tiled=True)
 
@@ -218,11 +248,12 @@
             in_specs=[VMEM] * 2 + [VMEM, ANY][: len(old)],
             out_specs=VMEM,
             compiler_params=params(20),
-            cost_estimate=cost((high - low) * lookup_flops, (high - low) * lookup_bytes),
+            cost_estimate=SMALL if old else cost((high - low) * lookup_flops, 1),
             name="direct",
         )(table, own_coded, *old)
 
-    direct = direct_for(0, slabs // 2)
+    cuts = sorted({0, min(2, slabs), min(4, slabs), slabs})
+    direct = direct_for(cuts[0], cuts[1])
     coded, direct = lax.optimization_barrier((coded, direct))
 
     def crossed_for(masks, name, *after):
@@ -232,26 +263,27 @@
             in_specs=[VMEM] * 2 + [ANY] * len(after),
             out_specs=VMEM,
             compiler_params=params(20),
-            cost_estimate=cost(len(masks) * lookup_flops, len(masks) * lookup_bytes),
+            cost_estimate=SMALL,
             name=name,
         )(table, coded, *after)
 
+    pairs_of = [near[at : at + 2] for at in reversed(range(0, slabs // 2, 2))]
     arrived, last = [], ()
-    for at in reversed(range(0, len(far), 2)):
-        last = (crossed_for(far[at : at + 2], "crossed_far", *last),)
-        arrived.insert(0, swap(last[0], "cd", slabs, 1))
-    crossed = crossed_for(near, "crossed_near", *last)
-    direct = direct_for(slabs // 2, slabs, direct, crossed)
-    merged = [crossed[k] + arrived[k // 2][k % 2] for k in range(len(near))]
-    got = [swap(merged[k], "cd", slabs, near[k]) for k in reversed(range(1, len(near)))]
-    crossed = merged[0].astype(jnp.float32)
-    for block in got:
-        crossed = crossed + block.astype(jnp.float32)
-
-    slots = jnp.arange(columns, dtype=jnp.int32)
-    live = (slots < live_cols[0]).astype(jnp.float32)
+    for masks in pairs_of:
+        last = (crossed_for([mask + 1 for mask in masks], "crossed_far", *last),)
+        arrived.append(swap(last[0], "cd", slabs, 1))
+    got = []
+    for masks, block in zip(pairs_of, arrived):
+        merged = crossed_for(masks, "crossed_near", *last) + block
+        last = (merged,)
+        for k in reversed(range(len(masks))):
+            if masks[k]:
+                got.append(swap(merged[k], "cd", slabs, masks[k]))
+    for low, high in zip(cuts[1:], cuts[2:]):
+        direct = direct_for(low, high, direct, *last)
+    crossed = add_up(merged[0].astype(jnp.float32), got)
     half = jnp.where(cd_first == cd_second, jnp.float32(0.5), jnp.float32(1.0))
-    packed = ((direct.astype(jnp.float32) + crossed) * (half * live)[None, :]).astype(jnp.bfloat16)
+    packed = ((direct.astype(jnp.float32) + crossed) * half[None, :]).astype(jnp.bfloat16)
 
     gathered = [lax.all_gather(packed[:pair_block], "ab", axis=0, tiled=True)]
     all_pairs = blocks * pair_block
@@ -274,8 +306,7 @@
         last = (ladder_for([mask, mask + 1], jnp.bfloat16, "ladder", *last),)
         got.append(swap(last[0], "cd", slabs, mask))
     total = ladder_for([0, 1], jnp.float32, "ladder_own", *last)
-    for part in got:
-        total = total + part.astype(jnp.float32)
+    total = add_up(total, got)
     total = total[0] + swap(total[1].astype(jnp.bfloat16), "cd", slabs, 1).astype(jnp.float32)
     return total.astype(jnp.bfloat16)
 

time: 57.3 us -> 56 us (0.977)
  waiting for transfers between devices: 10.5 us -> 9.53 us
  starting transfers between devices: 22 us -> 21.3 us
    ppermute x9, waiting for transfers between devices: 10.5 us -> 8.24 us  [swap(): return lax.ppermute(x, axis, [(i, i ^ mask) for i in range(size)])]
    all_to_all x1, waiting for transfers between devices: 0.01 us -> 1.29 us  [on_device(): coded = lax.all_to_all(coded, 'cd', split_axis=0, concat_axis=0, tiled=True)]
    ppermute x9, starting transfers between devices: 14.6 us -> 13.9 us  [swap(): return lax.ppermute(x, axis, [(i, i ^ mask) for i in range(size)])]
    pallas_call x2 -> x3, Pallas kernels: 7.3 us -> 7.65 us  [direct_for(): pl.pallas_call(functools.partial(direct_kernel if old else direct_first,...]
    pallas_call x3 -> x4, Pallas kernels: 1.8 us -> 1.74 us  [crossed_for(): pl.pallas_call(functools.partial(crossed_kernel, group, pairs, shift, orb...]
  transfers between devices with their start and end apart: 10 -> 10, of which waited for: 6 -> 5; matrix products, arithmetic and copies ran while one was open for 0% -> 0% of each run, Pallas kernels for 20% -> 24%
where the time goes in v4:
time: 56 us; the launch traced here: 55.6 us
  starting transfers between devices  21.3 us (38%)
  Pallas kernels  15.5 us (28%)
  waiting for transfers between devices  9.53 us (17%)
  blocking collectives  5.83 us (10%)
  local copies, waits for them, and re-layouts  1.85 us (3%)
  between operations  0.91 us (2%)
  other arithmetic  0.76 us (1%)
    ppermute x9, starting transfers between devices, swap(): return lax.ppermute(x, axis, [(i, i ^ mask) for i in range(size)])  13.9 us
    ppermute x9, waiting for transfers between devices, swap(): return lax.ppermute(x, axis, [(i, i ^ mask) for i in range(size)])  8.24 us
    pallas_call x3, Pallas kernels, direct_for(): pl.pallas_call(functools.partial(direct_kernel if old else direct_first,...  7.65 us
    all_to_all x1, starting transfers between devices, on_device(): coded = lax.all_to_all(coded, 'cd', split_axis=0, concat_axis=0, tiled=True)  7.4 us
    all_gather x1, blocking collectives, on_device(): gathered = [lax.all_gather(packed[:pair_block], 'ab', axis=0, tiled=True)]  5.83 us
    pallas_call x4, Pallas kernels, ladder_for(): pl.pallas_call(functools.partial(ladder_kernel, masks, len(gathered)), ou...  2.96 us
    unnamed x12, local copies, waits for them, and re-layouts  1.84 us
    pallas_call x4, Pallas kernels, crossed_for(): pl.pallas_call(functools.partial(crossed_kernel, group, pairs, shift, orb...  1.74 us
  transfers between devices with their start and end apart: 10, of which 5 were waited for; matrix products, arithmetic and copies ran while one was open for 0% of the time, Pallas kernels for 24%

profile of v4, /device:TPU:0, one launch (start us, length us, event | category | flops | bytes accessed | tf_op | source)
XLA Modules:
  0.0 55.6 jit_solution(2164332008272653732)
XLA Ops:
  0.7 1.4 %code.1.args_1_.coded_ref = s32[8,16,128]{2,1,0:T(8,128)} custom-call(s32[16,128]{1,0:T(8,128)} %bitcast.27, s32[16,128]{1,0:T(8,128)} %bitcast.28, s32[1]{0:T(128)S(6)} %copy.6.live_ref), custom_call_target="tpu_custom_call" | custom-call | flops 22000001024 | bytes 1 | tf_op jit(solution)/shard_map/code/pallas_call | solution.py:210
  2.0 0.0 copy-start.1
  2.0 7.4 %all-to-all-start = ((s32[8,16,128]{2,1,0:T(8,128)}), s32[8,16,128]{2,1,0:T(8,128)S(1)}, u32[]{:S(2)}, u32[]{:S(2)}) async-start(s32[8,16,128]{2,1,0:T(8,128)} %code.1.args_1_.coded_ref), calls=%async_computation | async-start | bytes 131072 | tf_op jit(solution)/shard_map/all_to_all | solution.py:222
  9.4 0.0 copy-start
  9.4 1.8 %copy-done = bf16[16,100,800]{2,0,1:T(8,128)(2,1)S(1)} copy-done((bf16[16,100,800]{2,0,1:T(8,128)(2,1)S(1)}, bf16[16,100,800]{2,0,1:T(8,128)(2,1)}, u32[]{:S(2)}) %copy-start) | copy-done | bytes 2560024
  11.3 1.7 %pack.1.args_0_.packed_ref = bf16[8,320,512]{2,1,0:T(8,128)(2,1)S(1)} custom-call(bf16[1600,800]{1,0:T(8,128)(2,1)S(1)} %bitcast.26), custom_call_target="tpu_custom_call" | custom-call | bytes 5120000 | tf_op jit(solution)/shard_map/pack/pallas_call | solution.py:230
  13.0 0.0 copy-done.1
  13.0 0.0 copy-start.2
  13.0 0.0 copy-start.3
  13.0 2.0 %direct.3.refs_0_ = bf16[16,2048]{1,0:T(8,128)(2,1)S(1)} custom-call(bf16[8,320,512]{2,1,0:T(8,128)(2,1)S(1)} %pack.1.args_0_.packed_ref, s32[8,16,128]{2,1,0:T(8,128)S(1)} %copy-done.1), custom_call_target="tpu_custom_call" | custom-call | flops 1342177280 | bytes 1 | tf_op jit(solution)/shard_map/direct/pallas_call | solution.py:245
  15.1 1.3 %all-to-all-done.coded_ref = s32[8,16,128]{2,1,0:T(8,128)S(1)} async-done(((s32[8,16,128]{2,1,0:T(8,128)}), s32[8,16,128]{2,1,0:T(8,128)S(1)}, u32[]{:S(2)}, u32[]{:S(2)}) %all-to-all-start) | async-done | bytes 65568 | tf_op jit(solution)/shard_map/all_to_all | solution.py:222
  16.4 0.8 %collective-permute-start = (bf16[2,16,2048]{2,1,0:T(8,128)(2,1)S(1)}, bf16[2,16,2048]{2,1,0:T(8,128)(2,1)S(1)}, u32[]{:S(2)}, u32[]{:S(2)}) collective-permute-start(bf16[2,16,2048]{2,1,0:T(8,128)(2,1)S(1)} %crossed_far.2.refs_0_), channel_id=1, source_target_pairs={{0,1},{1,0},{2,3},{3,2},{4,5},{5,4},{6,7},{7,6},{8,9},{9,8},{10,11... | collective-permute-start | bytes 393224 | tf_op jit(solution)/shard_map/ppermute | solution.py:37
  17.2 0.0 copy-done.2
  17.2 0.0 copy-done.3
  17.2 3.1 %collective-permute-start.1 = (bf16[2,16,2048]{2,1,0:T(8,128)(2,1)S(1)}, bf16[2,16,2048]{2,1,0:T(8,128)(2,1)S(1)}, u32[]{:S(2)}, u32[]{:S(2)}) collective-permute-start(bf16[2,16,2048]{2,1,0:T(8,128)(2,1)S(1)} %crossed_far.3.refs_0_), channel_id=1, source_target_pairs={{0,1},{1,0},{2,3},{3,2},{4,5},{5,4},{6,7},{7,6},{8,9},{9,8},{10,11... | collective-permute-start | bytes 393224 | tf_op jit(solution)/shard_map/ppermute | solution.py:37
  20.3 0.0 slice-start
  20.3 1.8 %collective-permute-done = bf16[2,16,2048]{2,1,0:T(8,128)(2,1)S(1)} collective-permute-done((bf16[2,16,2048]{2,1,0:T(8,128)(2,1)S(1)}, bf16[2,16,2048]{2,1,0:T(8,128)(2,1)S(1)}, u32[]{:S(2)}, u32[]{:S(2)}) %collective-permute-start) | collective-permute-done | bytes 131104 | tf_op jit(solution)/shard_map/ppermute | solution.py:37
  22.1 4.6 %collective-permute-start.2 = (bf16[16,2048]{1,0:T(8,128)(2,1)S(1)}, bf16[16,2048]{1,0:T(8,128)(2,1)S(1)}, u32[]{:S(2)}, u32[]{:S(2)}) collective-permute-start(bf16[16,2048]{1,0:T(8,128)(2,1)S(1)} %get-tuple-element.12), channel_id=1, source_target_pairs={{0,6},{1,7},{2,4},{3,5},{4,2},{5,3},{6,0},{7,1},{8,14},{9,15},{10,... | collective-permute-start | bytes 196616 | tf_op jit(solution)/shard_map/ppermute | solution.py:37
  26.8 0.0 collective-permute-start.3
  26.8 1.7 %crossed_near.3 = bf16[2,16,2048]{2,1,0:T(8,128)(2,1)S(1)} custom-call(bf16[8,320,512]{2,1,0:T(8,128)(2,1)S(1)} %pack.1.args_0_.packed_ref, s32[8,16,128]{2,1,0:T(8,128)S(1)} %all-to-all-done.coded_ref, bf16[2,16,2048]{2,1,0:T(8,128)(2,1)S(1)} %add.22.refs_0_), custom_call_target="tpu_custom_call" | custom-call | flops 11000000 | bytes 1 | tf_op jit(solution)/shard_map/crossed_near/pallas_call | solution.py:260
  28.5 0.0 collective-permute-done.1
  28.5 0.0 slice-start.1
  28.6 0.7 %collective-permute-start.4 = (bf16[16,2048]{1,0:T(8,128)(2,1)S(1)}, bf16[16,2048]{1,0:T(8,128)(2,1)S(1)}, u32[]{:S(2)}, u32[]{:S(2)}) collective-permute-start(bf16[16,2048]{1,0:T(8,128)(2,1)S(1)} %get-tuple-element.9), channel_id=1, source_target_pairs={{0,2},{1,3},{2,0},{3,1},{4,6},{5,7},{6,4},{7,5},{8,10},{9,11},{10,... | collective-permute-start | bytes 196616 | tf_op jit(solution)/shard_map/ppermute | solution.py:37
  29.3 1.8 %direct.4.refs_0_ = bf16[16,2048]{1,0:T(8,128)(2,1)S(1)} custom-call(bf16[8,320,512]{2,1,0:T(8,128)(2,1)S(1)} %pack.1.args_0_.packed_ref, s32[8,16,128]{2,1,0:T(8,128)S(1)} %copy-done.1, bf16[16,2048]{1,0:T(8,128)(2,1)S(1)} %direct.3.refs_0_, bf16[2,16,2048]{2,1,0:T(8,128)(2,1)S(1)} %add.23.refs_1_), custom_call_target="tpu_custom_call" | custom-call | flops 11000000 | bytes 1 | tf_op jit(solution)/shard_map/direct/pallas_call | solution.py:245
  31.1 3.8 %direct.5 = bf16[16,2048]{1,0:T(8,128)(2,1)S(1)} custom-call(bf16[8,320,512]{2,1,0:T(8,128)(2,1)S(1)} %pack.1.args_0_.packed_ref, s32[8,16,128]{2,1,0:T(8,128)S(1)} %copy-done.1, bf16[16,2048]{1,0:T(8,128)(2,1)S(1)} %direct.4.refs_0_, bf16[2,16,2048]{2,1,0:T(8,128)(2,1)S(1)} %add.23.refs_1_), custom_call_target="tpu_custom_call" | custom-call | flops 11000000 | bytes 1 | tf_op jit(solution)/shard_map/direct/pallas_call | solution.py:245
  34.9 0.0 collective-permute-done.2.refs_1_
  34.9 0.0 collective-permute-done.3.refs_1_
  35.0 0.0 collective-permute-done.4
  35.0 5.8 %all_gather.3.refs_0_ = bf16[64,2048]{1,0:T(8,128)(2,1)S(1)} all-gather(bf16[16,2048]{1,0:T(8,128)(2,1)S(1)} %multiply_convert_fusion), channel_id=1, replica_groups=mesh['ab'=4,'cd'=8] {'ab'}, dimensions={0}, use_global_device_ids=true | all-gather | bytes 327680 | tf_op jit(solution)/shard_map/all_gather | solution.py:288
  40.8 0.0 slice-done
  40.8 0.0 slice-done.1
  40.8 0.7 %ladder.3.refs_2_ = bf16[2,64,256]{2,1,0:T(8,128)(2,1)S(1)} custom-call(bf16[64,2048]{1,0:T(8,128)(2,1)S(1)} %all_gather.3.refs_0_, bf16[2048,2048]{1,0:T(8,128)(2,1)S(1)} %bitcast.25), custom_call_target="tpu_custom_call" | custom-call | flops 11000000 | bytes 1 | tf_op jit(solution)/shard_map/ladder/pallas_call | solution.py:294
  41.6 0.4 collective-permute-start.5
  41.9 0.7 %ladder.4.refs_2_ = bf16[2,64,256]{2,1,0:T(8,128)(2,1)S(1)} custom-call(bf16[64,2048]{1,0:T(8,128)(2,1)S(1)} %all_gather.3.refs_0_, bf16[2048,2048]{1,0:T(8,128)(2,1)S(1)} %bitcast.25, bf16[2,64,256]{2,1,0:T(8,128)(2,1)S(1)} %ladder.3.refs_2_), custom_call_target="tpu_custom_call" | custom-call | flops 11000000 | bytes 1 | tf_op jit(solution)/shard_map/ladder/pallas_call | solution.py:294
  42.7 0.9 %collective-permute-start.6 = (bf16[2,64,256]{2,1,0:T(8,128)(2,1)S(1)}, bf16[2,64,256]{2,1,0:T(8,128)(2,1)S(1)}, u32[]{:S(2)}, u32[]{:S(2)}) collective-permute-start(bf16[2,64,256]{2,1,0:T(8,128)(2,1)S(1)} %ladder.4.refs_2_), channel_id=1, source_target_pairs={{0,4},{1,5},{2,6},{3,7},{4,0},{5,1},{6,2},{7,3},{8,12},{9,13},{10,... | collective-permute-start | bytes 196616 | tf_op jit(solution)/shard_map/ppermute | solution.py:37
  43.5 0.7 %ladder.5.refs_2_ = bf16[2,64,256]{2,1,0:T(8,128)(2,1)S(1)} custom-call(bf16[64,2048]{1,0:T(8,128)(2,1)S(1)} %all_gather.3.refs_0_, bf16[2048,2048]{1,0:T(8,128)(2,1)S(1)} %bitcast.25, bf16[2,64,256]{2,1,0:T(8,128)(2,1)S(1)} %ladder.4.refs_2_), custom_call_target="tpu_custom_call" | custom-call | flops 11000000 | bytes 1 | tf_op jit(solution)/shard_map/ladder/pallas_call | solution.py:294
  44.3 3.4 %collective-permute-start.7 = (bf16[2,64,256]{2,1,0:T(8,128)(2,1)S(1)}, bf16[2,64,256]{2,1,0:T(8,128)(2,1)S(1)}, u32[]{:S(2)}, u32[]{:S(2)}) collective-permute-start(bf16[2,64,256]{2,1,0:T(8,128)(2,1)S(1)} %ladder.5.refs_2_), channel_id=1, source_target_pairs={{0,2},{1,3},{2,0},{3,1},{4,6},{5,7},{6,4},{7,5},{8,10},{9,11},{10,... | collective-permute-start | bytes 196616 | tf_op jit(solution)/shard_map/ppermute | solution.py:37
  47.7 0.8 %ladder_own.1.refs_0_ = f32[2,64,256]{2,1,0:T(8,128)S(1)} custom-call(bf16[64,2048]{1,0:T(8,128)(2,1)S(1)} %all_gather.3.refs_0_, bf16[2048,2048]{1,0:T(8,128)(2,1)S(1)} %bitcast.25, bf16[2,64,256]{2,1,0:T(8,128)(2,1)S(1)} %ladder.5.refs_2_), custom_call_target="tpu_custom_call" | custom-call | flops 11000000 | bytes 1 | tf_op jit(solution)/shard_map/ladder_own/pallas_call | solution.py:294
  48.4 0.0 collective-permute-done.5.refs_1_
  48.5 2.1 %collective-permute-done.6.refs_1_ = bf16[2,64,256]{2,1,0:T(8,128)(2,1)S(1)} collective-permute-done((bf16[2,64,256]{2,1,0:T(8,128)(2,1)S(1)}, bf16[2,64,256]{2,1,0:T(8,128)(2,1)S(1)}, u32[]{:S(2)}, u32[]{:S(2)}) %collective-permute-start.6) | collective-permute-done | bytes 65568 | tf_op jit(solution)/shard_map/ppermute | solution.py:37
  50.7 0.4 collective-permute-done.7
  51.0 0.1 collective-permute-start.8
  51.1 3.9 %collective-permute-done.8 = bf16[64,256]{1,0:T(8,128)(2,1)S(1)} collective-permute-done((bf16[64,256]{1,0:T(8,128)(2,1)S(1)}, bf16[64,256]{1,0:T(8,128)(2,1)S(1)}, u32[]{:S(2)}, u32[]{:S(2)}) %collective-permute-start.8) | collective-permute-done | bytes 32800 | tf_op jit(solution)/shard_map/ppermute | solution.py:37
  55.0 0.6 %fusion.1 = bf16[64,256]{1,0:T(8,128)(2,1)} fusion(f32[2,64,256]{2,1,0:T(8,128)S(1)} %convert_add_fusion, bf16[64,256]{1,0:T(8,128)(2,1)S(1)} %collective-permute-done.8), kind=kLoop, calls=%fused_computation.5 | loop fusion | flops 49152 | bytes 131072 | tf_op jit(solution)/shard_map/convert_element_type | solution.py:311
  (16 shorter events, 0.3 us)
Async XLA Ops:
  2.0 10.9 %copy-start.1 = (s32[8,16,128]{2,1,0:T(8,128)S(1)}, s32[8,16,128]{2,1,0:T(8,128)}, u32[]{:S(2)}) copy-start(s32[8,16,128]{2,1,0:T(8,128)} %code.1.args_1_.coded_ref) | copy-start | bytes 196612
  2.0 14.3 %all-to-all-start = ((s32[8,16,128]{2,1,0:T(8,128)}), s32[8,16,128]{2,1,0:T(8,128)S(1)}, u32[]{:S(2)}, u32[]{:S(2)}) async-start(s32[8,16,128]{2,1,0:T(8,128)} %code.1.args_1_.coded_ref), calls=%async_computation | async-start | bytes 131072 | tf_op jit(solution)/shard_map/all_to_all | solution.py:222
  9.4 1.8 %copy-start = (bf16[16,100,800]{2,0,1:T(8,128)(2,1)S(1)}, bf16[16,100,800]{2,0,1:T(8,128)(2,1)}, u32[]{:S(2)}) copy-start(bf16[16,100,800]{2,0,1:T(8,128)(2,1)} %param.6) | copy-start | bytes 7680004
  13.0 4.2 %copy-start.2 = (s32[2048]{0:T(1024)S(1)}, s32[2048]{0:T(1024)}, u32[]{:S(2)}) copy-start(s32[2048]{0:T(1024)} %param.7) | copy-start | bytes 24580
  13.0 4.2 %copy-start.3 = (s32[2048]{0:T(1024)S(1)}, s32[2048]{0:T(1024)}, u32[]{:S(2)}) copy-start(s32[2048]{0:T(1024)} %param.8) | copy-start | bytes 24580
  16.4 5.7 %collective-permute-start = (bf16[2,16,2048]{2,1,0:T(8,128)(2,1)S(1)}, bf16[2,16,2048]{2,1,0:T(8,128)(2,1)S(1)}, u32[]{:S(2)}, u32[]{:S(2)}) collective-permute-start(bf16[2,16,2048]{2,1,0:T(8,128)(2,1)S(1)} %crossed_far.2.refs_0_), channel_id=1, source_target_pairs={{0,1},{1,0},{2,3},{3,2},{4,5},{5,4},{6,7},{7,6},{8,9},{9,8},{10,11... | collective-permute-start | bytes 393224 | tf_op jit(solution)/shard_map/ppermute | solution.py:37
  17.2 11.2 %collective-permute-start.1 = (bf16[2,16,2048]{2,1,0:T(8,128)(2,1)S(1)}, bf16[2,16,2048]{2,1,0:T(8,128)(2,1)S(1)}, u32[]{:S(2)}, u32[]{:S(2)}) collective-permute-start(bf16[2,16,2048]{2,1,0:T(8,128)(2,1)S(1)} %crossed_far.3.refs_0_), channel_id=1, source_target_pairs={{0,1},{1,0},{2,3},{3,2},{4,5},{5,4},{6,7},{7,6},{8,9},{9,8},{10,11... | collective-permute-start | bytes 393224 | tf_op jit(solution)/shard_map/ppermute | solution.py:37
  20.3 20.6 %slice-start = ((s8[8388608]{0:T(1024)(128)(4,1)}), s8[4194304]{0:T(1024)(128)(4,1)S(1)}, s32[]{:S(2)}) async-start(s8[8388608]{0:T(1024)(128)(4,1)} %bitcast.24), calls=%async_computation.1 | async-start | bytes 8388608
  22.1 12.8 %collective-permute-start.2 = (bf16[16,2048]{1,0:T(8,128)(2,1)S(1)}, bf16[16,2048]{1,0:T(8,128)(2,1)S(1)}, u32[]{:S(2)}, u32[]{:S(2)}) collective-permute-start(bf16[16,2048]{1,0:T(8,128)(2,1)S(1)} %get-tuple-element.12), channel_id=1, source_target_pairs={{0,6},{1,7},{2,4},{3,5},{4,2},{5,3},{6,0},{7,1},{8,14},{9,15},{10,... | collective-permute-start | bytes 196616 | tf_op jit(solution)/shard_map/ppermute | solution.py:37
  26.8 8.2 %collective-permute-start.3 = (bf16[16,2048]{1,0:T(8,128)(2,1)S(1)}, bf16[16,2048]{1,0:T(8,128)(2,1)S(1)}, u32[]{:S(2)}, u32[]{:S(2)}) collective-permute-start(bf16[16,2048]{1,0:T(8,128)(2,1)S(1)} %get-tuple-element.11), channel_id=1, source_target_pairs={{0,4},{1,5},{2,6},{3,7},{4,0},{5,1},{6,2},{7,3},{8,12},{9,13},{10,... | collective-permute-start | bytes 196616 | tf_op jit(solution)/shard_map/ppermute | solution.py:37
  28.5 12.3 %slice-start.1 = ((s8[8388608]{0:T(1024)(128)(4,1)}), s8[4194304]{0:T(1024)(128)(4,1)S(1)}, s32[]{:S(2)}) async-start(s8[8388608]{0:T(1024)(128)(4,1)} %bitcast.24), calls=%async_computation.2 | async-start | bytes 8388608
  28.6 6.4 %collective-permute-start.4 = (bf16[16,2048]{1,0:T(8,128)(2,1)S(1)}, bf16[16,2048]{1,0:T(8,128)(2,1)S(1)}, u32[]{:S(2)}, u32[]{:S(2)}) collective-permute-start(bf16[16,2048]{1,0:T(8,128)(2,1)S(1)} %get-tuple-element.9), channel_id=1, source_target_pairs={{0,2},{1,3},{2,0},{3,1},{4,6},{5,7},{6,4},{7,5},{8,10},{9,11},{10,... | collective-permute-start | bytes 196616 | tf_op jit(solution)/shard_map/ppermute | solution.py:37
  41.6 6.9 %collective-permute-start.5 = (bf16[2,64,256]{2,1,0:T(8,128)(2,1)S(1)}, bf16[2,64,256]{2,1,0:T(8,128)(2,1)S(1)}, u32[]{:S(2)}, u32[]{:S(2)}) collective-permute-start(bf16[2,64,256]{2,1,0:T(8,128)(2,1)S(1)} %ladder.3.refs_2_), channel_id=1, source_target_pairs={{0,6},{1,7},{2,4},{3,5},{4,2},{5,3},{6,0},{7,1},{8,14},{9,15},{10,... | collective-permute-start | bytes 196616 | tf_op jit(solution)/shard_map/ppermute | solution.py:37
  42.7 8.0 %collective-permute-start.6 = (bf16[2,64,256]{2,1,0:T(8,128)(2,1)S(1)}, bf16[2,64,256]{2,1,0:T(8,128)(2,1)S(1)}, u32[]{:S(2)}, u32[]{:S(2)}) collective-permute-start(bf16[2,64,256]{2,1,0:T(8,128)(2,1)S(1)} %ladder.4.refs_2_), channel_id=1, source_target_pairs={{0,4},{1,5},{2,6},{3,7},{4,0},{5,1},{6,2},{7,3},{8,12},{9,13},{10,... | collective-permute-start | bytes 196616 | tf_op jit(solution)/shard_map/ppermute | solution.py:37
  44.3 6.7 %collective-permute-start.7 = (bf16[2,64,256]{2,1,0:T(8,128)(2,1)S(1)}, bf16[2,64,256]{2,1,0:T(8,128)(2,1)S(1)}, u32[]{:S(2)}, u32[]{:S(2)}) collective-permute-start(bf16[2,64,256]{2,1,0:T(8,128)(2,1)S(1)} %ladder.5.refs_2_), channel_id=1, source_target_pairs={{0,2},{1,3},{2,0},{3,1},{4,6},{5,7},{6,4},{7,5},{8,10},{9,11},{10,... | collective-permute-start | bytes 196616 | tf_op jit(solution)/shard_map/ppermute | solution.py:37
  51.0 4.0 %collective-permute-start.8 = (bf16[64,256]{1,0:T(8,128)(2,1)S(1)}, bf16[64,256]{1,0:T(8,128)(2,1)S(1)}, u32[]{:S(2)}, u32[]{:S(2)}) collective-permute-start(bf16[64,256]{1,0:T(8,128)(2,1)S(1)} %fusion.3), channel_id=1, source_target_pairs={{0,1},{1,0},{2,3},{3,2},{4,5},{5,4},{6,7},{7,6},{8,9},{9,8},{10,11... | collective-permute-start | bytes 98312 | tf_op jit(solution)/shard_map/ppermute | solution.py:37

commit v5 on v4

--- a/solution.py
+++ b/solution.py
@@ -12,6 +12,7 @@
 MIB = 1024 * 1024
 VMEM = pl.BlockSpec(memory_space=pltpu.VMEM)
 ANY = pl.BlockSpec(memory_space=pl.ANY)
+HBM = pl.BlockSpec(memory_space=pltpu.HBM)
 
 
 def group_size(orbits):
@@ -33,15 +34,18 @@
 SMALL = spent(0.01)
 
 
+def in_hbm(x):
+    return pltpu.with_memory_space_constraint(x, pltpu.HBM)
+
+
 def swap(x, axis, size, mask):
     return lax.ppermute(x, axis, [(i, i ^ mask) for i in range(size)])
 
 
-def code_kernel(slabs, orbits, shift, first_ref, second_ref, live_ref, coded_ref, first_here, second_here, live_here, sems):
+def code_kernel(slabs, orbits, shift, first_ref, second_ref, coded_ref, own_ref, first_here, second_here, sems):
     copies = [
         pltpu.make_async_copy(first_ref, first_here, sems.at[0]),
         pltpu.make_async_copy(second_ref, second_here, sems.at[1]),
-        pltpu.make_async_copy(live_ref, live_here, sems.at[2]),
     ]
     for copy in copies:
         copy.start()
@@ -49,23 +53,31 @@
         copy.wait()
     base = lax.axis_index("cd") * orbits
     coded = ((first_here[...] - base) << shift) + second_here[...]
-    shape = coded.shape
-    slots = lax.broadcasted_iota(jnp.int32, shape, 0) * shape[1] + lax.broadcasted_iota(jnp.int32, shape, 1)
-    coded = jnp.where(slots < live_here[0], coded, -1)
+    own_ref[...] = coded
     for s in range(slabs):
         coded_ref[s] = coded
 
 
-def pack_kernel(slabs, orbits, group, pairs, table_ref, packed_ref):
-    for s in range(slabs):
-        for g in range(table_ref.shape[0] // (group * pairs)):
-            parts = [
-                table_ref[(g * group + k) * pairs : (g * group + k + 1) * pairs, s * orbits : (s + 1) * orbits]
-                for k in range(group)
-            ]
-            if group * orbits < DEPTH:
-                parts.append(jnp.zeros((pairs, DEPTH - group * orbits), jnp.bfloat16))
-            packed_ref[s, g * pairs : (g + 1) * pairs, :] = jnp.concatenate(parts, axis=1)
+def pack_kernel(slabs, orbits, group, pairs, table_ref, packed_ref, here_ref, sems):
+    steps = sems.shape[0]
+    rows = table_ref.shape[0] // steps
+    copies = []
+    for i in range(steps):
+        at = pl.ds(i * rows, rows)
+        copies.append(pltpu.make_async_copy(table_ref.at[at], here_ref.at[at], sems.at[i]))
+        copies[i].start()
+    per_step = rows // (group * pairs)
+    for i in range(steps):
+        copies[i].wait()
+        for s in range(slabs):
+            for g in range(i * per_step, (i + 1) * per_step):
+                parts = [
+                    here_ref[(g * group + k) * pairs : (g * group + k + 1) * pairs, s * orbits : (s + 1) * orbits]
+                    for k in range(group)
+                ]
+                if group * orbits < DEPTH:
+                    parts.append(jnp.zeros((pairs, DEPTH - group * orbits), jnp.bfloat16))
+                packed_ref[s, g * pairs : (g + 1) * pairs, :] = jnp.concatenate(parts, axis=1)
 
 
 def lookup(table, pairs, keys, groups, totals):
@@ -96,7 +108,7 @@
         coded = coded_ref[slab]
         first = coded >> shift
         second = (coded & ((1 << shift) - 1)) - base
-        here = jnp.logical_and(coded >= 0, jnp.logical_and(second >= 0, second < orbits))
+        here = jnp.logical_and(second >= 0, second < orbits)
         second = jnp.where(here, second, 0)
         groups = lax.div(second, jnp.int32(group))
         keys = (second - groups * group) * orbits + first
@@ -121,24 +133,26 @@
                 crossed_ref[out] = jnp.zeros(crossed_ref.shape[1:], jnp.bfloat16)
 
 
-def direct_kernel(group, pairs, shift, orbits, slabs, low, high, packed_ref, coded_ref, *refs):
+def direct_kernel(group, pairs, shift, orbits, slabs, lower, upper, packed_ref, coded_ref, *refs):
     old_ref, direct_ref = refs[0], refs[-1]
     me = lax.axis_index("cd")
-    coded = coded_ref[0]
-    first = coded >> shift
-    second = coded & ((1 << shift) - 1)
-    groups = jnp.where(coded >= 0, lax.div(first, jnp.int32(group)), -1)
-    owner = lax.div(second, jnp.int32(orbits))
-    keys = lax.rem(first, jnp.int32(group)) * orbits + (second - owner * orbits)
-    lines = coded.shape[0]
-    step = min(lines, 4)
+    upper_half = lax.div(me, jnp.int32(slabs // 2))
+    begin = me + lower[0] + upper_half * (upper[0] - lower[0])
+    end = lax.min(me + lower[1] + upper_half * (upper[1] - lower[1]), jnp.int32(slabs))
     direct_ref[...] = jnp.zeros(direct_ref.shape, jnp.bfloat16) if old_ref is None else old_ref[...]
 
-    for ahead in range(low, high):
-
-        @pl.when(me + ahead < slabs)
-        def _(ahead=ahead):
-            slab = me + ahead
+    @pl.when(begin < end)
+    def _():
+        coded = coded_ref[...]
+        first = coded >> shift
+        second = coded & ((1 << shift) - 1)
+        groups = lax.div(first, jnp.int32(group))
+        owner = lax.div(second, jnp.int32(orbits))
+        keys = (first - groups * group) * orbits + (second - owner * orbits)
+        lines = coded.shape[0]
+        step = min(lines, 4)
+
+        def one(slab, carry):
             for i in range(0, lines, step):
                 here = slice(i * LANES, (i + step) * LANES)
                 old = direct_ref[:, here].astype(jnp.float32)
@@ -146,6 +160,9 @@
                 chosen = jnp.where(owner[i : i + step] == slab, groups[i : i + step], -1)
                 got = lookup(packed_ref[slab], pairs, keys[i : i + step], chosen, got)
                 direct_ref[:, here] = jnp.concatenate(got, axis=0).astype(jnp.bfloat16)
+            return carry
+
+        lax.fori_loop(begin, end, one, 0)
 
 
 def direct_first(*args):
@@ -207,18 +224,19 @@
     near = list(range(0, slabs, 2))
     far = list(range(1, slabs, 2))
 
-    coded = pl.pallas_call(
+    coded, own_coded = pl.pallas_call(
         functools.partial(code_kernel, slabs, orbits, shift),
-        out_shape=jax.ShapeDtypeStruct((slabs, lines, LANES), jnp.int32),
-        in_specs=[ANY] * 3,
-        out_specs=VMEM,
-        scratch_shapes=[pltpu.VMEM((lines, LANES), jnp.int32)] * 2
-        + [pltpu.SMEM((1,), jnp.int32), pltpu.SemaphoreType.DMA((3,))],
-        compiler_params=params(58),
+        out_shape=(
+            jax.ShapeDtypeStruct((slabs, lines, LANES), jnp.int32),
+            jax.ShapeDtypeStruct((lines, LANES), jnp.int32),
+        ),
+        in_specs=[HBM] * 2,
+        out_specs=(VMEM, VMEM),
+        scratch_shapes=[pltpu.VMEM((lines, LANES), jnp.int32)] * 2 + [pltpu.SemaphoreType.DMA((2,))],
+        compiler_params=params(4),
         cost_estimate=spent(20),
         name="code",
-    )(cd_first.reshape(lines, LANES), cd_second.reshape(lines, LANES), live_cols)
-    own_coded = coded
+    )(in_hbm(cd_first.reshape(lines, LANES)), in_hbm(cd_second.reshape(lines, LANES)))
     coded = lax.all_to_all(coded, "cd", split_axis=0, concat_axis=0, tiled=True)
 
     table = jnp.transpose(amplitudes, (1, 0, 2))
@@ -230,30 +248,34 @@
     table = pl.pallas_call(
         functools.partial(pack_kernel, slabs, orbits, group, pairs),
         out_shape=jax.ShapeDtypeStruct((slabs, packed_rows, DEPTH), jnp.bfloat16),
-        grid=(steps,),
-        in_specs=[pl.BlockSpec((orbits * pairs // steps, orbitals), lambda i: (i, 0))],
-        out_specs=pl.BlockSpec((slabs, packed_rows // steps, DEPTH), lambda i: (0, i, 0)),
+        in_specs=[HBM],
+        out_specs=VMEM,
+        scratch_shapes=[
+            pltpu.VMEM((orbits * pairs, orbitals), jnp.bfloat16),
+            pltpu.SemaphoreType.DMA((steps,)),
+        ],
         compiler_params=params(16),
         cost_estimate=cost(0, 4 * orbits * pairs * orbitals),
         name="pack",
-    )(table)
+    )(in_hbm(table))
 
     lookup_flops = 2 * packed_rows * DEPTH * columns
     lookup_bytes = packed_rows * DEPTH * 2 + columns * pairs * 2
 
-    def direct_for(low, high, *old):
+    def direct_for(lower, upper, *old):
         return pl.pallas_call(
-            functools.partial(direct_kernel if old else direct_first, group, pairs, shift, orbits, slabs, low, high),
+            functools.partial(direct_kernel if old else direct_first, group, pairs, shift, orbits, slabs, lower, upper),
             out_shape=jax.ShapeDtypeStruct((pairs, columns), jnp.bfloat16),
             in_specs=[VMEM] * 2 + [VMEM, ANY][: len(old)],
             out_specs=VMEM,
             compiler_params=params(20),
-            cost_estimate=SMALL if old else cost((high - low) * lookup_flops, 1),
+            cost_estimate=SMALL if old else spent(2),
             name="direct",
         )(table, own_coded, *old)
 
-    cuts = sorted({0, min(2, slabs), min(4, slabs), slabs})
-    direct = direct_for(cuts[0], cuts[1])
+    half = max(slabs // 2, 1)
+    ends = [0, half - half // 4, 2 * (half - half // 4), slabs]
+    direct = direct_for((ends[0], ends[1]), (0, 0))
     coded, direct = lax.optimization_barrier((coded, direct))
 
     def crossed_for(masks, name, *after):
@@ -270,6 +292,9 @@
     pairs_of = [near[at : at + 2] for at in reversed(range(0, slabs // 2, 2))]
     arrived, last = [], ()
     for masks in pairs_of:
+        if arrived:
+            direct = direct_for((ends[1], ends[2]), (0, 0), direct, *last)
+            last = (direct,)
         last = (crossed_for([mask + 1 for mask in masks], "crossed_far", *last),)
         arrived.append(swap(last[0], "cd", slabs, 1))
     got = []
@@ -279,11 +304,13 @@
         for k in reversed(range(len(masks))):
             if masks[k]:
                 got.append(swap(merged[k], "cd", slabs, masks[k]))
-    for low, high in zip(cuts[1:], cuts[2:]):
-        direct = direct_for(low, high, direct, *last)
+    direct = direct_for((ends[2], ends[3]), (0, slabs - half), direct, *last)
     crossed = add_up(merged[0].astype(jnp.float32), got)
-    half = jnp.where(cd_first == cd_second, jnp.float32(0.5), jnp.float32(1.0))
-    packed = ((direct.astype(jnp.float32) + crossed) * half[None, :]).astype(jnp.bfloat16)
+    live_cols, _ = lax.optimization_barrier((live_cols, merged))
+    slots = jnp.arange(columns, dtype=jnp.int32)
+    live = (slots < live_cols[0]).astype(jnp.float32)
+    weight = jnp.where(cd_first == cd_second, jnp.float32(0.5), jnp.float32(1.0)) * live
+    packed = ((direct.astype(jnp.float32) + crossed) * weight[None, :]).astype(jnp.bfloat16)
 
     gathered = [lax.all_gather(packed[:pair_block], "ab", axis=0, tiled=True)]
     all_pairs = blocks * pair_block

time: 56 us -> 53.1 us (0.948)
  local copies, waits for them, and re-layouts: 1.85 us -> 0.04 us
  waiting for transfers between devices: 9.53 us -> 7.99 us
  Pallas kernels: 15.5 us -> 16.1 us
    unnamed x12 -> x8, local copies, waits for them, and re-layouts: 1.84 us -> 0.02 us
    ppermute x9, waiting for transfers between devices: 8.24 us -> 7.21 us  [swap(): return lax.ppermute(x, axis, [(i, i ^ mask) for i in range(size)])]
    pallas_call x1, Pallas kernels: 1.72 us -> 2.73 us  [on_device(): pl.pallas_call(functools.partial(pack_kernel, slabs, orbits, group, pairs...]
  transfers between devices with their start and end apart: 10 -> 10, of which waited for: 5 -> 5; matrix products, arithmetic and copies ran while one was open for 0% -> 0% of each run, Pallas kernels for 24% -> 27%
where the time goes in v5:
time: 53.1 us; the launch traced here: 52.7 us
  starting transfers between devices  21.1 us (40%)
  Pallas kernels  16.1 us (30%)
  waiting for transfers between devices  7.99 us (15%)
  blocking collectives  5.79 us (11%)
  between operations  0.88 us (2%)
  other arithmetic  0.76 us (1%)
    ppermute x9, starting transfers between devices, swap(): return lax.ppermute(x, axis, [(i, i ^ mask) for i in range(size)])  13.9 us
    all_to_all x1, starting transfers between devices, on_device(): coded = lax.all_to_all(coded, 'cd', split_axis=0, concat_axis=0, tiled=True)  7.26 us
    pallas_call x3, Pallas kernels, direct_for(): pl.pallas_call(functools.partial(direct_kernel if old else direct_first,...  7.24 us
    ppermute x9, waiting for transfers between devices, swap(): return lax.ppermute(x, axis, [(i, i ^ mask) for i in range(size)])  7.21 us
    all_gather x1, blocking collectives, on_device(): gathered = [lax.all_gather(packed[:pair_block], 'ab', axis=0, tiled=True)]  5.79 us
    pallas_call x4, Pallas kernels, ladder_for(): pl.pallas_call(functools.partial(ladder_kernel, masks, len(gathered)), ou...  2.96 us
    pallas_call x1, Pallas kernels, on_device(): pl.pallas_call(functools.partial(pack_kernel, slabs, orbits, group, pairs...  2.73 us
    pallas_call x4, Pallas kernels, crossed_for(): pl.pallas_call(functools.partial(crossed_kernel, group, pairs, shift, orb...  1.77 us
  transfers between devices with their start and end apart: 10, of which 5 were waited for; matrix products, arithmetic and copies ran while one was open for 0% of the time, Pallas kernels for 27%

profile of v5, /device:TPU:0, one launch (start us, length us, event | category | flops | bytes accessed | tf_op | source)
XLA Modules:
  0.0 52.7 jit_solution(14563769226976494828)
XLA Ops:
  0.0 1.4 %code.1 = (s32[8,16,128]{2,1,0:T(8,128)}, s32[16,128]{1,0:T(8,128)S(1)}) custom-call(s32[16,128]{1,0:T(8,128)} %bitcast.29, s32[16,128]{1,0:T(8,128)} %bitcast.30), custom_call_target="tpu_custom_call" | custom-call | flops 22000001024 | bytes 1 | tf_op jit(solution)/shard_map/code/pallas_call | solution.py:227
  1.4 7.3 %all-to-all-start = ((s32[8,16,128]{2,1,0:T(8,128)}), s32[8,16,128]{2,1,0:T(8,128)S(1)}, u32[]{:S(2)}, u32[]{:S(2)}) async-start(s32[8,16,128]{2,1,0:T(8,128)} %get-tuple-element.11), calls=%async_computation | async-start | bytes 131072 | tf_op jit(solution)/shard_map/all_to_all | solution.py:240
  8.6 2.7 %pack.1.args_0_.packed_ref = bf16[8,320,512]{2,1,0:T(8,128)(2,1)S(1)} custom-call(bf16[1600,800]{1,0:T(8,128)(2,1)} %bitcast.28), custom_call_target="tpu_custom_call" | custom-call | bytes 5120000 | tf_op jit(solution)/shard_map/pack/pallas_call | solution.py:248
  12.0 0.0 copy-start
  12.0 0.0 copy-start.1
  12.0 2.7 %direct.3.refs_0_ = bf16[16,2048]{1,0:T(8,128)(2,1)S(1)} custom-call(bf16[8,320,512]{2,1,0:T(8,128)(2,1)S(1)} %pack.1.args_0_.packed_ref, s32[16,128]{1,0:T(8,128)S(1)} %get-tuple-element.10.args_1_.coded_ref), custom_call_target="tpu_custom_call" | custom-call | flops 2200000000 | bytes 1 | tf_op jit(solution)/shard_map/direct/pallas_call | solution.py:266
  14.8 0.8 %all-to-all-done.coded_ref = s32[8,16,128]{2,1,0:T(8,128)S(1)} async-done(((s32[8,16,128]{2,1,0:T(8,128)}), s32[8,16,128]{2,1,0:T(8,128)S(1)}, u32[]{:S(2)}, u32[]{:S(2)}) %all-to-all-start) | async-done | bytes 65568 | tf_op jit(solution)/shard_map/all_to_all | solution.py:240
  15.6 1.3 %collective-permute-start = (bf16[2,16,2048]{2,1,0:T(8,128)(2,1)S(1)}, bf16[2,16,2048]{2,1,0:T(8,128)(2,1)S(1)}, u32[]{:S(2)}, u32[]{:S(2)}) collective-permute-start(bf16[2,16,2048]{2,1,0:T(8,128)(2,1)S(1)} %crossed_far.2.refs_1_), channel_id=1, source_target_pairs={{0,1},{1,0},{2,3},{3,2},{4,5},{5,4},{6,7},{7,6},{8,9},{9,8},{10,11... | collective-permute-start | bytes 393224 | tf_op jit(solution)/shard_map/ppermute | solution.py:42
  16.9 0.0 copy-done
  16.9 0.0 copy-done.1
  16.9 2.7 %direct.4.refs_0_ = bf16[16,2048]{1,0:T(8,128)(2,1)S(1)} custom-call(bf16[8,320,512]{2,1,0:T(8,128)(2,1)S(1)} %pack.1.args_0_.packed_ref, s32[16,128]{1,0:T(8,128)S(1)} %get-tuple-element.10.args_1_.coded_ref, bf16[16,2048]{1,0:T(8,128)(2,1)S(1)} %direct.3.refs_0_, bf16[2,16,2048]{2,1,0:T(8,128)(2,1)S(1)} %crossed_far.2.refs_1_), custom_call_target="tpu_custom_call" | custom-call | flops 11000000 | bytes 1 | tf_op jit(solution)/shard_map/direct/pallas_call | solution.py:266
  19.6 0.0 slice-start
  19.7 2.5 %collective-permute-start.1 = (bf16[2,16,2048]{2,1,0:T(8,128)(2,1)S(1)}, bf16[2,16,2048]{2,1,0:T(8,128)(2,1)S(1)}, u32[]{:S(2)}, u32[]{:S(2)}) collective-permute-start(bf16[2,16,2048]{2,1,0:T(8,128)(2,1)S(1)} %crossed_far.3.refs_0_), channel_id=1, source_target_pairs={{0,1},{1,0},{2,3},{3,2},{4,5},{5,4},{6,7},{7,6},{8,9},{9,8},{10,11... | collective-permute-start | bytes 393224 | tf_op jit(solution)/shard_map/ppermute | solution.py:42
  22.2 0.0 collective-permute-done
  22.3 1.4 %collective-permute-start.2 = (bf16[16,2048]{1,0:T(8,128)(2,1)S(1)}, bf16[16,2048]{1,0:T(8,128)(2,1)S(1)}, u32[]{:S(2)}, u32[]{:S(2)}) collective-permute-start(bf16[16,2048]{1,0:T(8,128)(2,1)S(1)} %get-tuple-element.18), channel_id=1, source_target_pairs={{0,6},{1,7},{2,4},{3,5},{4,2},{5,3},{6,0},{7,1},{8,14},{9,15},{10,... | collective-permute-start | bytes 196616 | tf_op jit(solution)/shard_map/ppermute | solution.py:42
  23.7 0.0 slice-start.1
  23.7 0.9 %collective-permute-start.3 = (bf16[16,2048]{1,0:T(8,128)(2,1)S(1)}, bf16[16,2048]{1,0:T(8,128)(2,1)S(1)}, u32[]{:S(2)}, u32[]{:S(2)}) collective-permute-start(bf16[16,2048]{1,0:T(8,128)(2,1)S(1)} %get-tuple-element.17), channel_id=1, source_target_pairs={{0,4},{1,5},{2,6},{3,7},{4,0},{5,1},{6,2},{7,3},{8,12},{9,13},{10,... | collective-permute-start | bytes 196616 | tf_op jit(solution)/shard_map/ppermute | solution.py:42
  24.6 1.7 %crossed_near.3 = bf16[2,16,2048]{2,1,0:T(8,128)(2,1)S(1)} custom-call(bf16[8,320,512]{2,1,0:T(8,128)(2,1)S(1)} %pack.1.args_0_.packed_ref, s32[8,16,128]{2,1,0:T(8,128)S(1)} %all-to-all-done.coded_ref, bf16[2,16,2048]{2,1,0:T(8,128)(2,1)S(1)} %add.22.refs_0_), custom_call_target="tpu_custom_call" | custom-call | flops 11000000 | bytes 1 | tf_op jit(solution)/shard_map/crossed_near/pallas_call | solution.py:282
  26.3 0.0 collective-permute-done.1
  26.4 2.2 %collective-permute-start.4 = (bf16[16,2048]{1,0:T(8,128)(2,1)S(1)}, bf16[16,2048]{1,0:T(8,128)(2,1)S(1)}, u32[]{:S(2)}, u32[]{:S(2)}) collective-permute-start(bf16[16,2048]{1,0:T(8,128)(2,1)S(1)} %get-tuple-element.15), channel_id=1, source_target_pairs={{0,2},{1,3},{2,0},{3,1},{4,6},{5,7},{6,4},{7,5},{8,10},{9,11},{10,... | collective-permute-start | bytes 196616 | tf_op jit(solution)/shard_map/ppermute | solution.py:42
  28.6 1.8 %direct.5 = bf16[16,2048]{1,0:T(8,128)(2,1)S(1)} custom-call(bf16[8,320,512]{2,1,0:T(8,128)(2,1)S(1)} %pack.1.args_0_.packed_ref, s32[16,128]{1,0:T(8,128)S(1)} %get-tuple-element.10.args_1_.coded_ref, bf16[16,2048]{1,0:T(8,128)(2,1)S(1)} %direct.4.refs_0_, bf16[2,16,2048]{2,1,0:T(8,128)(2,1)S(1)} %add.23.refs_1_), custom_call_target="tpu_custom_call" | custom-call | flops 11000000 | bytes 1 | tf_op jit(solution)/shard_map/direct/pallas_call | solution.py:266
  30.5 0.0 collective-permute-done.2.refs_1_
  30.5 0.0 collective-permute-done.3.refs_1_
  30.5 0.4 collective-permute-done.4
  30.9 5.8 %all_gather.3.refs_0_ = bf16[64,2048]{1,0:T(8,128)(2,1)S(1)} all-gather(bf16[16,2048]{1,0:T(8,128)(2,1)S(1)} %multiply_convert_fusion), channel_id=1, replica_groups=mesh['ab'=4,'cd'=8] {'ab'}, dimensions={0}, use_global_device_ids=true | all-gather | bytes 327680 | tf_op jit(solution)/shard_map/all_gather | solution.py:315
  36.7 0.0 slice-done
  36.7 0.0 slice-done.1
  36.7 0.7 %ladder.3.refs_2_ = bf16[2,64,256]{2,1,0:T(8,128)(2,1)S(1)} custom-call(bf16[64,2048]{1,0:T(8,128)(2,1)S(1)} %all_gather.3.refs_0_, bf16[2048,2048]{1,0:T(8,128)(2,1)S(1)} %bitcast.27), custom_call_target="tpu_custom_call" | custom-call | flops 11000000 | bytes 1 | tf_op jit(solution)/shard_map/ladder/pallas_call | solution.py:321
  37.5 2.2 %collective-permute-start.5 = (bf16[2,64,256]{2,1,0:T(8,128)(2,1)S(1)}, bf16[2,64,256]{2,1,0:T(8,128)(2,1)S(1)}, u32[]{:S(2)}, u32[]{:S(2)}) collective-permute-start(bf16[2,64,256]{2,1,0:T(8,128)(2,1)S(1)} %ladder.3.refs_2_), channel_id=1, source_target_pairs={{0,6},{1,7},{2,4},{3,5},{4,2},{5,3},{6,0},{7,1},{8,14},{9,15},{10,... | collective-permute-start | bytes 196616 | tf_op jit(solution)/shard_map/ppermute | solution.py:42
  39.6 0.7 %ladder.4.refs_2_ = bf16[2,64,256]{2,1,0:T(8,128)(2,1)S(1)} custom-call(bf16[64,2048]{1,0:T(8,128)(2,1)S(1)} %all_gather.3.refs_0_, bf16[2048,2048]{1,0:T(8,128)(2,1)S(1)} %bitcast.27, bf16[2,64,256]{2,1,0:T(8,128)(2,1)S(1)} %ladder.3.refs_2_), custom_call_target="tpu_custom_call" | custom-call | flops 11000000 | bytes 1 | tf_op jit(solution)/shard_map/ladder/pallas_call | solution.py:321
  40.4 1.4 %collective-permute-start.6 = (bf16[2,64,256]{2,1,0:T(8,128)(2,1)S(1)}, bf16[2,64,256]{2,1,0:T(8,128)(2,1)S(1)}, u32[]{:S(2)}, u32[]{:S(2)}) collective-permute-start(bf16[2,64,256]{2,1,0:T(8,128)(2,1)S(1)} %ladder.4.refs_2_), channel_id=1, source_target_pairs={{0,4},{1,5},{2,6},{3,7},{4,0},{5,1},{6,2},{7,3},{8,12},{9,13},{10,... | collective-permute-start | bytes 196616 | tf_op jit(solution)/shard_map/ppermute | solution.py:42
  41.8 0.7 %ladder.5.refs_2_ = bf16[2,64,256]{2,1,0:T(8,128)(2,1)S(1)} custom-call(bf16[64,2048]{1,0:T(8,128)(2,1)S(1)} %all_gather.3.refs_0_, bf16[2048,2048]{1,0:T(8,128)(2,1)S(1)} %bitcast.27, bf16[2,64,256]{2,1,0:T(8,128)(2,1)S(1)} %ladder.4.refs_2_), custom_call_target="tpu_custom_call" | custom-call | flops 11000000 | bytes 1 | tf_op jit(solution)/shard_map/ladder/pallas_call | solution.py:321
  42.6 1.0 %collective-permute-start.7 = (bf16[2,64,256]{2,1,0:T(8,128)(2,1)S(1)}, bf16[2,64,256]{2,1,0:T(8,128)(2,1)S(1)}, u32[]{:S(2)}, u32[]{:S(2)}) collective-permute-start(bf16[2,64,256]{2,1,0:T(8,128)(2,1)S(1)} %ladder.5.refs_2_), channel_id=1, source_target_pairs={{0,2},{1,3},{2,0},{3,1},{4,6},{5,7},{6,4},{7,5},{8,10},{9,11},{10,... | collective-permute-start | bytes 196616 | tf_op jit(solution)/shard_map/ppermute | solution.py:42
  43.5 0.8 %ladder_own.1.refs_0_ = f32[2,64,256]{2,1,0:T(8,128)S(1)} custom-call(bf16[64,2048]{1,0:T(8,128)(2,1)S(1)} %all_gather.3.refs_0_, bf16[2048,2048]{1,0:T(8,128)(2,1)S(1)} %bitcast.27, bf16[2,64,256]{2,1,0:T(8,128)(2,1)S(1)} %ladder.5.refs_2_), custom_call_target="tpu_custom_call" | custom-call | flops 11000000 | bytes 1 | tf_op jit(solution)/shard_map/ladder_own/pallas_call | solution.py:321
  44.3 0.0 collective-permute-done.5.refs_1_
  44.3 3.3 %collective-permute-done.6.refs_1_ = bf16[2,64,256]{2,1,0:T(8,128)(2,1)S(1)} collective-permute-done((bf16[2,64,256]{2,1,0:T(8,128)(2,1)S(1)}, bf16[2,64,256]{2,1,0:T(8,128)(2,1)S(1)}, u32[]{:S(2)}, u32[]{:S(2)}) %collective-permute-start.6) | collective-permute-done | bytes 65568 | tf_op jit(solution)/shard_map/ppermute | solution.py:42
  47.7 0.4 collective-permute-done.7
  48.1 0.9 %collective-permute-start.8 = (bf16[64,256]{1,0:T(8,128)(2,1)S(1)}, bf16[64,256]{1,0:T(8,128)(2,1)S(1)}, u32[]{:S(2)}, u32[]{:S(2)}) collective-permute-start(bf16[64,256]{1,0:T(8,128)(2,1)S(1)} %fusion.3), channel_id=1, source_target_pairs={{0,1},{1,0},{2,3},{3,2},{4,5},{5,4},{6,7},{7,6},{8,9},{9,8},{10,11... | collective-permute-start | bytes 98312 | tf_op jit(solution)/shard_map/ppermute | solution.py:42
  49.0 3.1 %collective-permute-done.8 = bf16[64,256]{1,0:T(8,128)(2,1)S(1)} collective-permute-done((bf16[64,256]{1,0:T(8,128)(2,1)S(1)}, bf16[64,256]{1,0:T(8,128)(2,1)S(1)}, u32[]{:S(2)}, u32[]{:S(2)}) %collective-permute-start.8) | collective-permute-done | bytes 32800 | tf_op jit(solution)/shard_map/ppermute | solution.py:42
  52.1 0.6 %fusion.1 = bf16[64,256]{1,0:T(8,128)(2,1)} fusion(f32[2,64,256]{2,1,0:T(8,128)S(1)} %convert_add_fusion, bf16[64,256]{1,0:T(8,128)(2,1)S(1)} %collective-permute-done.8), kind=kLoop, calls=%fused_computation.5 | loop fusion | flops 49152 | bytes 131072 | tf_op jit(solution)/shard_map/convert_element_type | solution.py:338
  (16 shorter events, 0.3 us)
Async XLA Ops:
  1.4 14.2 %all-to-all-start = ((s32[8,16,128]{2,1,0:T(8,128)}), s32[8,16,128]{2,1,0:T(8,128)S(1)}, u32[]{:S(2)}, u32[]{:S(2)}) async-start(s32[8,16,128]{2,1,0:T(8,128)} %get-tuple-element.11), calls=%async_computation | async-start | bytes 131072 | tf_op jit(solution)/shard_map/all_to_all | solution.py:240
  12.0 4.9 %copy-start = (s32[2048]{0:T(1024)S(1)}, s32[2048]{0:T(1024)}, u32[]{:S(2)}) copy-start(s32[2048]{0:T(1024)} %param.7) | copy-start | bytes 24580
  12.0 4.9 %copy-start.1 = (s32[2048]{0:T(1024)S(1)}, s32[2048]{0:T(1024)}, u32[]{:S(2)}) copy-start(s32[2048]{0:T(1024)} %param.8) | copy-start | bytes 24580
  15.6 6.7 %collective-permute-start = (bf16[2,16,2048]{2,1,0:T(8,128)(2,1)S(1)}, bf16[2,16,2048]{2,1,0:T(8,128)(2,1)S(1)}, u32[]{:S(2)}, u32[]{:S(2)}) collective-permute-start(bf16[2,16,2048]{2,1,0:T(8,128)(2,1)S(1)} %crossed_far.2.refs_1_), channel_id=1, source_target_pairs={{0,1},{1,0},{2,3},{3,2},{4,5},{5,4},{6,7},{7,6},{8,9},{9,8},{10,11... | collective-permute-start | bytes 393224 | tf_op jit(solution)/shard_map/ppermute | solution.py:42
  19.6 17.1 %slice-start = ((s8[8388608]{0:T(1024)(128)(4,1)}), s8[4194304]{0:T(1024)(128)(4,1)S(1)}, s32[]{:S(2)}) async-start(s8[8388608]{0:T(1024)(128)(4,1)} %bitcast.26), calls=%async_computation.1 | async-start | bytes 8388608
  19.7 6.6 %collective-permute-start.1 = (bf16[2,16,2048]{2,1,0:T(8,128)(2,1)S(1)}, bf16[2,16,2048]{2,1,0:T(8,128)(2,1)S(1)}, u32[]{:S(2)}, u32[]{:S(2)}) collective-permute-start(bf16[2,16,2048]{2,1,0:T(8,128)(2,1)S(1)} %crossed_far.3.refs_0_), channel_id=1, source_target_pairs={{0,1},{1,0},{2,3},{3,2},{4,5},{5,4},{6,7},{7,6},{8,9},{9,8},{10,11... | collective-permute-start | bytes 393224 | tf_op jit(solution)/shard_map/ppermute | solution.py:42
  22.3 8.2 %collective-permute-start.2 = (bf16[16,2048]{1,0:T(8,128)(2,1)S(1)}, bf16[16,2048]{1,0:T(8,128)(2,1)S(1)}, u32[]{:S(2)}, u32[]{:S(2)}) collective-permute-start(bf16[16,2048]{1,0:T(8,128)(2,1)S(1)} %get-tuple-element.18), channel_id=1, source_target_pairs={{0,6},{1,7},{2,4},{3,5},{4,2},{5,3},{6,0},{7,1},{8,14},{9,15},{10,... | collective-permute-start | bytes 196616 | tf_op jit(solution)/shard_map/ppermute | solution.py:42
  23.7 13.0 %slice-start.1 = ((s8[8388608]{0:T(1024)(128)(4,1)}), s8[4194304]{0:T(1024)(128)(4,1)S(1)}, s32[]{:S(2)}) async-start(s8[8388608]{0:T(1024)(128)(4,1)} %bitcast.26), calls=%async_computation.2 | async-start | bytes 8388608
  23.7 6.8 %collective-permute-start.3 = (bf16[16,2048]{1,0:T(8,128)(2,1)S(1)}, bf16[16,2048]{1,0:T(8,128)(2,1)S(1)}, u32[]{:S(2)}, u32[]{:S(2)}) collective-permute-start(bf16[16,2048]{1,0:T(8,128)(2,1)S(1)} %get-tuple-element.17), channel_id=1, source_target_pairs={{0,4},{1,5},{2,6},{3,7},{4,0},{5,1},{6,2},{7,3},{8,12},{9,13},{10,... | collective-permute-start | bytes 196616 | tf_op jit(solution)/shard_map/ppermute | solution.py:42
  26.4 4.5 %collective-permute-start.4 = (bf16[16,2048]{1,0:T(8,128)(2,1)S(1)}, bf16[16,2048]{1,0:T(8,128)(2,1)S(1)}, u32[]{:S(2)}, u32[]{:S(2)}) collective-permute-start(bf16[16,2048]{1,0:T(8,128)(2,1)S(1)} %get-tuple-element.15), channel_id=1, source_target_pairs={{0,2},{1,3},{2,0},{3,1},{4,6},{5,7},{6,4},{7,5},{8,10},{9,11},{10,... | collective-permute-start | bytes 196616 | tf_op jit(solution)/shard_map/ppermute | solution.py:42
  37.5 6.8 %collective-permute-start.5 = (bf16[2,64,256]{2,1,0:T(8,128)(2,1)S(1)}, bf16[2,64,256]{2,1,0:T(8,128)(2,1)S(1)}, u32[]{:S(2)}, u32[]{:S(2)}) collective-permute-start(bf16[2,64,256]{2,1,0:T(8,128)(2,1)S(1)} %ladder.3.refs_2_), channel_id=1, source_target_pairs={{0,6},{1,7},{2,4},{3,5},{4,2},{5,3},{6,0},{7,1},{8,14},{9,15},{10,... | collective-permute-start | bytes 196616 | tf_op jit(solution)/shard_map/ppermute | solution.py:42
  40.4 7.3 %collective-permute-start.6 = (bf16[2,64,256]{2,1,0:T(8,128)(2,1)S(1)}, bf16[2,64,256]{2,1,0:T(8,128)(2,1)S(1)}, u32[]{:S(2)}, u32[]{:S(2)}) collective-permute-start(bf16[2,64,256]{2,1,0:T(8,128)(2,1)S(1)} %ladder.4.refs_2_), channel_id=1, source_target_pairs={{0,4},{1,5},{2,6},{3,7},{4,0},{5,1},{6,2},{7,3},{8,12},{9,13},{10,... | collective-permute-start | bytes 196616 | tf_op jit(solution)/shard_map/ppermute | solution.py:42
  42.6 5.5 %collective-permute-start.7 = (bf16[2,64,256]{2,1,0:T(8,128)(2,1)S(1)}, bf16[2,64,256]{2,1,0:T(8,128)(2,1)S(1)}, u32[]{:S(2)}, u32[]{:S(2)}) collective-permute-start(bf16[2,64,256]{2,1,0:T(8,128)(2,1)S(1)} %ladder.5.refs_2_), channel_id=1, source_target_pairs={{0,2},{1,3},{2,0},{3,1},{4,6},{5,7},{6,4},{7,5},{8,10},{9,11},{10,... | collective-permute-start | bytes 196616 | tf_op jit(solution)/shard_map/ppermute | solution.py:42
  48.1 4.0 %collective-permute-start.8 = (bf16[64,256]{1,0:T(8,128)(2,1)S(1)}, bf16[64,256]{1,0:T(8,128)(2,1)S(1)}, u32[]{:S(2)}, u32[]{:S(2)}) collective-permute-start(bf16[64,256]{1,0:T(8,128)(2,1)S(1)} %fusion.3), channel_id=1, source_target_pairs={{0,1},{1,0},{2,3},{3,2},{4,5},{5,4},{6,7},{7,6},{8,9},{9,8},{10,11... | collective-permute-start | bytes 98312 | tf_op jit(solution)/shard_map/ppermute | solution.py:42

commit v6 on v5

--- a/solution.py
+++ b/solution.py
@@ -133,12 +133,13 @@
                 crossed_ref[out] = jnp.zeros(crossed_ref.shape[1:], jnp.bfloat16)
 
 
-def direct_kernel(group, pairs, shift, orbits, slabs, lower, upper, packed_ref, coded_ref, *refs):
+def direct_kernel(group, pairs, shift, orbits, slabs, shares, packed_ref, coded_ref, *refs):
     old_ref, direct_ref = refs[0], refs[-1]
     me = lax.axis_index("cd")
-    upper_half = lax.div(me, jnp.int32(slabs // 2))
-    begin = me + lower[0] + upper_half * (upper[0] - lower[0])
-    end = lax.min(me + lower[1] + upper_half * (upper[1] - lower[1]), jnp.int32(slabs))
+    begin = end = jnp.int32(0)
+    for k, (low, high) in enumerate(shares):
+        begin = jnp.where(me == k, jnp.int32(low), begin)
+        end = jnp.where(me == k, jnp.int32(high), end)
     direct_ref[...] = jnp.zeros(direct_ref.shape, jnp.bfloat16) if old_ref is None else old_ref[...]
 
     @pl.when(begin < end)
@@ -197,7 +198,7 @@
     refs[-1][...] = total
 
 
-def add_up(total, parts):
+def add_up(total, parts, weight):
     for part in parts[:-1]:
         total = pl.pallas_call(
             add_kernel,
@@ -205,7 +206,7 @@
             in_specs=[VMEM] * 2,
             out_specs=VMEM,
             compiler_params=params(8),
-            cost_estimate=spent(0.5),
+            cost_estimate=spent(weight),
             name="add",
         )(total, part)
     return total + parts[-1].astype(jnp.float32)
@@ -262,9 +263,9 @@
     lookup_flops = 2 * packed_rows * DEPTH * columns
     lookup_bytes = packed_rows * DEPTH * 2 + columns * pairs * 2
 
-    def direct_for(lower, upper, *old):
+    def direct_for(part, *old):
         return pl.pallas_call(
-            functools.partial(direct_kernel if old else direct_first, group, pairs, shift, orbits, slabs, lower, upper),
+            functools.partial(direct_kernel if old else direct_first, group, pairs, shift, orbits, slabs, shares[part]),
             out_shape=jax.ShapeDtypeStruct((pairs, columns), jnp.bfloat16),
             in_specs=[VMEM] * 2 + [VMEM, ANY][: len(old)],
             out_specs=VMEM,
@@ -273,9 +274,15 @@
             name="direct",
         )(table, own_coded, *old)
 
-    half = max(slabs // 2, 1)
-    ends = [0, half - half // 4, 2 * (half - half // 4), slabs]
-    direct = direct_for((ends[0], ends[1]), (0, 0))
+    half = slabs // 2
+    first = [half - half // 4 if k < half else 0 for k in range(slabs)]
+    second = [first[0] if k == 0 else half // 2 if k == half else 0 for k in range(slabs)]
+    shares = [
+        [(k, k + first[k]) for k in range(slabs)],
+        [(k + first[k], k + first[k] + second[k]) for k in range(slabs)],
+        [(k + first[k] + second[k], slabs) for k in range(slabs)],
+    ]
+    direct = direct_for(0)
     coded, direct = lax.optimization_barrier((coded, direct))
 
     def crossed_for(masks, name, *after):
@@ -293,7 +300,7 @@
     arrived, last = [], ()
     for masks in pairs_of:
         if arrived:
-            direct = direct_for((ends[1], ends[2]), (0, 0), direct, *last)
+            direct = direct_for(1, direct, *last)
             last = (direct,)
         last = (crossed_for([mask + 1 for mask in masks], "crossed_far", *last),)
         arrived.append(swap(last[0], "cd", slabs, 1))
@@ -304,8 +311,8 @@
         for k in reversed(range(len(masks))):
             if masks[k]:
                 got.append(swap(merged[k], "cd", slabs, masks[k]))
-    direct = direct_for((ends[2], ends[3]), (0, slabs - half), direct, *last)
-    crossed = add_up(merged[0].astype(jnp.float32), got)
+    direct = direct_for(2, direct, *last)
+    crossed = add_up(merged[0].astype(jnp.float32), got, 0.5)
     live_cols, _ = lax.optimization_barrier((live_cols, merged))
     slots = jnp.arange(columns, dtype=jnp.int32)
     live = (slots < live_cols[0]).astype(jnp.float32)
@@ -328,14 +335,19 @@
             name=name,
         )(*gathered, pair_values, *after)
 
-    got, last = [], ()
-    for mask in reversed(near[1:]):
-        last = (ladder_for([mask, mask + 1], jnp.bfloat16, "ladder", *last),)
-        got.append(swap(last[0], "cd", slabs, mask))
-    total = ladder_for([0, 1], jnp.float32, "ladder_own", *last)
-    total = add_up(total, got)
-    total = total[0] + swap(total[1].astype(jnp.bfloat16), "cd", slabs, 1).astype(jnp.float32)
-    return total.astype(jnp.bfloat16)
+    arrived, last = [], ()
+    for masks in pairs_of:
+        last = (ladder_for([mask + 1 for mask in masks], jnp.bfloat16, "ladder_far", *last),)
+        arrived.append(swap(last[0], "cd", slabs, 1))
+    got = []
+    for masks, block in zip(pairs_of, arrived):
+        merged = ladder_for(masks, jnp.float32, "ladder_near", *last) + block.astype(jnp.float32)
+        sent = merged.astype(jnp.bfloat16)
+        last = (sent,)
+        for k in reversed(range(len(masks))):
+            if masks[k]:
+                got.append(swap(sent[k], "cd", slabs, masks[k]))
+    return add_up(merged[0], got, 0.02).astype(jnp.bfloat16)
 
 
 def solution(mesh):

time: 53.1 us -> 50.4 us (0.949)
  waiting for transfers between devices: 7.99 us -> 6.51 us
  starting transfers between devices: 21.1 us -> 19.9 us
    ppermute x9 -> x10, waiting for transfers between devices: 7.21 us -> 5.74 us  [swap(): return lax.ppermute(x, axis, [(i, i ^ mask) for i in range(size)])]
    ppermute x9 -> x10, starting transfers between devices: 13.9 us -> 12.6 us  [swap(): return lax.ppermute(x, axis, [(i, i ^ mask) for i in range(size)])]
  transfers between devices with their start and end apart: 10 -> 11, of which waited for: 5 -> 8; matrix products, arithmetic and copies ran while one was open for 0% -> 0% of each run, Pallas kernels for 27% -> 28%
where the time goes in v6:
time: 50.4 us; the launch traced here: 50 us
  starting transfers between devices  19.9 us (39%)
  Pallas kernels  16.2 us (32%)
  waiting for transfers between devices  6.51 us (13%)
  blocking collectives  5.79 us (11%)
  between operations  0.87 us (2%)
  other arithmetic  0.77 us (2%)
    ppermute x10, starting transfers between devices, swap(): return lax.ppermute(x, axis, [(i, i ^ mask) for i in range(size)])  12.6 us
    all_to_all x1, starting transfers between devices, on_device(): coded = lax.all_to_all(coded, 'cd', split_axis=0, concat_axis=0, tiled=True)  7.26 us
    pallas_call x3, Pallas kernels, direct_for(): pl.pallas_call(functools.partial(direct_kernel if old else direct_first,...  7.25 us
    all_gather x1, blocking collectives, on_device(): gathered = [lax.all_gather(packed[:pair_block], 'ab', axis=0, tiled=True)]  5.79 us
    ppermute x10, waiting for transfers between devices, swap(): return lax.ppermute(x, axis, [(i, i ^ mask) for i in range(size)])  5.74 us
    pallas_call x4, Pallas kernels, ladder_for(): pl.pallas_call(functools.partial(ladder_kernel, masks, len(gathered)), ou...  3 us
    pallas_call x1, Pallas kernels, on_device(): pl.pallas_call(functools.partial(pack_kernel, slabs, orbits, group, pairs...  2.73 us
    pallas_call x4, Pallas kernels, crossed_for(): pl.pallas_call(functools.partial(crossed_kernel, group, pairs, shift, orb...  1.78 us
  transfers between devices with their start and end apart: 11, of which 8 were waited for; matrix products, arithmetic and copies ran while one was open for 0% of the time, Pallas kernels for 28%

profile of v6, /device:TPU:0, one launch (start us, length us, event | category | flops | bytes accessed | tf_op | source)
XLA Modules:
  0.0 50.0 jit_solution(16334053078854090234)
XLA Ops:
  0.0 1.4 %code.1 = (s32[8,16,128]{2,1,0:T(8,128)}, s32[16,128]{1,0:T(8,128)S(1)}) custom-call(s32[16,128]{1,0:T(8,128)} %bitcast.29, s32[16,128]{1,0:T(8,128)} %bitcast.30), custom_call_target="tpu_custom_call" | custom-call | flops 22000001024 | bytes 1 | tf_op jit(solution)/shard_map/code/pallas_call | solution.py:228
  1.4 7.3 %all-to-all-start = ((s32[8,16,128]{2,1,0:T(8,128)}), s32[8,16,128]{2,1,0:T(8,128)S(1)}, u32[]{:S(2)}, u32[]{:S(2)}) async-start(s32[8,16,128]{2,1,0:T(8,128)} %get-tuple-element.11), calls=%async_computation | async-start | bytes 131072 | tf_op jit(solution)/shard_map/all_to_all | solution.py:241
  8.6 2.7 %pack.1.args_0_.packed_ref = bf16[8,320,512]{2,1,0:T(8,128)(2,1)S(1)} custom-call(bf16[1600,800]{1,0:T(8,128)(2,1)} %bitcast.28), custom_call_target="tpu_custom_call" | custom-call | bytes 5120000 | tf_op jit(solution)/shard_map/pack/pallas_call | solution.py:249
  12.0 0.0 copy-start
  12.0 0.0 copy-start.1
  12.0 2.7 %direct.3.refs_0_ = bf16[16,2048]{1,0:T(8,128)(2,1)S(1)} custom-call(bf16[8,320,512]{2,1,0:T(8,128)(2,1)S(1)} %pack.1.args_0_.packed_ref, s32[16,128]{1,0:T(8,128)S(1)} %get-tuple-element.10.args_1_.coded_ref), custom_call_target="tpu_custom_call" | custom-call | flops 2200000000 | bytes 1 | tf_op jit(solution)/shard_map/direct/pallas_call | solution.py:267
  14.8 0.8 %all-to-all-done.coded_ref = s32[8,16,128]{2,1,0:T(8,128)S(1)} async-done(((s32[8,16,128]{2,1,0:T(8,128)}), s32[8,16,128]{2,1,0:T(8,128)S(1)}, u32[]{:S(2)}, u32[]{:S(2)}) %all-to-all-start) | async-done | bytes 65568 | tf_op jit(solution)/shard_map/all_to_all | solution.py:241
  15.6 1.3 %collective-permute-start = (bf16[2,16,2048]{2,1,0:T(8,128)(2,1)S(1)}, bf16[2,16,2048]{2,1,0:T(8,128)(2,1)S(1)}, u32[]{:S(2)}, u32[]{:S(2)}) collective-permute-start(bf16[2,16,2048]{2,1,0:T(8,128)(2,1)S(1)} %crossed_far.2.refs_1_), channel_id=1, source_target_pairs={{0,1},{1,0},{2,3},{3,2},{4,5},{5,4},{6,7},{7,6},{8,9},{9,8},{10,11... | collective-permute-start | bytes 393224 | tf_op jit(solution)/shard_map/ppermute | solution.py:42
  16.9 0.0 copy-done
  16.9 0.0 copy-done.1
  16.9 2.7 %direct.4.refs_0_ = bf16[16,2048]{1,0:T(8,128)(2,1)S(1)} custom-call(bf16[8,320,512]{2,1,0:T(8,128)(2,1)S(1)} %pack.1.args_0_.packed_ref, s32[16,128]{1,0:T(8,128)S(1)} %get-tuple-element.10.args_1_.coded_ref, bf16[16,2048]{1,0:T(8,128)(2,1)S(1)} %direct.3.refs_0_, bf16[2,16,2048]{2,1,0:T(8,128)(2,1)S(1)} %crossed_far.2.refs_1_), custom_call_target="tpu_custom_call" | custom-call | flops 11000000 | bytes 1 | tf_op jit(solution)/shard_map/direct/pallas_call | solution.py:267
  19.6 0.0 slice-start
  19.7 0.1 collective-permute-start.1
  19.8 0.8 %collective-permute-done = bf16[2,16,2048]{2,1,0:T(8,128)(2,1)S(1)} collective-permute-done((bf16[2,16,2048]{2,1,0:T(8,128)(2,1)S(1)}, bf16[2,16,2048]{2,1,0:T(8,128)(2,1)S(1)}, u32[]{:S(2)}, u32[]{:S(2)}) %collective-permute-start) | collective-permute-done | bytes 131104 | tf_op jit(solution)/shard_map/ppermute | solution.py:42
  20.6 3.1 %collective-permute-start.2 = (bf16[16,2048]{1,0:T(8,128)(2,1)S(1)}, bf16[16,2048]{1,0:T(8,128)(2,1)S(1)}, u32[]{:S(2)}, u32[]{:S(2)}) collective-permute-start(bf16[16,2048]{1,0:T(8,128)(2,1)S(1)} %get-tuple-element.18), channel_id=1, source_target_pairs={{0,6},{1,7},{2,4},{3,5},{4,2},{5,3},{6,0},{7,1},{8,14},{9,15},{10,... | collective-permute-start | bytes 196616 | tf_op jit(solution)/shard_map/ppermute | solution.py:42
  23.7 0.0 slice-start.1
  23.7 0.3 collective-permute-start.3
  24.1 1.7 %crossed_near.3 = bf16[2,16,2048]{2,1,0:T(8,128)(2,1)S(1)} custom-call(bf16[8,320,512]{2,1,0:T(8,128)(2,1)S(1)} %pack.1.args_0_.packed_ref, s32[8,16,128]{2,1,0:T(8,128)S(1)} %all-to-all-done.coded_ref, bf16[2,16,2048]{2,1,0:T(8,128)(2,1)S(1)} %add.25.refs_0_), custom_call_target="tpu_custom_call" | custom-call | flops 11000000 | bytes 1 | tf_op jit(solution)/shard_map/crossed_near/pallas_call | solution.py:289
  25.8 0.0 collective-permute-done.1
  25.9 1.1 %collective-permute-start.4 = (bf16[16,2048]{1,0:T(8,128)(2,1)S(1)}, bf16[16,2048]{1,0:T(8,128)(2,1)S(1)}, u32[]{:S(2)}, u32[]{:S(2)}) collective-permute-start(bf16[16,2048]{1,0:T(8,128)(2,1)S(1)} %get-tuple-element.15), channel_id=1, source_target_pairs={{0,2},{1,3},{2,0},{3,1},{4,6},{5,7},{6,4},{7,5},{8,10},{9,11},{10,... | collective-permute-start | bytes 196616 | tf_op jit(solution)/shard_map/ppermute | solution.py:42
  27.0 1.8 %direct.5 = bf16[16,2048]{1,0:T(8,128)(2,1)S(1)} custom-call(bf16[8,320,512]{2,1,0:T(8,128)(2,1)S(1)} %pack.1.args_0_.packed_ref, s32[16,128]{1,0:T(8,128)S(1)} %get-tuple-element.10.args_1_.coded_ref, bf16[16,2048]{1,0:T(8,128)(2,1)S(1)} %direct.4.refs_0_, bf16[2,16,2048]{2,1,0:T(8,128)(2,1)S(1)} %add.26.refs_1_), custom_call_target="tpu_custom_call" | custom-call | flops 11000000 | bytes 1 | tf_op jit(solution)/shard_map/direct/pallas_call | solution.py:267
  28.8 0.0 collective-permute-done.2.refs_1_
  28.8 0.6 %collective-permute-done.3.refs_1_ = bf16[16,2048]{1,0:T(8,128)(2,1)S(1)} collective-permute-done((bf16[16,2048]{1,0:T(8,128)(2,1)S(1)}, bf16[16,2048]{1,0:T(8,128)(2,1)S(1)}, u32[]{:S(2)}, u32[]{:S(2)}) %collective-permute-start.3) | collective-permute-done | bytes 65568 | tf_op jit(solution)/shard_map/ppermute | solution.py:42
  29.4 0.8 %collective-permute-done.4 = bf16[16,2048]{1,0:T(8,128)(2,1)S(1)} collective-permute-done((bf16[16,2048]{1,0:T(8,128)(2,1)S(1)}, bf16[16,2048]{1,0:T(8,128)(2,1)S(1)}, u32[]{:S(2)}, u32[]{:S(2)}) %collective-permute-start.4) | collective-permute-done | bytes 65568 | tf_op jit(solution)/shard_map/ppermute | solution.py:42
  30.2 5.8 %all_gather.3.refs_0_ = bf16[64,2048]{1,0:T(8,128)(2,1)S(1)} all-gather(bf16[16,2048]{1,0:T(8,128)(2,1)S(1)} %multiply_convert_fusion), channel_id=1, replica_groups=mesh['ab'=4,'cd'=8] {'ab'}, dimensions={0}, use_global_device_ids=true | all-gather | bytes 327680 | tf_op jit(solution)/shard_map/all_gather | solution.py:322
  36.0 0.0 slice-done
  36.0 0.0 slice-done.1
  36.0 0.7 %ladder_far.2.refs_2_ = bf16[2,64,256]{2,1,0:T(8,128)(2,1)S(1)} custom-call(bf16[64,2048]{1,0:T(8,128)(2,1)S(1)} %all_gather.3.refs_0_, bf16[2048,2048]{1,0:T(8,128)(2,1)S(1)} %bitcast.27), custom_call_target="tpu_custom_call" | custom-call | flops 11000000 | bytes 1 | tf_op jit(solution)/shard_map/ladder_far/pallas_call | solution.py:328
  36.8 2.0 %collective-permute-start.5 = (bf16[2,64,256]{2,1,0:T(8,128)(2,1)S(1)}, bf16[2,64,256]{2,1,0:T(8,128)(2,1)S(1)}, u32[]{:S(2)}, u32[]{:S(2)}) collective-permute-start(bf16[2,64,256]{2,1,0:T(8,128)(2,1)S(1)} %ladder_far.2.refs_2_), channel_id=1, source_target_pairs={{0,1},{1,0},{2,3},{3,2},{4,5},{5,4},{6,7},{7,6},{8,9},{9,8},{10,11... | collective-permute-start | bytes 196616 | tf_op jit(solution)/shard_map/ppermute | solution.py:42
  38.8 0.7 %ladder_far.3.refs_2_ = bf16[2,64,256]{2,1,0:T(8,128)(2,1)S(1)} custom-call(bf16[64,2048]{1,0:T(8,128)(2,1)S(1)} %all_gather.3.refs_0_, bf16[2048,2048]{1,0:T(8,128)(2,1)S(1)} %bitcast.27, bf16[2,64,256]{2,1,0:T(8,128)(2,1)S(1)} %ladder_far.2.refs_2_), custom_call_target="tpu_custom_call" | custom-call | flops 11000000 | bytes 1 | tf_op jit(solution)/shard_map/ladder_far/pallas_call | solution.py:328
  39.6 0.1 collective-permute-start.6
  39.7 0.8 %ladder_near.2 = f32[2,64,256]{2,1,0:T(8,128)S(1)} custom-call(bf16[64,2048]{1,0:T(8,128)(2,1)S(1)} %all_gather.3.refs_0_, bf16[2048,2048]{1,0:T(8,128)(2,1)S(1)} %bitcast.27, bf16[2,64,256]{2,1,0:T(8,128)(2,1)S(1)} %ladder_far.3.refs_2_), custom_call_target="tpu_custom_call" | custom-call | flops 11000000 | bytes 1 | tf_op jit(solution)/shard_map/ladder_near/pallas_call | solution.py:328
  40.4 1.0 %collective-permute-done.5 = bf16[2,64,256]{2,1,0:T(8,128)(2,1)S(1)} collective-permute-done((bf16[2,64,256]{2,1,0:T(8,128)(2,1)S(1)}, bf16[2,64,256]{2,1,0:T(8,128)(2,1)S(1)}, u32[]{:S(2)}, u32[]{:S(2)}) %collective-permute-start.5) | collective-permute-done | bytes 65568 | tf_op jit(solution)/shard_map/ppermute | solution.py:42
  41.4 2.8 %collective-permute-start.7 = (bf16[64,256]{1,0:T(8,128)(2,1)S(1)}, bf16[64,256]{1,0:T(8,128)(2,1)S(1)}, u32[]{:S(2)}, u32[]{:S(2)}) collective-permute-start(bf16[64,256]{1,0:T(8,128)(2,1)S(1)} %get-tuple-element.20), channel_id=1, source_target_pairs={{0,6},{1,7},{2,4},{3,5},{4,2},{5,3},{6,0},{7,1},{8,14},{9,15},{10,... | collective-permute-start | bytes 98312 | tf_op jit(solution)/shard_map/ppermute | solution.py:42
  44.3 0.0 collective-permute-start.8
  44.3 0.8 %ladder_near.3 = f32[2,64,256]{2,1,0:T(8,128)S(1)} custom-call(bf16[64,2048]{1,0:T(8,128)(2,1)S(1)} %all_gather.3.refs_0_, bf16[2048,2048]{1,0:T(8,128)(2,1)S(1)} %bitcast.27, bf16[2,64,256]{2,1,0:T(8,128)(2,1)S(1)} %add_convert_fusion.refs_2_), custom_call_target="tpu_custom_call" | custom-call | flops 11000000 | bytes 1 | tf_op jit(solution)/shard_map/ladder_near/pallas_call | solution.py:328
  45.0 0.0 collective-permute-done.6
  45.1 1.7 %collective-permute-start.9 = (bf16[64,256]{1,0:T(8,128)(2,1)S(1)}, bf16[64,256]{1,0:T(8,128)(2,1)S(1)}, u32[]{:S(2)}, u32[]{:S(2)}) collective-permute-start(bf16[64,256]{1,0:T(8,128)(2,1)S(1)} %fusion.1), channel_id=1, source_target_pairs={{0,2},{1,3},{2,0},{3,1},{4,6},{5,7},{6,4},{7,5},{8,10},{9,11},{10,... | collective-permute-start | bytes 98312 | tf_op jit(solution)/shard_map/ppermute | solution.py:42
  46.8 0.6 %collective-permute-done.7.refs_1_ = bf16[64,256]{1,0:T(8,128)(2,1)S(1)} collective-permute-done((bf16[64,256]{1,0:T(8,128)(2,1)S(1)}, bf16[64,256]{1,0:T(8,128)(2,1)S(1)}, u32[]{:S(2)}, u32[]{:S(2)}) %collective-permute-start.7) | collective-permute-done | bytes 32800 | tf_op jit(solution)/shard_map/ppermute | solution.py:42
  47.4 1.8 %collective-permute-done.8.refs_1_ = bf16[64,256]{1,0:T(8,128)(2,1)S(1)} collective-permute-done((bf16[64,256]{1,0:T(8,128)(2,1)S(1)}, bf16[64,256]{1,0:T(8,128)(2,1)S(1)}, u32[]{:S(2)}, u32[]{:S(2)}) %collective-permute-start.8) | collective-permute-done | bytes 32800 | tf_op jit(solution)/shard_map/ppermute | solution.py:42
  49.2 0.2 collective-permute-done.9
  49.4 0.6 %add_convert_fusion.1 = bf16[64,256]{1,0:T(8,128)(2,1)} fusion(f32[64,256]{1,0:T(8,128)S(1)} %add.40, bf16[64,256]{1,0:T(8,128)(2,1)S(1)} %collective-permute-done.9), kind=kLoop, calls=%fused_computation.10 | loop fusion | flops 49152 | bytes 131072 | tf_op jit(solution)/shard_map/convert_element_type | solution.py:350
  (19 shorter events, 0.3 us)
Async XLA Ops:
  1.4 14.2 %all-to-all-start = ((s32[8,16,128]{2,1,0:T(8,128)}), s32[8,16,128]{2,1,0:T(8,128)S(1)}, u32[]{:S(2)}, u32[]{:S(2)}) async-start(s32[8,16,128]{2,1,0:T(8,128)} %get-tuple-element.11), calls=%async_computation | async-start | bytes 131072 | tf_op jit(solution)/shard_map/all_to_all | solution.py:241
  12.0 4.9 %copy-start = (s32[2048]{0:T(1024)S(1)}, s32[2048]{0:T(1024)}, u32[]{:S(2)}) copy-start(s32[2048]{0:T(1024)} %param.7) | copy-start | bytes 24580
  12.0 4.9 %copy-start.1 = (s32[2048]{0:T(1024)S(1)}, s32[2048]{0:T(1024)}, u32[]{:S(2)}) copy-start(s32[2048]{0:T(1024)} %param.8) | copy-start | bytes 24580
  15.6 5.0 %collective-permute-start = (bf16[2,16,2048]{2,1,0:T(8,128)(2,1)S(1)}, bf16[2,16,2048]{2,1,0:T(8,128)(2,1)S(1)}, u32[]{:S(2)}, u32[]{:S(2)}) collective-permute-start(bf16[2,16,2048]{2,1,0:T(8,128)(2,1)S(1)} %crossed_far.2.refs_1_), channel_id=1, source_target_pairs={{0,1},{1,0},{2,3},{3,2},{4,5},{5,4},{6,7},{7,6},{8,9},{9,8},{10,11... | collective-permute-start | bytes 393224 | tf_op jit(solution)/shard_map/ppermute | solution.py:42
  19.6 16.4 %slice-start = ((s8[8388608]{0:T(1024)(128)(4,1)}), s8[4194304]{0:T(1024)(128)(4,1)S(1)}, s32[]{:S(2)}) async-start(s8[8388608]{0:T(1024)(128)(4,1)} %bitcast.26), calls=%async_computation.1 | async-start | bytes 8388608
  19.7 6.1 %collective-permute-start.1 = (bf16[2,16,2048]{2,1,0:T(8,128)(2,1)S(1)}, bf16[2,16,2048]{2,1,0:T(8,128)(2,1)S(1)}, u32[]{:S(2)}, u32[]{:S(2)}) collective-permute-start(bf16[2,16,2048]{2,1,0:T(8,128)(2,1)S(1)} %crossed_far.3.refs_0_), channel_id=1, source_target_pairs={{0,1},{1,0},{2,3},{3,2},{4,5},{5,4},{6,7},{7,6},{8,9},{9,8},{10,11... | collective-permute-start | bytes 393224 | tf_op jit(solution)/shard_map/ppermute | solution.py:42
  20.6 8.2 %collective-permute-start.2 = (bf16[16,2048]{1,0:T(8,128)(2,1)S(1)}, bf16[16,2048]{1,0:T(8,128)(2,1)S(1)}, u32[]{:S(2)}, u32[]{:S(2)}) collective-permute-start(bf16[16,2048]{1,0:T(8,128)(2,1)S(1)} %get-tuple-element.18), channel_id=1, source_target_pairs={{0,6},{1,7},{2,4},{3,5},{4,2},{5,3},{6,0},{7,1},{8,14},{9,15},{10,... | collective-permute-start | bytes 196616 | tf_op jit(solution)/shard_map/ppermute | solution.py:42
  23.7 12.3 %slice-start.1 = ((s8[8388608]{0:T(1024)(128)(4,1)}), s8[4194304]{0:T(1024)(128)(4,1)S(1)}, s32[]{:S(2)}) async-start(s8[8388608]{0:T(1024)(128)(4,1)} %bitcast.26), calls=%async_computation.2 | async-start | bytes 8388608
  23.7 5.7 %collective-permute-start.3 = (bf16[16,2048]{1,0:T(8,128)(2,1)S(1)}, bf16[16,2048]{1,0:T(8,128)(2,1)S(1)}, u32[]{:S(2)}, u32[]{:S(2)}) collective-permute-start(bf16[16,2048]{1,0:T(8,128)(2,1)S(1)} %get-tuple-element.17), channel_id=1, source_target_pairs={{0,4},{1,5},{2,6},{3,7},{4,0},{5,1},{6,2},{7,3},{8,12},{9,13},{10,... | collective-permute-start | bytes 196616 | tf_op jit(solution)/shard_map/ppermute | solution.py:42
  25.9 4.3 %collective-permute-start.4 = (bf16[16,2048]{1,0:T(8,128)(2,1)S(1)}, bf16[16,2048]{1,0:T(8,128)(2,1)S(1)}, u32[]{:S(2)}, u32[]{:S(2)}) collective-permute-start(bf16[16,2048]{1,0:T(8,128)(2,1)S(1)} %get-tuple-element.15), channel_id=1, source_target_pairs={{0,2},{1,3},{2,0},{3,1},{4,6},{5,7},{6,4},{7,5},{8,10},{9,11},{10,... | collective-permute-start | bytes 196616 | tf_op jit(solution)/shard_map/ppermute | solution.py:42
  36.8 4.6 %collective-permute-start.5 = (bf16[2,64,256]{2,1,0:T(8,128)(2,1)S(1)}, bf16[2,64,256]{2,1,0:T(8,128)(2,1)S(1)}, u32[]{:S(2)}, u32[]{:S(2)}) collective-permute-start(bf16[2,64,256]{2,1,0:T(8,128)(2,1)S(1)} %ladder_far.2.refs_2_), channel_id=1, source_target_pairs={{0,1},{1,0},{2,3},{3,2},{4,5},{5,4},{6,7},{7,6},{8,9},{9,8},{10,11... | collective-permute-start | bytes 196616 | tf_op jit(solution)/shard_map/ppermute | solution.py:42
  39.6 5.5 %collective-permute-start.6 = (bf16[2,64,256]{2,1,0:T(8,128)(2,1)S(1)}, bf16[2,64,256]{2,1,0:T(8,128)(2,1)S(1)}, u32[]{:S(2)}, u32[]{:S(2)}) collective-permute-start(bf16[2,64,256]{2,1,0:T(8,128)(2,1)S(1)} %ladder_far.3.refs_2_), channel_id=1, source_target_pairs={{0,1},{1,0},{2,3},{3,2},{4,5},{5,4},{6,7},{7,6},{8,9},{9,8},{10,11... | collective-permute-start | bytes 196616 | tf_op jit(solution)/shard_map/ppermute | solution.py:42
  41.4 6.0 %collective-permute-start.7 = (bf16[64,256]{1,0:T(8,128)(2,1)S(1)}, bf16[64,256]{1,0:T(8,128)(2,1)S(1)}, u32[]{:S(2)}, u32[]{:S(2)}) collective-permute-start(bf16[64,256]{1,0:T(8,128)(2,1)S(1)} %get-tuple-element.20), channel_id=1, source_target_pairs={{0,6},{1,7},{2,4},{3,5},{4,2},{5,3},{6,0},{7,1},{8,14},{9,15},{10,... | collective-permute-start | bytes 98312 | tf_op jit(solution)/shard_map/ppermute | solution.py:42
  44.3 4.9 %collective-permute-start.8 = (bf16[64,256]{1,0:T(8,128)(2,1)S(1)}, bf16[64,256]{1,0:T(8,128)(2,1)S(1)}, u32[]{:S(2)}, u32[]{:S(2)}) collective-permute-start(bf16[64,256]{1,0:T(8,128)(2,1)S(1)} %get-tuple-element.19), channel_id=1, source_target_pairs={{0,4},{1,5},{2,6},{3,7},{4,0},{5,1},{6,2},{7,3},{8,12},{9,13},{10,... | collective-permute-start | bytes 98312 | tf_op jit(solution)/shard_map/ppermute | solution.py:42
  45.1 4.3 %collective-permute-start.9 = (bf16[64,256]{1,0:T(8,128)(2,1)S(1)}, bf16[64,256]{1,0:T(8,128)(2,1)S(1)}, u32[]{:S(2)}, u32[]{:S(2)}) collective-permute-start(bf16[64,256]{1,0:T(8,128)(2,1)S(1)} %fusion.1), channel_id=1, source_target_pairs={{0,2},{1,3},{2,0},{3,1},{4,6},{5,7},{6,4},{7,5},{8,10},{9,11},{10,... | collective-permute-start | bytes 98312 | tf_op jit(solution)/shard_map/ppermute | solution.py:42

commit v7 on v6

--- a/solution.py
+++ b/solution.py
@@ -276,7 +276,8 @@
 
     half = slabs // 2
     first = [half - half // 4 if k < half else 0 for k in range(slabs)]
-    second = [first[0] if k == 0 else half // 2 if k == half else 0 for k in range(slabs)]
+    early = {0: first[0], 1: first[0] // 2, half: half // 2}
+    second = [early.get(k, 0) for k in range(slabs)]
     shares = [
         [(k, k + first[k]) for k in range(slabs)],
         [(k + first[k], k + first[k] + second[k]) for k in range(slabs)],
@@ -341,9 +342,10 @@
         arrived.append(swap(last[0], "cd", slabs, 1))
     got = []
     for masks, block in zip(pairs_of, arrived):
-        merged = ladder_for(masks, jnp.float32, "ladder_near", *last) + block.astype(jnp.float32)
+        own = ladder_for(masks, jnp.float32, "ladder_near", *last)
+        last = (own,)
+        merged = own + block.astype(jnp.float32)
         sent = merged.astype(jnp.bfloat16)
-        last = (sent,)
         for k in reversed(range(len(masks))):
             if masks[k]:
                 got.append(swap(sent[k], "cd", slabs, masks[k]))

time: 50.4 us -> 50.2 us (level)
  waiting for transfers between devices: 6.51 us -> 5.69 us
  starting transfers between devices: 19.9 us -> 20.5 us
    ppermute x10, waiting for transfers between devices: 5.74 us -> 4.91 us  [swap(): return lax.ppermute(x, axis, [(i, i ^ mask) for i in range(size)])]
    ppermute x10, starting transfers between devices: 12.6 us -> 13.3 us  [swap(): return lax.ppermute(x, axis, [(i, i ^ mask) for i in range(size)])]
  transfers between devices with their start and end apart: 11 -> 11, of which waited for: 8 -> 7; matrix products, arithmetic and copies ran while one was open for 0% -> 0% of each run, Pallas kernels for 28% -> 28%
where the time goes in v7:
time: 50.2 us; the launch traced here: 49.9 us
  starting transfers between devices  20.5 us (41%)
  Pallas kernels  16.2 us (32%)
  blocking collectives  5.79 us (12%)
  waiting for transfers between devices  5.69 us (11%)
  between operations  0.86 us (2%)
  other arithmetic  0.77 us (2%)
    ppermute x10, starting transfers between devices, swap(): return lax.ppermute(x, axis, [(i, i ^ mask) for i in range(size)])  13.3 us
    all_to_all x1, starting transfers between devices, on_device(): coded = lax.all_to_all(coded, 'cd', split_axis=0, concat_axis=0, tiled=True)  7.26 us
    pallas_call x3, Pallas kernels, direct_for(): pl.pallas_call(functools.partial(direct_kernel if old else direct_first,...  7.25 us
    all_gather x1, blocking collectives, on_device(): gathered = [lax.all_gather(packed[:pair_block], 'ab', axis=0, tiled=True)]  5.79 us
    ppermute x10, waiting for transfers between devices, swap(): return lax.ppermute(x, axis, [(i, i ^ mask) for i in range(size)])  4.91 us
    pallas_call x4, Pallas kernels, ladder_for(): pl.pallas_call(functools.partial(ladder_kernel, masks, len(gathered)), ou...  3.02 us
    pallas_call x1, Pallas kernels, on_device(): pl.pallas_call(functools.partial(pack_kernel, slabs, orbits, group, pairs...  2.73 us
    pallas_call x4, Pallas kernels, crossed_for(): pl.pallas_call(functools.partial(crossed_kernel, group, pairs, shift, orb...  1.77 us
  transfers between devices with their start and end apart: 11, of which 7 were waited for; matrix products, arithmetic and copies ran while one was open for 0% of the time, Pallas kernels for 28%

profile of v7, /device:TPU:0, one launch (start us, length us, event | category | flops | bytes accessed | tf_op | source)
XLA Modules:
  0.0 49.9 jit_solution(12013914533763501667)
XLA Ops:
  0.0 1.4 %code.1 = (s32[8,16,128]{2,1,0:T(8,128)}, s32[16,128]{1,0:T(8,128)S(1)}) custom-call(s32[16,128]{1,0:T(8,128)} %bitcast.29, s32[16,128]{1,0:T(8,128)} %bitcast.30), custom_call_target="tpu_custom_call" | custom-call | flops 22000001024 | bytes 1 | tf_op jit(solution)/shard_map/code/pallas_call | solution.py:228
  1.4 7.3 %all-to-all-start = ((s32[8,16,128]{2,1,0:T(8,128)}), s32[8,16,128]{2,1,0:T(8,128)S(1)}, u32[]{:S(2)}, u32[]{:S(2)}) async-start(s32[8,16,128]{2,1,0:T(8,128)} %get-tuple-element.11), calls=%async_computation | async-start | bytes 131072 | tf_op jit(solution)/shard_map/all_to_all | solution.py:241
  8.6 2.7 %pack.1.args_0_.packed_ref = bf16[8,320,512]{2,1,0:T(8,128)(2,1)S(1)} custom-call(bf16[1600,800]{1,0:T(8,128)(2,1)} %bitcast.28), custom_call_target="tpu_custom_call" | custom-call | bytes 5120000 | tf_op jit(solution)/shard_map/pack/pallas_call | solution.py:249
  12.0 0.0 copy-start
  12.0 0.0 copy-start.1
  12.0 2.7 %direct.3.refs_0_ = bf16[16,2048]{1,0:T(8,128)(2,1)S(1)} custom-call(bf16[8,320,512]{2,1,0:T(8,128)(2,1)S(1)} %pack.1.args_0_.packed_ref, s32[16,128]{1,0:T(8,128)S(1)} %get-tuple-element.10.args_1_.coded_ref), custom_call_target="tpu_custom_call" | custom-call | flops 2200000000 | bytes 1 | tf_op jit(solution)/shard_map/direct/pallas_call | solution.py:267
  14.8 0.8 %all-to-all-done.coded_ref = s32[8,16,128]{2,1,0:T(8,128)S(1)} async-done(((s32[8,16,128]{2,1,0:T(8,128)}), s32[8,16,128]{2,1,0:T(8,128)S(1)}, u32[]{:S(2)}, u32[]{:S(2)}) %all-to-all-start) | async-done | bytes 65568 | tf_op jit(solution)/shard_map/all_to_all | solution.py:241
  15.6 1.3 %collective-permute-start = (bf16[2,16,2048]{2,1,0:T(8,128)(2,1)S(1)}, bf16[2,16,2048]{2,1,0:T(8,128)(2,1)S(1)}, u32[]{:S(2)}, u32[]{:S(2)}) collective-permute-start(bf16[2,16,2048]{2,1,0:T(8,128)(2,1)S(1)} %crossed_far.2.refs_1_), channel_id=1, source_target_pairs={{0,1},{1,0},{2,3},{3,2},{4,5},{5,4},{6,7},{7,6},{8,9},{9,8},{10,11... | collective-permute-start | bytes 393224 | tf_op jit(solution)/shard_map/ppermute | solution.py:42
  16.9 0.0 copy-done
  16.9 0.0 copy-done.1
  16.9 2.7 %direct.4.refs_0_ = bf16[16,2048]{1,0:T(8,128)(2,1)S(1)} custom-call(bf16[8,320,512]{2,1,0:T(8,128)(2,1)S(1)} %pack.1.args_0_.packed_ref, s32[16,128]{1,0:T(8,128)S(1)} %get-tuple-element.10.args_1_.coded_ref, bf16[16,2048]{1,0:T(8,128)(2,1)S(1)} %direct.3.refs_0_, bf16[2,16,2048]{2,1,0:T(8,128)(2,1)S(1)} %crossed_far.2.refs_1_), custom_call_target="tpu_custom_call" | custom-call | flops 11000000 | bytes 1 | tf_op jit(solution)/shard_map/direct/pallas_call | solution.py:267
  19.6 0.0 slice-start
  19.7 0.7 %collective-permute-start.1 = (bf16[2,16,2048]{2,1,0:T(8,128)(2,1)S(1)}, bf16[2,16,2048]{2,1,0:T(8,128)(2,1)S(1)}, u32[]{:S(2)}, u32[]{:S(2)}) collective-permute-start(bf16[2,16,2048]{2,1,0:T(8,128)(2,1)S(1)} %crossed_far.3.refs_0_), channel_id=1, source_target_pairs={{0,1},{1,0},{2,3},{3,2},{4,5},{5,4},{6,7},{7,6},{8,9},{9,8},{10,11... | collective-permute-start | bytes 393224 | tf_op jit(solution)/shard_map/ppermute | solution.py:42
  20.4 0.1 collective-permute-done
  20.6 3.1 %collective-permute-start.2 = (bf16[16,2048]{1,0:T(8,128)(2,1)S(1)}, bf16[16,2048]{1,0:T(8,128)(2,1)S(1)}, u32[]{:S(2)}, u32[]{:S(2)}) collective-permute-start(bf16[16,2048]{1,0:T(8,128)(2,1)S(1)} %get-tuple-element.18), channel_id=1, source_target_pairs={{0,6},{1,7},{2,4},{3,5},{4,2},{5,3},{6,0},{7,1},{8,14},{9,15},{10,... | collective-permute-start | bytes 196616 | tf_op jit(solution)/shard_map/ppermute | solution.py:42
  23.7 0.0 slice-start.1
  23.7 0.3 collective-permute-start.3
  24.1 1.7 %crossed_near.3 = bf16[2,16,2048]{2,1,0:T(8,128)(2,1)S(1)} custom-call(bf16[8,320,512]{2,1,0:T(8,128)(2,1)S(1)} %pack.1.args_0_.packed_ref, s32[8,16,128]{2,1,0:T(8,128)S(1)} %all-to-all-done.coded_ref, bf16[2,16,2048]{2,1,0:T(8,128)(2,1)S(1)} %add.25.refs_0_), custom_call_target="tpu_custom_call" | custom-call | flops 11000000 | bytes 1 | tf_op jit(solution)/shard_map/crossed_near/pallas_call | solution.py:290
  25.8 0.0 collective-permute-done.1
  25.9 1.1 %collective-permute-start.4 = (bf16[16,2048]{1,0:T(8,128)(2,1)S(1)}, bf16[16,2048]{1,0:T(8,128)(2,1)S(1)}, u32[]{:S(2)}, u32[]{:S(2)}) collective-permute-start(bf16[16,2048]{1,0:T(8,128)(2,1)S(1)} %get-tuple-element.15), channel_id=1, source_target_pairs={{0,2},{1,3},{2,0},{3,1},{4,6},{5,7},{6,4},{7,5},{8,10},{9,11},{10,... | collective-permute-start | bytes 196616 | tf_op jit(solution)/shard_map/ppermute | solution.py:42
  27.0 1.8 %direct.5 = bf16[16,2048]{1,0:T(8,128)(2,1)S(1)} custom-call(bf16[8,320,512]{2,1,0:T(8,128)(2,1)S(1)} %pack.1.args_0_.packed_ref, s32[16,128]{1,0:T(8,128)S(1)} %get-tuple-element.10.args_1_.coded_ref, bf16[16,2048]{1,0:T(8,128)(2,1)S(1)} %direct.4.refs_0_, bf16[2,16,2048]{2,1,0:T(8,128)(2,1)S(1)} %add.26.refs_1_), custom_call_target="tpu_custom_call" | custom-call | flops 11000000 | bytes 1 | tf_op jit(solution)/shard_map/direct/pallas_call | solution.py:267
  28.8 0.0 collective-permute-done.2.refs_1_
  28.8 0.6 %collective-permute-done.3.refs_1_ = bf16[16,2048]{1,0:T(8,128)(2,1)S(1)} collective-permute-done((bf16[16,2048]{1,0:T(8,128)(2,1)S(1)}, bf16[16,2048]{1,0:T(8,128)(2,1)S(1)}, u32[]{:S(2)}, u32[]{:S(2)}) %collective-permute-start.3) | collective-permute-done | bytes 65568 | tf_op jit(solution)/shard_map/ppermute | solution.py:42
  29.4 0.8 %collective-permute-done.4 = bf16[16,2048]{1,0:T(8,128)(2,1)S(1)} collective-permute-done((bf16[16,2048]{1,0:T(8,128)(2,1)S(1)}, bf16[16,2048]{1,0:T(8,128)(2,1)S(1)}, u32[]{:S(2)}, u32[]{:S(2)}) %collective-permute-start.4) | collective-permute-done | bytes 65568 | tf_op jit(solution)/shard_map/ppermute | solution.py:42
  30.2 5.8 %all_gather.3.refs_0_ = bf16[64,2048]{1,0:T(8,128)(2,1)S(1)} all-gather(bf16[16,2048]{1,0:T(8,128)(2,1)S(1)} %multiply_convert_fusion), channel_id=1, replica_groups=mesh['ab'=4,'cd'=8] {'ab'}, dimensions={0}, use_global_device_ids=true | all-gather | bytes 327680 | tf_op jit(solution)/shard_map/all_gather | solution.py:323
  36.0 0.0 slice-done
  36.0 0.0 slice-done.1
  36.0 0.7 %ladder_far.2.refs_2_ = bf16[2,64,256]{2,1,0:T(8,128)(2,1)S(1)} custom-call(bf16[64,2048]{1,0:T(8,128)(2,1)S(1)} %all_gather.3.refs_0_, bf16[2048,2048]{1,0:T(8,128)(2,1)S(1)} %bitcast.27), custom_call_target="tpu_custom_call" | custom-call | flops 11000000 | bytes 1 | tf_op jit(solution)/shard_map/ladder_far/pallas_call | solution.py:329
  36.8 1.9 %collective-permute-start.6 = (bf16[2,64,256]{2,1,0:T(8,128)(2,1)S(1)}, bf16[2,64,256]{2,1,0:T(8,128)(2,1)S(1)}, u32[]{:S(2)}, u32[]{:S(2)}) collective-permute-start(bf16[2,64,256]{2,1,0:T(8,128)(2,1)S(1)} %ladder_far.2.refs_2_), channel_id=1, source_target_pairs={{0,1},{1,0},{2,3},{3,2},{4,5},{5,4},{6,7},{7,6},{8,9},{9,8},{10,11... | collective-permute-start | bytes 196616 | tf_op jit(solution)/shard_map/ppermute | solution.py:42
  38.7 0.7 %ladder_far.3.refs_2_ = bf16[2,64,256]{2,1,0:T(8,128)(2,1)S(1)} custom-call(bf16[64,2048]{1,0:T(8,128)(2,1)S(1)} %all_gather.3.refs_0_, bf16[2048,2048]{1,0:T(8,128)(2,1)S(1)} %bitcast.27, bf16[2,64,256]{2,1,0:T(8,128)(2,1)S(1)} %ladder_far.2.refs_2_), custom_call_target="tpu_custom_call" | custom-call | flops 11000000 | bytes 1 | tf_op jit(solution)/shard_map/ladder_far/pallas_call | solution.py:329
  39.5 0.2 collective-permute-start.5
  39.7 0.8 %ladder_near.2.refs_2_ = f32[2,64,256]{2,1,0:T(8,128)S(1)} custom-call(bf16[64,2048]{1,0:T(8,128)(2,1)S(1)} %all_gather.3.refs_0_, bf16[2048,2048]{1,0:T(8,128)(2,1)S(1)} %bitcast.27, bf16[2,64,256]{2,1,0:T(8,128)(2,1)S(1)} %ladder_far.3.refs_2_), custom_call_target="tpu_custom_call" | custom-call | flops 11000000 | bytes 1 | tf_op jit(solution)/shard_map/ladder_near/pallas_call | solution.py:329
  40.4 0.8 %ladder_near.3 = f32[2,64,256]{2,1,0:T(8,128)S(1)} custom-call(bf16[64,2048]{1,0:T(8,128)(2,1)S(1)} %all_gather.3.refs_0_, bf16[2048,2048]{1,0:T(8,128)(2,1)S(1)} %bitcast.27, f32[2,64,256]{2,1,0:T(8,128)S(1)} %ladder_near.2.refs_2_), custom_call_target="tpu_custom_call" | custom-call | flops 11000000 | bytes 1 | tf_op jit(solution)/shard_map/ladder_near/pallas_call | solution.py:329
  41.2 0.1 collective-permute-done.6
  41.3 2.9 %collective-permute-start.7 = (bf16[64,256]{1,0:T(8,128)(2,1)S(1)}, bf16[64,256]{1,0:T(8,128)(2,1)S(1)}, u32[]{:S(2)}, u32[]{:S(2)}) collective-permute-start(bf16[64,256]{1,0:T(8,128)(2,1)S(1)} %get-tuple-element.20), channel_id=1, source_target_pairs={{0,6},{1,7},{2,4},{3,5},{4,2},{5,3},{6,0},{7,1},{8,14},{9,15},{10,... | collective-permute-start | bytes 98312 | tf_op jit(solution)/shard_map/ppermute | solution.py:42
  44.3 0.0 collective-permute-start.8
  44.3 0.0 collective-permute-done.5
  44.3 1.6 %collective-permute-start.9 = (bf16[64,256]{1,0:T(8,128)(2,1)S(1)}, bf16[64,256]{1,0:T(8,128)(2,1)S(1)}, u32[]{:S(2)}, u32[]{:S(2)}) collective-permute-start(bf16[64,256]{1,0:T(8,128)(2,1)S(1)} %fusion.1), channel_id=1, source_target_pairs={{0,2},{1,3},{2,0},{3,1},{4,6},{5,7},{6,4},{7,5},{8,10},{9,11},{10,... | collective-permute-start | bytes 98312 | tf_op jit(solution)/shard_map/ppermute | solution.py:42
  45.9 1.5 %collective-permute-done.7.refs_1_ = bf16[64,256]{1,0:T(8,128)(2,1)S(1)} collective-permute-done((bf16[64,256]{1,0:T(8,128)(2,1)S(1)}, bf16[64,256]{1,0:T(8,128)(2,1)S(1)}, u32[]{:S(2)}, u32[]{:S(2)}) %collective-permute-start.7) | collective-permute-done | bytes 32800 | tf_op jit(solution)/shard_map/ppermute | solution.py:42
  47.4 1.9 %collective-permute-done.8.refs_1_ = bf16[64,256]{1,0:T(8,128)(2,1)S(1)} collective-permute-done((bf16[64,256]{1,0:T(8,128)(2,1)S(1)}, bf16[64,256]{1,0:T(8,128)(2,1)S(1)}, u32[]{:S(2)}, u32[]{:S(2)}) %collective-permute-start.8) | collective-permute-done | bytes 32800 | tf_op jit(solution)/shard_map/ppermute | solution.py:42
  49.2 0.0 collective-permute-done.9
  49.2 0.6 %add_convert_fusion.1 = bf16[64,256]{1,0:T(8,128)(2,1)} fusion(f32[64,256]{1,0:T(8,128)S(1)} %add.40, bf16[64,256]{1,0:T(8,128)(2,1)S(1)} %collective-permute-done.9), kind=kLoop, calls=%fused_computation.10 | loop fusion | flops 49152 | bytes 131072 | tf_op jit(solution)/shard_map/convert_element_type | solution.py:352
  (19 shorter events, 0.3 us)
Async XLA Ops:
  1.4 14.2 %all-to-all-start = ((s32[8,16,128]{2,1,0:T(8,128)}), s32[8,16,128]{2,1,0:T(8,128)S(1)}, u32[]{:S(2)}, u32[]{:S(2)}) async-start(s32[8,16,128]{2,1,0:T(8,128)} %get-tuple-element.11), calls=%async_computation | async-start | bytes 131072 | tf_op jit(solution)/shard_map/all_to_all | solution.py:241
  12.0 4.9 %copy-start = (s32[2048]{0:T(1024)S(1)}, s32[2048]{0:T(1024)}, u32[]{:S(2)}) copy-start(s32[2048]{0:T(1024)} %param.7) | copy-start | bytes 24580
  12.0 4.9 %copy-start.1 = (s32[2048]{0:T(1024)S(1)}, s32[2048]{0:T(1024)}, u32[]{:S(2)}) copy-start(s32[2048]{0:T(1024)} %param.8) | copy-start | bytes 24580
  15.6 5.0 %collective-permute-start = (bf16[2,16,2048]{2,1,0:T(8,128)(2,1)S(1)}, bf16[2,16,2048]{2,1,0:T(8,128)(2,1)S(1)}, u32[]{:S(2)}, u32[]{:S(2)}) collective-permute-start(bf16[2,16,2048]{2,1,0:T(8,128)(2,1)S(1)} %crossed_far.2.refs_1_), channel_id=1, source_target_pairs={{0,1},{1,0},{2,3},{3,2},{4,5},{5,4},{6,7},{7,6},{8,9},{9,8},{10,11... | collective-permute-start | bytes 393224 | tf_op jit(solution)/shard_map/ppermute | solution.py:42
  19.6 16.4 %slice-start = ((s8[8388608]{0:T(1024)(128)(4,1)}), s8[4194304]{0:T(1024)(128)(4,1)S(1)}, s32[]{:S(2)}) async-start(s8[8388608]{0:T(1024)(128)(4,1)} %bitcast.26), calls=%async_computation.1 | async-start | bytes 8388608
  19.7 6.1 %collective-permute-start.1 = (bf16[2,16,2048]{2,1,0:T(8,128)(2,1)S(1)}, bf16[2,16,2048]{2,1,0:T(8,128)(2,1)S(1)}, u32[]{:S(2)}, u32[]{:S(2)}) collective-permute-start(bf16[2,16,2048]{2,1,0:T(8,128)(2,1)S(1)} %crossed_far.3.refs_0_), channel_id=1, source_target_pairs={{0,1},{1,0},{2,3},{3,2},{4,5},{5,4},{6,7},{7,6},{8,9},{9,8},{10,11... | collective-permute-start | bytes 393224 | tf_op jit(solution)/shard_map/ppermute | solution.py:42
  20.6 8.2 %collective-permute-start.2 = (bf16[16,2048]{1,0:T(8,128)(2,1)S(1)}, bf16[16,2048]{1,0:T(8,128)(2,1)S(1)}, u32[]{:S(2)}, u32[]{:S(2)}) collective-permute-start(bf16[16,2048]{1,0:T(8,128)(2,1)S(1)} %get-tuple-element.18), channel_id=1, source_target_pairs={{0,6},{1,7},{2,4},{3,5},{4,2},{5,3},{6,0},{7,1},{8,14},{9,15},{10,... | collective-permute-start | bytes 196616 | tf_op jit(solution)/shard_map/ppermute | solution.py:42
  23.7 12.3 %slice-start.1 = ((s8[8388608]{0:T(1024)(128)(4,1)}), s8[4194304]{0:T(1024)(128)(4,1)S(1)}, s32[]{:S(2)}) async-start(s8[8388608]{0:T(1024)(128)(4,1)} %bitcast.26), calls=%async_computation.2 | async-start | bytes 8388608
  23.7 5.7 %collective-permute-start.3 = (bf16[16,2048]{1,0:T(8,128)(2,1)S(1)}, bf16[16,2048]{1,0:T(8,128)(2,1)S(1)}, u32[]{:S(2)}, u32[]{:S(2)}) collective-permute-start(bf16[16,2048]{1,0:T(8,128)(2,1)S(1)} %get-tuple-element.17), channel_id=1, source_target_pairs={{0,4},{1,5},{2,6},{3,7},{4,0},{5,1},{6,2},{7,3},{8,12},{9,13},{10,... | collective-permute-start | bytes 196616 | tf_op jit(solution)/shard_map/ppermute | solution.py:42
  25.9 4.3 %collective-permute-start.4 = (bf16[16,2048]{1,0:T(8,128)(2,1)S(1)}, bf16[16,2048]{1,0:T(8,128)(2,1)S(1)}, u32[]{:S(2)}, u32[]{:S(2)}) collective-permute-start(bf16[16,2048]{1,0:T(8,128)(2,1)S(1)} %get-tuple-element.15), channel_id=1, source_target_pairs={{0,2},{1,3},{2,0},{3,1},{4,6},{5,7},{6,4},{7,5},{8,10},{9,11},{10,... | collective-permute-start | bytes 196616 | tf_op jit(solution)/shard_map/ppermute | solution.py:42
  36.8 4.5 %collective-permute-start.6 = (bf16[2,64,256]{2,1,0:T(8,128)(2,1)S(1)}, bf16[2,64,256]{2,1,0:T(8,128)(2,1)S(1)}, u32[]{:S(2)}, u32[]{:S(2)}) collective-permute-start(bf16[2,64,256]{2,1,0:T(8,128)(2,1)S(1)} %ladder_far.2.refs_2_), channel_id=1, source_target_pairs={{0,1},{1,0},{2,3},{3,2},{4,5},{5,4},{6,7},{7,6},{8,9},{9,8},{10,11... | collective-permute-start | bytes 196616 | tf_op jit(solution)/shard_map/ppermute | solution.py:42
  39.5 4.8 %collective-permute-start.5 = (bf16[2,64,256]{2,1,0:T(8,128)(2,1)S(1)}, bf16[2,64,256]{2,1,0:T(8,128)(2,1)S(1)}, u32[]{:S(2)}, u32[]{:S(2)}) collective-permute-start(bf16[2,64,256]{2,1,0:T(8,128)(2,1)S(1)} %ladder_far.3.refs_2_), channel_id=1, source_target_pairs={{0,1},{1,0},{2,3},{3,2},{4,5},{5,4},{6,7},{7,6},{8,9},{9,8},{10,11... | collective-permute-start | bytes 196616 | tf_op jit(solution)/shard_map/ppermute | solution.py:42
  41.3 6.0 %collective-permute-start.7 = (bf16[64,256]{1,0:T(8,128)(2,1)S(1)}, bf16[64,256]{1,0:T(8,128)(2,1)S(1)}, u32[]{:S(2)}, u32[]{:S(2)}) collective-permute-start(bf16[64,256]{1,0:T(8,128)(2,1)S(1)} %get-tuple-element.20), channel_id=1, source_target_pairs={{0,6},{1,7},{2,4},{3,5},{4,2},{5,3},{6,0},{7,1},{8,14},{9,15},{10,... | collective-permute-start | bytes 98312 | tf_op jit(solution)/shard_map/ppermute | solution.py:42
  44.3 5.0 %collective-permute-start.8 = (bf16[64,256]{1,0:T(8,128)(2,1)S(1)}, bf16[64,256]{1,0:T(8,128)(2,1)S(1)}, u32[]{:S(2)}, u32[]{:S(2)}) collective-permute-start(bf16[64,256]{1,0:T(8,128)(2,1)S(1)} %get-tuple-element.19), channel_id=1, source_target_pairs={{0,4},{1,5},{2,6},{3,7},{4,0},{5,1},{6,2},{7,3},{8,12},{9,13},{10,... | collective-permute-start | bytes 98312 | tf_op jit(solution)/shard_map/ppermute | solution.py:42
  44.3 4.9 %collective-permute-start.9 = (bf16[64,256]{1,0:T(8,128)(2,1)S(1)}, bf16[64,256]{1,0:T(8,128)(2,1)S(1)}, u32[]{:S(2)}, u32[]{:S(2)}) collective-permute-start(bf16[64,256]{1,0:T(8,128)(2,1)S(1)} %fusion.1), channel_id=1, source_target_pairs={{0,2},{1,3},{2,0},{3,1},{4,6},{5,7},{6,4},{7,5},{8,10},{9,11},{10,... | collective-permute-start | bytes 98312 | tf_op jit(solution)/shard_map/ppermute | solution.py:42

commit v8 on v7

--- a/solution.py
+++ b/solution.py
@@ -245,7 +245,7 @@
         table = jnp.pad(table, ((0, 0), (0, pairs - pair_block), (0, 0)))
     table = table.reshape(orbits * pairs, orbitals)
     packed_rows = orbits // group * pairs
-    steps = 4 if orbits // group % 4 == 0 else 1
+    steps = 10 if orbits // group % 10 == 0 else 1
     table = pl.pallas_call(
         functools.partial(pack_kernel, slabs, orbits, group, pairs),
         out_shape=jax.ShapeDtypeStruct((slabs, packed_rows, DEPTH), jnp.bfloat16),

time: 50.2 us -> 50 us (level)
  waiting for transfers between devices: 5.69 us -> 4.95 us
  transfers between devices with their start and end apart: 11 -> 11, of which waited for: 7 -> 7; matrix products, arithmetic and copies ran while one was open for 0% -> 0% of each run, Pallas kernels for 28% -> 29%
where the time goes in v8:
time: 50 us; the launch traced here: 49.6 us
  starting transfers between devices  20.7 us (41%)
  Pallas kernels  16.5 us (33%)
  blocking collectives  5.79 us (12%)
  waiting for transfers between devices  4.95 us (10%)
  between operations  0.86 us (2%)
  other arithmetic  0.77 us (2%)
    ppermute x10, starting transfers between devices, swap(): return lax.ppermute(x, axis, [(i, i ^ mask) for i in range(size)])  13.5 us
    all_to_all x1, starting transfers between devices, on_device(): coded = lax.all_to_all(coded, 'cd', split_axis=0, concat_axis=0, tiled=True)  7.26 us
    pallas_call x3, Pallas kernels, direct_for(): pl.pallas_call(functools.partial(direct_kernel if old else direct_first,...  7.25 us
    all_gather x1, blocking collectives, on_device(): gathered = [lax.all_gather(packed[:pair_block], 'ab', axis=0, tiled=True)]  5.79 us
    ppermute x10, waiting for transfers between devices, swap(): return lax.ppermute(x, axis, [(i, i ^ mask) for i in range(size)])  4.49 us
    pallas_call x1, Pallas kernels, on_device(): pl.pallas_call(functools.partial(pack_kernel, slabs, orbits, group, pairs...  3.05 us
    pallas_call x4, Pallas kernels, ladder_for(): pl.pallas_call(functools.partial(ladder_kernel, masks, len(gathered)), ou...  3.01 us
    pallas_call x4, Pallas kernels, crossed_for(): pl.pallas_call(functools.partial(crossed_kernel, group, pairs, shift, orb...  1.77 us
  transfers between devices with their start and end apart: 11, of which 7 were waited for; matrix products, arithmetic and copies ran while one was open for 0% of the time, Pallas kernels for 29%

profile of v8, /device:TPU:0, one launch (start us, length us, event | category | flops | bytes accessed | tf_op | source)
XLA Modules:
  0.0 49.6 jit_solution(3310610704670404573)
XLA Ops:
  0.0 1.4 %code.1 = (s32[8,16,128]{2,1,0:T(8,128)}, s32[16,128]{1,0:T(8,128)S(1)}) custom-call(s32[16,128]{1,0:T(8,128)} %bitcast.29, s32[16,128]{1,0:T(8,128)} %bitcast.30), custom_call_target="tpu_custom_call" | custom-call | flops 22000001024 | bytes 1 | tf_op jit(solution)/shard_map/code/pallas_call | solution.py:228
  1.4 7.3 %all-to-all-start = ((s32[8,16,128]{2,1,0:T(8,128)}), s32[8,16,128]{2,1,0:T(8,128)S(1)}, u32[]{:S(2)}, u32[]{:S(2)}) async-start(s32[8,16,128]{2,1,0:T(8,128)} %get-tuple-element.11), calls=%async_computation | async-start | bytes 131072 | tf_op jit(solution)/shard_map/all_to_all | solution.py:241
  8.6 3.0 %pack.1.args_0_.packed_ref = bf16[8,320,512]{2,1,0:T(8,128)(2,1)S(1)} custom-call(bf16[1600,800]{1,0:T(8,128)(2,1)} %bitcast.28), custom_call_target="tpu_custom_call" | custom-call | bytes 5120000 | tf_op jit(solution)/shard_map/pack/pallas_call | solution.py:249
  12.3 0.0 copy-start
  12.3 0.0 copy-start.1
  12.4 2.7 %direct.3.refs_0_ = bf16[16,2048]{1,0:T(8,128)(2,1)S(1)} custom-call(bf16[8,320,512]{2,1,0:T(8,128)(2,1)S(1)} %pack.1.args_0_.packed_ref, s32[16,128]{1,0:T(8,128)S(1)} %get-tuple-element.10.args_1_.coded_ref), custom_call_target="tpu_custom_call" | custom-call | flops 2200000000 | bytes 1 | tf_op jit(solution)/shard_map/direct/pallas_call | solution.py:267
  15.1 0.5 all-to-all-done.coded_ref
  15.6 1.7 %collective-permute-start = (bf16[2,16,2048]{2,1,0:T(8,128)(2,1)S(1)}, bf16[2,16,2048]{2,1,0:T(8,128)(2,1)S(1)}, u32[]{:S(2)}, u32[]{:S(2)}) collective-permute-start(bf16[2,16,2048]{2,1,0:T(8,128)(2,1)S(1)} %crossed_far.2.refs_1_), channel_id=1, source_target_pairs={{0,1},{1,0},{2,3},{3,2},{4,5},{5,4},{6,7},{7,6},{8,9},{9,8},{10,11... | collective-permute-start | bytes 393224 | tf_op jit(solution)/shard_map/ppermute | solution.py:42
  17.2 0.0 copy-done
  17.2 0.0 copy-done.1
  17.2 2.7 %direct.4.refs_0_ = bf16[16,2048]{1,0:T(8,128)(2,1)S(1)} custom-call(bf16[8,320,512]{2,1,0:T(8,128)(2,1)S(1)} %pack.1.args_0_.packed_ref, s32[16,128]{1,0:T(8,128)S(1)} %get-tuple-element.10.args_1_.coded_ref, bf16[16,2048]{1,0:T(8,128)(2,1)S(1)} %direct.3.refs_0_, bf16[2,16,2048]{2,1,0:T(8,128)(2,1)S(1)} %crossed_far.2.refs_1_), custom_call_target="tpu_custom_call" | custom-call | flops 11000000 | bytes 1 | tf_op jit(solution)/shard_map/direct/pallas_call | solution.py:267
  20.0 0.0 slice-start
  20.0 0.4 collective-permute-start.1
  20.4 0.1 collective-permute-done
  20.6 3.2 %collective-permute-start.2 = (bf16[16,2048]{1,0:T(8,128)(2,1)S(1)}, bf16[16,2048]{1,0:T(8,128)(2,1)S(1)}, u32[]{:S(2)}, u32[]{:S(2)}) collective-permute-start(bf16[16,2048]{1,0:T(8,128)(2,1)S(1)} %get-tuple-element.18), channel_id=1, source_target_pairs={{0,6},{1,7},{2,4},{3,5},{4,2},{5,3},{6,0},{7,1},{8,14},{9,15},{10,... | collective-permute-start | bytes 196616 | tf_op jit(solution)/shard_map/ppermute | solution.py:42
  23.8 0.0 slice-start.1
  23.8 0.0 collective-permute-start.3
  23.8 1.7 %crossed_near.3 = bf16[2,16,2048]{2,1,0:T(8,128)(2,1)S(1)} custom-call(bf16[8,320,512]{2,1,0:T(8,128)(2,1)S(1)} %pack.1.args_0_.packed_ref, s32[8,16,128]{2,1,0:T(8,128)S(1)} %all-to-all-done.coded_ref, bf16[2,16,2048]{2,1,0:T(8,128)(2,1)S(1)} %add.25.refs_0_), custom_call_target="tpu_custom_call" | custom-call | flops 11000000 | bytes 1 | tf_op jit(solution)/shard_map/crossed_near/pallas_call | solution.py:290
  25.6 0.0 collective-permute-done.1
  25.7 1.3 %collective-permute-start.4 = (bf16[16,2048]{1,0:T(8,128)(2,1)S(1)}, bf16[16,2048]{1,0:T(8,128)(2,1)S(1)}, u32[]{:S(2)}, u32[]{:S(2)}) collective-permute-start(bf16[16,2048]{1,0:T(8,128)(2,1)S(1)} %get-tuple-element.15), channel_id=1, source_target_pairs={{0,2},{1,3},{2,0},{3,1},{4,6},{5,7},{6,4},{7,5},{8,10},{9,11},{10,... | collective-permute-start | bytes 196616 | tf_op jit(solution)/shard_map/ppermute | solution.py:42
  27.0 1.8 %direct.5 = bf16[16,2048]{1,0:T(8,128)(2,1)S(1)} custom-call(bf16[8,320,512]{2,1,0:T(8,128)(2,1)S(1)} %pack.1.args_0_.packed_ref, s32[16,128]{1,0:T(8,128)S(1)} %get-tuple-element.10.args_1_.coded_ref, bf16[16,2048]{1,0:T(8,128)(2,1)S(1)} %direct.4.refs_0_, bf16[2,16,2048]{2,1,0:T(8,128)(2,1)S(1)} %add.26.refs_1_), custom_call_target="tpu_custom_call" | custom-call | flops 11000000 | bytes 1 | tf_op jit(solution)/shard_map/direct/pallas_call | solution.py:267
  28.8 0.0 collective-permute-done.2.refs_1_
  28.8 0.7 %collective-permute-done.3.refs_1_ = bf16[16,2048]{1,0:T(8,128)(2,1)S(1)} collective-permute-done((bf16[16,2048]{1,0:T(8,128)(2,1)S(1)}, bf16[16,2048]{1,0:T(8,128)(2,1)S(1)}, u32[]{:S(2)}, u32[]{:S(2)}) %collective-permute-start.3) | collective-permute-done | bytes 65568 | tf_op jit(solution)/shard_map/ppermute | solution.py:42
  29.5 0.7 %collective-permute-done.4 = bf16[16,2048]{1,0:T(8,128)(2,1)S(1)} collective-permute-done((bf16[16,2048]{1,0:T(8,128)(2,1)S(1)}, bf16[16,2048]{1,0:T(8,128)(2,1)S(1)}, u32[]{:S(2)}, u32[]{:S(2)}) %collective-permute-start.4) | collective-permute-done | bytes 65568 | tf_op jit(solution)/shard_map/ppermute | solution.py:42
  30.2 5.8 %all_gather.3.refs_0_ = bf16[64,2048]{1,0:T(8,128)(2,1)S(1)} all-gather(bf16[16,2048]{1,0:T(8,128)(2,1)S(1)} %multiply_convert_fusion), channel_id=1, replica_groups=mesh['ab'=4,'cd'=8] {'ab'}, dimensions={0}, use_global_device_ids=true | all-gather | bytes 327680 | tf_op jit(solution)/shard_map/all_gather | solution.py:323
  36.0 0.0 slice-done
  36.0 0.0 slice-done.1
  36.0 0.7 %ladder_far.2.refs_2_ = bf16[2,64,256]{2,1,0:T(8,128)(2,1)S(1)} custom-call(bf16[64,2048]{1,0:T(8,128)(2,1)S(1)} %all_gather.3.refs_0_, bf16[2048,2048]{1,0:T(8,128)(2,1)S(1)} %bitcast.27), custom_call_target="tpu_custom_call" | custom-call | flops 11000000 | bytes 1 | tf_op jit(solution)/shard_map/ladder_far/pallas_call | solution.py:329
  36.8 2.3 %collective-permute-start.6 = (bf16[2,64,256]{2,1,0:T(8,128)(2,1)S(1)}, bf16[2,64,256]{2,1,0:T(8,128)(2,1)S(1)}, u32[]{:S(2)}, u32[]{:S(2)}) collective-permute-start(bf16[2,64,256]{2,1,0:T(8,128)(2,1)S(1)} %ladder_far.2.refs_2_), channel_id=1, source_target_pairs={{0,1},{1,0},{2,3},{3,2},{4,5},{5,4},{6,7},{7,6},{8,9},{9,8},{10,11... | collective-permute-start | bytes 196616 | tf_op jit(solution)/shard_map/ppermute | solution.py:42
  39.0 0.7 %ladder_far.3.refs_2_ = bf16[2,64,256]{2,1,0:T(8,128)(2,1)S(1)} custom-call(bf16[64,2048]{1,0:T(8,128)(2,1)S(1)} %all_gather.3.refs_0_, bf16[2048,2048]{1,0:T(8,128)(2,1)S(1)} %bitcast.27, bf16[2,64,256]{2,1,0:T(8,128)(2,1)S(1)} %ladder_far.2.refs_2_), custom_call_target="tpu_custom_call" | custom-call | flops 11000000 | bytes 1 | tf_op jit(solution)/shard_map/ladder_far/pallas_call | solution.py:329
  39.8 0.1 collective-permute-start.5
  39.9 0.8 %ladder_near.2.refs_2_ = f32[2,64,256]{2,1,0:T(8,128)S(1)} custom-call(bf16[64,2048]{1,0:T(8,128)(2,1)S(1)} %all_gather.3.refs_0_, bf16[2048,2048]{1,0:T(8,128)(2,1)S(1)} %bitcast.27, bf16[2,64,256]{2,1,0:T(8,128)(2,1)S(1)} %ladder_far.3.refs_2_), custom_call_target="tpu_custom_call" | custom-call | flops 11000000 | bytes 1 | tf_op jit(solution)/shard_map/ladder_near/pallas_call | solution.py:329
  40.6 0.8 %ladder_near.3 = f32[2,64,256]{2,1,0:T(8,128)S(1)} custom-call(bf16[64,2048]{1,0:T(8,128)(2,1)S(1)} %all_gather.3.refs_0_, bf16[2048,2048]{1,0:T(8,128)(2,1)S(1)} %bitcast.27, f32[2,64,256]{2,1,0:T(8,128)S(1)} %ladder_near.2.refs_2_), custom_call_target="tpu_custom_call" | custom-call | flops 11000000 | bytes 1 | tf_op jit(solution)/shard_map/ladder_near/pallas_call | solution.py:329
  41.4 0.2 collective-permute-done.6
  41.7 2.1 %collective-permute-start.7 = (bf16[64,256]{1,0:T(8,128)(2,1)S(1)}, bf16[64,256]{1,0:T(8,128)(2,1)S(1)}, u32[]{:S(2)}, u32[]{:S(2)}) collective-permute-start(bf16[64,256]{1,0:T(8,128)(2,1)S(1)} %get-tuple-element.20), channel_id=1, source_target_pairs={{0,6},{1,7},{2,4},{3,5},{4,2},{5,3},{6,0},{7,1},{8,14},{9,15},{10,... | collective-permute-start | bytes 98312 | tf_op jit(solution)/shard_map/ppermute | solution.py:42
  43.8 0.3 collective-permute-start.8
  44.1 0.0 collective-permute-done.5
  44.2 2.1 %collective-permute-start.9 = (bf16[64,256]{1,0:T(8,128)(2,1)S(1)}, bf16[64,256]{1,0:T(8,128)(2,1)S(1)}, u32[]{:S(2)}, u32[]{:S(2)}) collective-permute-start(bf16[64,256]{1,0:T(8,128)(2,1)S(1)} %fusion.1), channel_id=1, source_target_pairs={{0,2},{1,3},{2,0},{3,1},{4,6},{5,7},{6,4},{7,5},{8,10},{9,11},{10,... | collective-permute-start | bytes 98312 | tf_op jit(solution)/shard_map/ppermute | solution.py:42
  46.2 1.7 %collective-permute-done.7.refs_1_ = bf16[64,256]{1,0:T(8,128)(2,1)S(1)} collective-permute-done((bf16[64,256]{1,0:T(8,128)(2,1)S(1)}, bf16[64,256]{1,0:T(8,128)(2,1)S(1)}, u32[]{:S(2)}, u32[]{:S(2)}) %collective-permute-start.7) | collective-permute-done | bytes 32800 | tf_op jit(solution)/shard_map/ppermute | solution.py:42
  48.0 1.0 %collective-permute-done.8.refs_1_ = bf16[64,256]{1,0:T(8,128)(2,1)S(1)} collective-permute-done((bf16[64,256]{1,0:T(8,128)(2,1)S(1)}, bf16[64,256]{1,0:T(8,128)(2,1)S(1)}, u32[]{:S(2)}, u32[]{:S(2)}) %collective-permute-start.8) | collective-permute-done | bytes 32800 | tf_op jit(solution)/shard_map/ppermute | solution.py:42
  49.0 0.0 collective-permute-done.9
  49.0 0.6 %add_convert_fusion.1 = bf16[64,256]{1,0:T(8,128)(2,1)} fusion(f32[64,256]{1,0:T(8,128)S(1)} %add.40, bf16[64,256]{1,0:T(8,128)(2,1)S(1)} %collective-permute-done.9), kind=kLoop, calls=%fused_computation.10 | loop fusion | flops 49152 | bytes 131072 | tf_op jit(solution)/shard_map/convert_element_type | solution.py:352
  (19 shorter events, 0.3 us)
Async XLA Ops:
  1.4 14.2 %all-to-all-start = ((s32[8,16,128]{2,1,0:T(8,128)}), s32[8,16,128]{2,1,0:T(8,128)S(1)}, u32[]{:S(2)}, u32[]{:S(2)}) async-start(s32[8,16,128]{2,1,0:T(8,128)} %get-tuple-element.11), calls=%async_computation | async-start | bytes 131072 | tf_op jit(solution)/shard_map/all_to_all | solution.py:241
  12.3 4.9 %copy-start = (s32[2048]{0:T(1024)S(1)}, s32[2048]{0:T(1024)}, u32[]{:S(2)}) copy-start(s32[2048]{0:T(1024)} %param.7) | copy-start | bytes 24580
  12.3 4.9 %copy-start.1 = (s32[2048]{0:T(1024)S(1)}, s32[2048]{0:T(1024)}, u32[]{:S(2)}) copy-start(s32[2048]{0:T(1024)} %param.8) | copy-start | bytes 24580
  15.6 5.0 %collective-permute-start = (bf16[2,16,2048]{2,1,0:T(8,128)(2,1)S(1)}, bf16[2,16,2048]{2,1,0:T(8,128)(2,1)S(1)}, u32[]{:S(2)}, u32[]{:S(2)}) collective-permute-start(bf16[2,16,2048]{2,1,0:T(8,128)(2,1)S(1)} %crossed_far.2.refs_1_), channel_id=1, source_target_pairs={{0,1},{1,0},{2,3},{3,2},{4,5},{5,4},{6,7},{7,6},{8,9},{9,8},{10,11... | collective-permute-start | bytes 393224 | tf_op jit(solution)/shard_map/ppermute | solution.py:42
  20.0 16.1 %slice-start = ((s8[8388608]{0:T(1024)(128)(4,1)}), s8[4194304]{0:T(1024)(128)(4,1)S(1)}, s32[]{:S(2)}) async-start(s8[8388608]{0:T(1024)(128)(4,1)} %bitcast.26), calls=%async_computation.1 | async-start | bytes 8388608
  20.0 5.6 %collective-permute-start.1 = (bf16[2,16,2048]{2,1,0:T(8,128)(2,1)S(1)}, bf16[2,16,2048]{2,1,0:T(8,128)(2,1)S(1)}, u32[]{:S(2)}, u32[]{:S(2)}) collective-permute-start(bf16[2,16,2048]{2,1,0:T(8,128)(2,1)S(1)} %crossed_far.3.refs_0_), channel_id=1, source_target_pairs={{0,1},{1,0},{2,3},{3,2},{4,5},{5,4},{6,7},{7,6},{8,9},{9,8},{10,11... | collective-permute-start | bytes 393224 | tf_op jit(solution)/shard_map/ppermute | solution.py:42
  20.6 8.2 %collective-permute-start.2 = (bf16[16,2048]{1,0:T(8,128)(2,1)S(1)}, bf16[16,2048]{1,0:T(8,128)(2,1)S(1)}, u32[]{:S(2)}, u32[]{:S(2)}) collective-permute-start(bf16[16,2048]{1,0:T(8,128)(2,1)S(1)} %get-tuple-element.18), channel_id=1, source_target_pairs={{0,6},{1,7},{2,4},{3,5},{4,2},{5,3},{6,0},{7,1},{8,14},{9,15},{10,... | collective-permute-start | bytes 196616 | tf_op jit(solution)/shard_map/ppermute | solution.py:42
  23.8 12.2 %slice-start.1 = ((s8[8388608]{0:T(1024)(128)(4,1)}), s8[4194304]{0:T(1024)(128)(4,1)S(1)}, s32[]{:S(2)}) async-start(s8[8388608]{0:T(1024)(128)(4,1)} %bitcast.26), calls=%async_computation.2 | async-start | bytes 8388608
  23.8 5.7 %collective-permute-start.3 = (bf16[16,2048]{1,0:T(8,128)(2,1)S(1)}, bf16[16,2048]{1,0:T(8,128)(2,1)S(1)}, u32[]{:S(2)}, u32[]{:S(2)}) collective-permute-start(bf16[16,2048]{1,0:T(8,128)(2,1)S(1)} %get-tuple-element.17), channel_id=1, source_target_pairs={{0,4},{1,5},{2,6},{3,7},{4,0},{5,1},{6,2},{7,3},{8,12},{9,13},{10,... | collective-permute-start | bytes 196616 | tf_op jit(solution)/shard_map/ppermute | solution.py:42
  25.7 4.5 %collective-permute-start.4 = (bf16[16,2048]{1,0:T(8,128)(2,1)S(1)}, bf16[16,2048]{1,0:T(8,128)(2,1)S(1)}, u32[]{:S(2)}, u32[]{:S(2)}) collective-permute-start(bf16[16,2048]{1,0:T(8,128)(2,1)S(1)} %get-tuple-element.15), channel_id=1, source_target_pairs={{0,2},{1,3},{2,0},{3,1},{4,6},{5,7},{6,4},{7,5},{8,10},{9,11},{10,... | collective-permute-start | bytes 196616 | tf_op jit(solution)/shard_map/ppermute | solution.py:42
  36.8 4.9 %collective-permute-start.6 = (bf16[2,64,256]{2,1,0:T(8,128)(2,1)S(1)}, bf16[2,64,256]{2,1,0:T(8,128)(2,1)S(1)}, u32[]{:S(2)}, u32[]{:S(2)}) collective-permute-start(bf16[2,64,256]{2,1,0:T(8,128)(2,1)S(1)} %ladder_far.2.refs_2_), channel_id=1, source_target_pairs={{0,1},{1,0},{2,3},{3,2},{4,5},{5,4},{6,7},{7,6},{8,9},{9,8},{10,11... | collective-permute-start | bytes 196616 | tf_op jit(solution)/shard_map/ppermute | solution.py:42
  39.8 4.3 %collective-permute-start.5 = (bf16[2,64,256]{2,1,0:T(8,128)(2,1)S(1)}, bf16[2,64,256]{2,1,0:T(8,128)(2,1)S(1)}, u32[]{:S(2)}, u32[]{:S(2)}) collective-permute-start(bf16[2,64,256]{2,1,0:T(8,128)(2,1)S(1)} %ladder_far.3.refs_2_), channel_id=1, source_target_pairs={{0,1},{1,0},{2,3},{3,2},{4,5},{5,4},{6,7},{7,6},{8,9},{9,8},{10,11... | collective-permute-start | bytes 196616 | tf_op jit(solution)/shard_map/ppermute | solution.py:42
  41.7 6.3 %collective-permute-start.7 = (bf16[64,256]{1,0:T(8,128)(2,1)S(1)}, bf16[64,256]{1,0:T(8,128)(2,1)S(1)}, u32[]{:S(2)}, u32[]{:S(2)}) collective-permute-start(bf16[64,256]{1,0:T(8,128)(2,1)S(1)} %get-tuple-element.20), channel_id=1, source_target_pairs={{0,6},{1,7},{2,4},{3,5},{4,2},{5,3},{6,0},{7,1},{8,14},{9,15},{10,... | collective-permute-start | bytes 98312 | tf_op jit(solution)/shard_map/ppermute | solution.py:42
  43.8 5.2 %collective-permute-start.8 = (bf16[64,256]{1,0:T(8,128)(2,1)S(1)}, bf16[64,256]{1,0:T(8,128)(2,1)S(1)}, u32[]{:S(2)}, u32[]{:S(2)}) collective-permute-start(bf16[64,256]{1,0:T(8,128)(2,1)S(1)} %get-tuple-element.19), channel_id=1, source_target_pairs={{0,4},{1,5},{2,6},{3,7},{4,0},{5,1},{6,2},{7,3},{8,12},{9,13},{10,... | collective-permute-start | bytes 98312 | tf_op jit(solution)/shard_map/ppermute | solution.py:42
  44.2 4.8 %collective-permute-start.9 = (bf16[64,256]{1,0:T(8,128)(2,1)S(1)}, bf16[64,256]{1,0:T(8,128)(2,1)S(1)}, u32[]{:S(2)}, u32[]{:S(2)}) collective-permute-start(bf16[64,256]{1,0:T(8,128)(2,1)S(1)} %fusion.1), channel_id=1, source_target_pairs={{0,2},{1,3},{2,0},{3,1},{4,6},{5,7},{6,4},{7,5},{8,10},{9,11},{10,... | collective-permute-start | bytes 98312 | tf_op jit(solution)/shard_map/ppermute | solution.py:42
